TPU v7x, 256 devices: a whole 4x4x8 slice. The times are simulated.
256 devices in a mesh: crop: 16 (over y, x), proto: 16 (over z, core).
Axes of the slice: x: 4, y: 4, z: 8, core: 2. Of those that a mesh axis runs over, the one named last changes fastest.
Arguments:
- student_rows: bfloat16 [4096, 256], P(('crop', 'proto')), may hold values from -0.5 to 0.5
- teacher_rows: bfloat16 [4096, 256], P(('crop', 'proto')), may hold values from -0.5 to 0.5
- student_protos: bfloat16 [131072, 256], P(('proto', 'crop')), may hold values from -0.5 to 0.5
- teacher_protos: bfloat16 [131072, 256], P(('proto', 'crop')), may hold values from -0.5 to 0.5
Outputs:
- row_grad: float32 [4096, 256], P(('crop', 'proto'))
- proto_grad: float32 [131072, 256], P(('proto', 'crop'))
All inputs are finite; a program needn't handle non-finite values.
Results may differ from a plain program's by a relative error of at most 0.0025.
The roundings to bfloat16 on the way count: a program that leaves them out, or rounds other values in their place, can miss the bound.
Values may be sent and summed in bfloat16 or wider, within the bound.
No kernel may reach another device: no remote copies, remote signals or barrier semaphores. Data moves between devices by JAX's collectives and lax.ppermute only.
A program may use at most 64 MiB of HBM per device.

v0:
```python
import math

import jax
import jax.numpy as jnp
from jax import lax
from jax.sharding import PartitionSpec as P

SWEEPS = 3


TEACHER_TEMP = 0.04
STUDENT_TEMP = 0.1
EPSILON = 1e-06
BLOCK_COLS = 1024


def normalize(raw):
    values = raw.astype(jnp.float32)
    inverse = lax.rsqrt(jnp.sum(values * values, axis=1, keepdims=True) + EPSILON)
    return (values * inverse, inverse)


def scores(rows, weights):
    return lax.dot_general(
        rows, weights, (((1,), (1,)), ((), ())), preferred_element_type=jnp.float32
    )


def everywhere(values):
    return lax.psum((values[0],), "proto")


def column_scale(local_mass):
    return 1.0 / lax.psum(local_mass, "crop")


def body(student_rows, teacher_rows, student_protos, teacher_protos):
    student_unit, student_inverse = normalize(student_rows)
    teacher_unit, unused_one = normalize(teacher_rows)
    proto_unit, proto_inverse = normalize(student_protos)
    target_unit, unused_two = normalize(teacher_protos)
    student_feat, teacher_feat = (
        lax.all_gather(student_unit.astype(jnp.bfloat16), "proto", axis=0, tiled=True),
        lax.all_gather(teacher_unit.astype(jnp.bfloat16), "proto", axis=0, tiled=True),
    )
    student_weight, teacher_weight = (
        lax.all_gather(proto_unit.astype(jnp.bfloat16), "crop", axis=0, tiled=True),
        lax.all_gather(target_unit.astype(jnp.bfloat16), "crop", axis=0, tiled=True),
    )
    local_protos = student_weight.shape[0]
    features = student_weight.shape[1]
    crop_rows = student_feat.shape[0]
    width = math.gcd(local_protos, BLOCK_COLS)
    count = local_protos // width
    factor = student_protos.shape[0] * lax.axis_size("crop") * lax.axis_size("proto") / 16.0
    student_blocks = student_weight.reshape(count, width, features)
    teacher_blocks = teacher_weight.reshape(count, width, features)

    def teacher_exp(weights):
        return jnp.exp(scores(teacher_feat, weights) / TEACHER_TEMP)

    def student_exp(weights):
        return jnp.exp(scores(student_feat, weights) / STUDENT_TEMP)

    def local_rows(scales):

        def add_rows(total, pieces):
            return (total + jnp.sum(teacher_exp(pieces[0]) * pieces[1][None, :], axis=1), None)

        total, unused = lax.scan(
            add_rows,
            jnp.zeros((crop_rows,), jnp.float32),
            (teacher_blocks, scales.reshape(count, width)),
        )
        return total

    row_scale = jnp.ones((crop_rows,), jnp.float32)
    col_scale = jnp.ones((local_protos,), jnp.float32)
    for sweep in range(SWEEPS):
        scales_now = row_scale
        col_mass = lax.map(
            lambda weights: jnp.sum(teacher_exp(weights) * scales_now[:, None], axis=0),
            teacher_blocks,
        )
        col_scale = column_scale(col_mass.reshape(local_protos))
        if sweep + 1 < SWEEPS:
            row_scale = 1.0 / everywhere((local_rows(col_scale),))[0]
    row_scale = 1.0 / everywhere((local_rows(col_scale),))[0]

    def add_student(total, weights):
        return (total + jnp.sum(student_exp(weights), axis=1), None)

    student_local, unused_four = lax.scan(
        add_student, jnp.zeros((crop_rows,), jnp.float32), student_blocks
    )
    student_total = lax.psum(student_local, "proto")

    def backward(feat_grad, pieces):
        teacher_w, student_w, scales = pieces
        target = teacher_exp(teacher_w) * scales[None, :] * row_scale[:, None]
        prob = student_exp(student_w) / student_total[:, None]
        grad_logits = ((prob - target) * factor).astype(jnp.bfloat16)
        feat_grad = feat_grad + jnp.dot(grad_logits, student_w, preferred_element_type=jnp.float32)
        weight_block = lax.dot_general(
            grad_logits, student_feat, (((0,), (0,)), ((), ())), preferred_element_type=jnp.float32
        )
        return (feat_grad, weight_block)

    feat_grad, weight_blocks = lax.scan(
        backward,
        jnp.zeros((crop_rows, features), jnp.float32),
        (teacher_blocks, student_blocks, col_scale.reshape(count, width)),
    )
    weight_grad = weight_blocks.reshape(local_protos, features)
    feat_share = lax.psum_scatter(feat_grad, "proto", scatter_dimension=0, tiled=True)
    weight_share = lax.psum_scatter(weight_grad, "crop", scatter_dimension=0, tiled=True)
    row_grad = (
        feat_share - student_unit * jnp.sum(student_unit * feat_share, axis=1, keepdims=True)
    ) * student_inverse
    proto_grad = (
        weight_share - proto_unit * jnp.sum(proto_unit * weight_share, axis=1, keepdims=True)
    ) * proto_inverse
    return (row_grad, proto_grad)


def solution(mesh):
    placed = (
        P(("crop", "proto"), None),
        P(("crop", "proto"), None),
        P(("proto", "crop"), None),
        P(("proto", "crop"), None),
    )
    return jax.shard_map(
        body,
        mesh=mesh,
        in_specs=placed,
        out_specs=(P(("crop", "proto"), None), P(("proto", "crop"), None)),
        check_vma=False,
    )
```

profile of v0, /device:TPU:32, one launch (start us, length us, event | category | flops | bytes accessed | tf_op | source)
XLA Modules:
  0.0 639.6 jit_solution(6791252348640359794)
XLA Ops:
  8.3 1.8 fusion.66
  11.3 1.8 fusion.60
  14.8 18.2 %all_gather.15 = bf16[256,256]{1,0:T(8,128)(2,1)S(1)} all-gather(bf16[16,256]{1,0:T(8,128)(2,1)S(1)} %fusion.75), channel_id=1, replica_groups=mesh['crop'=16,'proto'=16] {'proto'}, dimensions={0}, use_global_device_ids=true | all-gather | bytes 139264 | tf_op jit(solution)/shard_map/all_gather | solution.py:44
  34.6 16.7 %all_gather.13 = bf16[256,256]{1,0:T(8,128)(2,1)S(1)} all-gather(bf16[16,256]{1,0:T(8,128)(2,1)S(1)} %fusion.69), channel_id=1, replica_groups=mesh['crop'=16,'proto'=16] {'proto'}, dimensions={0}, use_global_device_ids=true | all-gather | bytes 139264 | tf_op jit(solution)/shard_map/all_gather | solution.py:43
  51.3 18.4 %all-gather.5.cloned.1.call-done = bf16[8192,256]{1,0:T(8,128)(2,1)} async-done(((bf16[512,256]{1,0:T(8,128)(2,1)}), bf16[8192,256]{1,0:T(8,128)(2,1)}) %all-gather.5.cloned.1.call-update) | async-done | bytes 4194320 | tf_op jit(solution)/shard_map/all_gather | solution.py:48
  69.6 12.3 %while.87 = (s32[]{:T(128)}, f32[8,1024]{1,0:T(8,128)S(1)}, bf16[8,1024,256]{2,1,0:T(8,128)(2,1)}, bf16[256,256]{1,0:T(8,128)(2,1)S(1)}, s32[]{:T(128)}, /*index=5*/s32[]{:T(128)}) while((s32[]{:T(128)}, f32[8,1024]{1,0:T(8,128)S(1)}, bf16[8,1024,256]{2,1,0:T(8,128)(2,1)}, bf16[256,256]{1,0:T(8,128)(2,1)S(1)}, s32[]{:T(128)}, ...), condition=%wide.region_5.0_spmd, body=%wide.region_3.5_spmd.sunk | while | flops 134740992 | bytes 668233 | solution.py:81
  81.9 72.8 %psum.50 = f32[8192]{0:T(1024)S(1)} all-reduce(f32[8192]{0:T(1024)S(1)} %bitcast.132), channel_id=1, replica_groups=mesh['crop'=16,'proto'=16] {'crop'}, use_global_device_ids=true, to_apply=%region_6.7 | all-reduce | flops 8192 | bytes 65536 | tf_op jit(solution)/shard_map/psum | solution.py:34
  154.8 12.2 %while.91 = (s32[]{:T(128)}, f32[256]{0:T(256)S(1)}, bf16[8,1024,256]{2,1,0:T(8,128)(2,1)}, bf16[256,256]{1,0:T(8,128)(2,1)S(1)}, f32[8,1024]{1,0:T(8,128)S(1)}, /*index=5*/s32[]{:T(128)}, s32[]{:T(128)}) while((s32[]{:T(128)}, f32[256]{0:T(256)S(1)}, bf16[8,1024,256]{2,1,0:T(8,128)(2,1)}, bf16[256,256]{1,0:T(8,128)(2,1)S(1)}, ...), condition=%wide.region_9.10_spmd.clone, body=%wide.region_7.9_spmd.clone.sunk | while | flops 135004416 | bytes 672347 | solution.py:70
  154.8 1.5 fusion.134
  156.3 1.5 fusion.134
  157.9 1.5 fusion.134
  159.4 1.5 fusion.134
  160.9 1.5 fusion.134
  162.4 1.5 fusion.134
  164.0 1.5 fusion.134
  165.5 1.5 fusion.134
  167.0 20.6 %psum.51 = f32[256]{0:T(256)S(1)} all-reduce(f32[256]{0:T(256)S(1)} %get-tuple-element.236), channel_id=1, replica_groups=mesh['crop'=16,'proto'=16] {'proto'}, use_global_device_ids=true, to_apply=%region_10.11 | all-reduce | flops 256 | bytes 2048 | tf_op jit(solution)/shard_map/psum | solution.py:30
  187.6 12.5 %while.88 = (s32[]{:T(128)}, f32[8,1024]{1,0:T(8,128)S(1)}, bf16[8,1024,256]{2,1,0:T(8,128)(2,1)}, bf16[256,256]{1,0:T(8,128)(2,1)S(1)}, f32[256]{0:T(256)S(1)}, /*index=5*/s32[]{:T(128)}, s32[]{:T(128)}) while((s32[]{:T(128)}, f32[8,1024]{1,0:T(8,128)S(1)}, bf16[8,1024,256]{2,1,0:T(8,128)(2,1)}, bf16[256,256]{1,0:T(8,128)(2,1)S(1)}, ...), condition=%wide.region_13.14_spmd, body=%wide.region_11.13_spmd.sunk | while | flops 135003136 | bytes 669265 | solution.py:81
  200.1 69.5 %psum.52 = f32[8192]{0:T(1024)S(1)} all-reduce(f32[8192]{0:T(1024)S(1)} %bitcast.133), channel_id=1, replica_groups=mesh['crop'=16,'proto'=16] {'crop'}, use_global_device_ids=true, to_apply=%region_14.15 | all-reduce | flops 8192 | bytes 65536 | tf_op jit(solution)/shard_map/psum | solution.py:34
  269.7 12.2 %while.92 = (s32[]{:T(128)}, f32[256]{0:T(256)S(1)}, bf16[8,1024,256]{2,1,0:T(8,128)(2,1)}, bf16[256,256]{1,0:T(8,128)(2,1)S(1)}, f32[8,1024]{1,0:T(8,128)S(1)}, /*index=5*/s32[]{:T(128)}, s32[]{:T(128)}) while((s32[]{:T(128)}, f32[256]{0:T(256)S(1)}, bf16[8,1024,256]{2,1,0:T(8,128)(2,1)}, bf16[256,256]{1,0:T(8,128)(2,1)S(1)}, ...), condition=%wide.region_17.18_spmd.clone, body=%wide.region_15.17_spmd.clone.sunk | while | flops 135004416 | bytes 672347 | solution.py:70
  269.7 1.5 fusion.137
  271.2 1.5 fusion.137
  272.8 1.5 fusion.137
  274.3 1.5 fusion.137
  275.8 1.5 fusion.137
  277.3 1.5 fusion.137
  278.9 1.5 fusion.137
  280.4 1.5 fusion.137
  281.9 23.5 %psum.53 = f32[256]{0:T(256)S(1)} all-reduce(f32[256]{0:T(256)S(1)} %get-tuple-element.238), channel_id=1, replica_groups=mesh['crop'=16,'proto'=16] {'proto'}, use_global_device_ids=true, to_apply=%region_18.19 | all-reduce | flops 256 | bytes 2048 | tf_op jit(solution)/shard_map/psum | solution.py:30
  305.5 12.5 %while.89 = (s32[]{:T(128)}, f32[8,1024]{1,0:T(8,128)S(1)}, bf16[8,1024,256]{2,1,0:T(8,128)(2,1)}, bf16[256,256]{1,0:T(8,128)(2,1)S(1)}, f32[256]{0:T(256)S(1)}, /*index=5*/s32[]{:T(128)}, s32[]{:T(128)}) while((s32[]{:T(128)}, f32[8,1024]{1,0:T(8,128)S(1)}, bf16[8,1024,256]{2,1,0:T(8,128)(2,1)}, bf16[256,256]{1,0:T(8,128)(2,1)S(1)}, ...), condition=%wide.region_21.22_spmd, body=%wide.region_19.21_spmd.sunk | while | flops 135003136 | bytes 669265 | solution.py:81
  318.0 69.5 %psum.54 = f32[8192]{0:T(1024)S(1)} all-reduce(f32[8192]{0:T(1024)S(1)} %bitcast.134), channel_id=1, replica_groups=mesh['crop'=16,'proto'=16] {'crop'}, use_global_device_ids=true, to_apply=%region_22.23 | all-reduce | flops 8192 | bytes 65536 | tf_op jit(solution)/shard_map/psum | solution.py:34
  387.6 12.2 %while.93 = (s32[]{:T(128)}, f32[256]{0:T(256)S(1)}, bf16[8,1024,256]{2,1,0:T(8,128)(2,1)}, bf16[256,256]{1,0:T(8,128)(2,1)S(1)}, f32[8,1024]{1,0:T(8,128)S(1)}, /*index=5*/s32[]{:T(128)}, s32[]{:T(128)}) while((s32[]{:T(128)}, f32[256]{0:T(256)S(1)}, bf16[8,1024,256]{2,1,0:T(8,128)(2,1)}, bf16[256,256]{1,0:T(8,128)(2,1)S(1)}, ...), condition=%wide.region_25.26_spmd.clone, body=%wide.region_23.25_spmd.clone.sunk | while | flops 135004416 | bytes 672347 | solution.py:70
  387.6 1.5 fusion.140
  389.1 1.5 fusion.140
  390.7 1.5 fusion.140
  392.2 1.5 fusion.140
  393.7 1.5 fusion.140
  395.2 1.5 fusion.140
  396.8 1.5 fusion.140
  398.3 1.5 fusion.140
  399.8 12.0 %while.90 = (s32[]{:T(128)}, f32[256]{0:T(256)S(1)}, bf16[8,1024,256]{2,1,0:T(8,128)(2,1)}, bf16[256,256]{1,0:T(8,128)(2,1)S(1)}, s32[]{:T(128)}, /*index=5*/s32[]{:T(128)}) while((s32[]{:T(128)}, f32[256]{0:T(256)S(1)}, bf16[8,1024,256]{2,1,0:T(8,128)(2,1)}, bf16[256,256]{1,0:T(8,128)(2,1)S(1)}, s32[]{:T(128)}, ...), condition=%wide.region_30.31_spmd.clone, body=%wide.region_28.30_spmd.clone.sunk | while | flops 134742272 | bytes 660047 | solution.py:93
  399.8 1.5 fusion.131
  401.3 1.5 fusion.131
  402.8 1.5 fusion.131
  404.3 1.5 fusion.131
  405.8 1.5 fusion.131
  407.3 1.5 fusion.131
  408.8 1.5 fusion.131
  410.3 1.5 fusion.131
  411.8 23.5 %all-reduce = (f32[256]{0:T(256)S(1)}, f32[256]{0:T(256)S(1)}) all-reduce(f32[256]{0:T(256)S(1)} %get-tuple-element.234, f32[256]{0:T(256)S(1)} %get-tuple-element.240), channel_id=1, replica_groups=mesh['crop'=16,'proto'=16] {'proto'}, use_global_device_ids=true, to_apply=%region_31.32 | all-reduce | flops 512 | bytes 4096 | tf_op jit(solution)/shard_map/psum | solution.py:96
  435.3 45.5 %while.94 = (s32[]{:T(128)}, f32[256,256]{1,0:T(8,128)S(1)}, f32[8,1024,256]{2,1,0:T(8,128)}, bf16[8,1024,256]{2,1,0:T(8,128)(2,1)}, bf16[256,256]{1,0:T(8,128)(...) while((s32[]{:T(128)}, f32[256,256]{1,0:T(8,128)S(1)}, ...), condition=%wide.region_33.34_spmd.clone, body=%wide.region_32.33_spmd.clone.sunk | while | flops 539099136 | bytes 7225475 | solution.py:109
  436.8 1.5 fusion.150
  442.4 1.5 fusion.150
  448.2 1.5 fusion.150
  453.8 1.5 fusion.150
  459.5 1.5 fusion.150
  462.3 1.4 convolution_add_fusion.2
  465.2 1.5 fusion.150
  470.9 1.5 fusion.150
  476.6 1.5 fusion.150
  479.4 1.4 convolution_add_fusion.2
  482.1 52.0 %reduce-scatter.3.cloned.1.call-done = f32[16,256]{1,0:T(8,128)} async-done(((f32[256,256]{1,0:T(8,128)}), f32[16,256]{1,0:T(8,128)}) %reduce-scatter.3.cloned.1.call-update) | async-done | bytes 16400 | tf_op jit(solution)/shard_map/reduce_scatter | solution.py:115
  536.4 93.3 %reduce-scatter.5.cloned.1.call-done = f32[512,256]{1,0:T(8,128)} async-done(((f32[8192,256]{1,0:T(8,128)}), f32[512,256]{1,0:T(8,128)}) %reduce-scatter.5.cloned.1.call-update) | async-done | bytes 524304 | tf_op jit(solution)/shard_map/reduce_scatter | solution.py:116
  631.0 2.0 fusion.63
  (183 shorter events, 77.9 us)
Async XLA Ops:
  7.2 62.5 %all-gather.5.cloned.1.call-start = ((), (), s32[]{:S(2)}) async-start(), calls=%async_computation.3 | async-start | bytes 4456448 | tf_op jit(solution)/shard_map/all_gather | solution.py:48
  10.1 389.7 %all-gather.3.cloned.1.call-start = ((), (), s32[]{:S(2)}) async-start(), calls=%async_computation.2 | async-start | bytes 4456448 | tf_op jit(solution)/shard_map/all_gather | solution.py:47
  13.1 521.0 %reduce-scatter.3.cloned.1.call-start = ((), (), s32[]{:S(2)}) async-start(), calls=%async_computation.4 | async-start | bytes 278528 | tf_op jit(solution)/shard_map/reduce_scatter | solution.py:115
  480.8 0.7 copy-start
  481.5 148.2 %reduce-scatter.5.cloned.1.call-start = ((), (), s32[]{:S(2)}) async-start(), calls=%async_computation.5 | async-start | bytes 8912896 | tf_op jit(solution)/shard_map/reduce_scatter | solution.py:116
  481.6 52.5 %copy-start.2 = (bf16[16,256]{1,0:T(8,128)(2,1)S(1)}, bf16[16,256]{1,0:T(8,128)(2,1)}, u32[]{:S(2)}) copy-start(bf16[16,256]{1,0:T(8,128)(2,1)} %param.20) | copy-start | bytes 24580
  481.6 148.2 %copy-start.1 = (bf16[512,256]{1,0:T(8,128)(2,1)S(1)}, bf16[512,256]{1,0:T(8,128)(2,1)}, u32[]{:S(2)}) copy-start(bf16[512,256]{1,0:T(8,128)(2,1)} %param.22) | copy-start | bytes 786436
Sparse Core Ops, SparseCore 0:
  10.4 59.1 all-gather.4
  72.6 56.8 all-gather.2
  481.7 52.4 reduce-scatter.2
  538.1 91.5 reduce-scatter.4
where the time goes:
time: 644 us; the launch traced here: 640 us
  blocking collectives  314 us (49%)
  waiting for transfers between devices  164 us (25%)
  matrix products  126 us (20%)
  other arithmetic  15 us (2%)
  between operations  14 us (2%)
    psum x3, blocking collectives, column_scale(): return 1.0 / lax.psum(local_mass, 'crop')  212 us
    dot_general x72, matrix products, scores(): lax.dot_general(rows, weights, (((1,), (1,)), ((), ())), preferred_elemen...  104 us
    reduce_scatter x1, waiting for transfers between devices, body(): lax.psum_scatter(weight_grad, 'crop', scatter_dimension=0, tiled=True)  93.3 us
    reduce_scatter x1, waiting for transfers between devices, body(): lax.psum_scatter(feat_grad, 'proto', scatter_dimension=0, tiled=True)  52 us
    psum x2, blocking collectives, everywhere(): return lax.psum((values[0],), 'proto')  44.1 us
    psum x1, blocking collectives, body(): student_total = lax.psum(student_local, 'proto')  23.5 us
    all_gather x1, waiting for transfers between devices, body(): lax.all_gather(target_unit.astype(jnp.bfloat16), 'crop', axis=0, tiled=True)  18.4 us
    all_gather x1, blocking collectives, body(): lax.all_gather(teacher_unit.astype(jnp.bfloat16), 'proto', axis=0, tiled=...  18.2 us
  transfers between devices with their start and end apart: 4, of which 3 were waited for; matrix products, arithmetic and copies ran while one was open for 13% of the time, Pallas kernels for 0%

commit v1 on v0

v1 whole, which is shorter than its diff:
```python
import jax
import jax.numpy as jnp
from jax import lax
from jax.sharding import Mesh, PartitionSpec as P

SWEEPS = 3
TEACHER_TEMP = 0.04
STUDENT_TEMP = 0.1
EPSILON = 1e-06
ROWS = ("y", "z")


def normalize(raw):
    values = raw.astype(jnp.float32)
    inverse = lax.rsqrt(jnp.sum(values * values, axis=1, keepdims=True) + EPSILON)
    return (values * inverse, inverse)


def scores(rows, weights):
    return lax.dot_general(
        rows, weights, (((1,), (1,)), ((), ())), preferred_element_type=jnp.float32
    )


def shift(values, axis, step):
    size = lax.axis_size(axis)
    return lax.ppermute(values, axis, [(i, (i + step) % size) for i in range(size)])


def spread(values):
    count = lax.axis_size(ROWS)
    return lax.all_to_all(
        jnp.broadcast_to(values[None], (count,) + values.shape), ROWS, 0, 0, tiled=True
    )


def gather_rows(feat):
    own = spread(feat).reshape(-1, feat.shape[1])
    return jnp.concatenate([own, shift(own, "core", 1)], axis=0)


def gather_protos(weight):
    return jnp.concatenate([weight] + [shift(weight, "x", k) for k in (1, 2, 3)], axis=0)


def sum_columns(local):
    blocks = local.reshape(4, -1)
    total = blocks
    for k in (1, 2, 3):
        total = total + shift(jnp.roll(blocks, k, axis=0), "x", k)
    return total.reshape(-1)


def sum_rows(local):
    half = local.shape[0] // 2
    both = local + shift(jnp.concatenate([local[half:], local[:half]]), "core", 1)
    return jnp.sum(spread(both.reshape(-1, 128)), axis=0).reshape(-1)


def body(student_rows, teacher_rows, student_protos, teacher_protos):
    student_unit, student_inverse = normalize(student_rows)
    teacher_unit, unused_one = normalize(teacher_rows)
    proto_unit, proto_inverse = normalize(student_protos)
    target_unit, unused_two = normalize(teacher_protos)
    teacher_feat = gather_rows(teacher_unit.astype(jnp.bfloat16))
    teacher_weight = gather_protos(target_unit.astype(jnp.bfloat16))
    student_feat = gather_rows(student_unit.astype(jnp.bfloat16))
    student_weight = gather_protos(proto_unit.astype(jnp.bfloat16))
    own_rows = student_rows.shape[0]
    own_protos = student_protos.shape[0]
    features = student_rows.shape[1]
    factor = own_protos * 256 / 16.0

    teacher_exp = jnp.exp(scores(teacher_feat, teacher_weight) / TEACHER_TEMP)
    student_exp = jnp.exp(scores(student_feat, student_weight) / STUDENT_TEMP)
    student_total = sum_rows(jnp.sum(student_exp, axis=1))

    row_scale = jnp.ones((teacher_feat.shape[0],), jnp.float32)
    for sweep in range(SWEEPS):
        col_scale = 1.0 / sum_columns(jnp.sum(teacher_exp * row_scale[:, None], axis=0))
        row_scale = 1.0 / sum_rows(jnp.sum(teacher_exp * col_scale[None, :], axis=1))

    target = teacher_exp * col_scale[None, :] * row_scale[:, None]
    prob = student_exp / student_total[:, None]
    grad_logits = ((prob - target) * factor).astype(jnp.bfloat16)
    feat_grad = jnp.dot(grad_logits, student_weight, preferred_element_type=jnp.float32)
    weight_grad = lax.dot_general(
        grad_logits, student_feat, (((0,), (0,)), ((), ())), preferred_element_type=jnp.float32
    )
    half = feat_grad.shape[0] // 2
    feat_pair = feat_grad[:half] + shift(feat_grad[half:], "core", 1)
    feat_share = jnp.sum(
        lax.all_to_all(feat_pair.reshape(-1, own_rows, features), ROWS, 0, 0, tiled=True), axis=0
    )
    weight_parts = weight_grad.reshape(4, own_protos, features)
    weight_share = weight_parts[0]
    for k in (1, 2, 3):
        weight_share = weight_share + shift(weight_parts[k], "x", -k)
    row_grad = (
        feat_share - student_unit * jnp.sum(student_unit * feat_share, axis=1, keepdims=True)
    ) * student_inverse
    proto_grad = (
        weight_share - proto_unit * jnp.sum(proto_unit * weight_share, axis=1, keepdims=True)
    ) * proto_inverse
    return (row_grad, proto_grad)


def solution(mesh):
    fine = Mesh(mesh.devices.reshape(4, 4, 8, 2), ("y", "x", "z", "core"))
    rows = P(("y", "x", "z", "core"), None)
    protos = P(("z", "core", "y", "x"), None)
    return jax.shard_map(
        body,
        mesh=fine,
        in_specs=(rows, rows, protos, protos),
        out_specs=(rows, protos),
        check_vma=False,
    )
```

time: 644 us -> 210 us (0.33)
  blocking collectives: 314 us -> 0 us
  matrix products: 126 us -> 12.8 us
  waiting for transfers between devices: 164 us -> 77.1 us
  starting transfers between devices: 0.16 us -> 74.6 us
  other arithmetic: 15 us -> 34.9 us
  between operations: 14 us -> 1.16 us
    psum x6 -> x0, blocking collectives: 280 us -> none  [the longest x3 212 us: column_scale(): return 1.0 / lax.psum(local_mass, 'crop')]
    reduce_scatter x2 -> x0, waiting for transfers between devices: 145 us -> none  [the longest x1 93.3 us: body(): lax.psum_scatter(weight_grad, 'crop', scatter_dimension=0, tiled=True)]
    dot_general x72 -> x2, matrix products: 104 us -> 10.2 us  [scores(): lax.dot_general(rows, weights, (((1,), (1,)), ((), ())), preferred_elemen...]
    all_to_all x0 -> x7, starting transfers between devices: none -> 49.7 us  [the longest x6 45.4 us: spread(): lax.all_to_all(jnp.broadcast_to(values[None], (count,) + values.shape), R...]
    all_to_all x0 -> x7, waiting for transfers between devices: none -> 39.5 us  [the longest x6 39.4 us: spread(): lax.all_to_all(jnp.broadcast_to(values[None], (count,) + values.shape), R...]
    ppermute x0 -> x25, waiting for transfers between devices: none -> 37.6 us  [shift(): lax.ppermute(values, axis, [(i, (i + step) % size) for i in range(size)])]
    all_gather x2 -> x0, blocking collectives: 34.9 us -> none  [the longest x1 18.2 us: body(): lax.all_gather(teacher_unit.astype(jnp.bfloat16), 'proto', axis=0, tiled=...]
    ppermute x0 -> x25, starting transfers between devices: none -> 24.9 us  [shift(): lax.ppermute(values, axis, [(i, (i + step) % size) for i in range(size)])]
  transfers between devices with their start and end apart: 4 -> 32, of which waited for: 3 -> 18; matrix products, arithmetic and copies ran while one was open for 13% -> 15% of each run, Pallas kernels for 0% -> 0%
where the time goes in v1:
time: 210 us; the launch traced here: 208 us
  waiting for transfers between devices  77.1 us (37%)
  starting transfers between devices  74.6 us (36%)
  other arithmetic  34.9 us (17%)
  matrix products  12.8 us (6%)
  local copies, waits for them, and re-layouts  7.62 us (4%)
    all_to_all x6, starting transfers between devices, spread(): lax.all_to_all(jnp.broadcast_to(values[None], (count,) + values.shape), R...  45.4 us
    all_to_all x6, waiting for transfers between devices, spread(): lax.all_to_all(jnp.broadcast_to(values[None], (count,) + values.shape), R...  39.4 us
    ppermute x25, waiting for transfers between devices, shift(): lax.ppermute(values, axis, [(i, (i + step) % size) for i in range(size)])  37.6 us
    ppermute x25, starting transfers between devices, shift(): lax.ppermute(values, axis, [(i, (i + step) % size) for i in range(size)])  24.9 us
    reduce_sum x3, other arithmetic, body(): jnp.sum(teacher_exp * col_scale[None, :], axis=1)  12.1 us
    dot_general x2, matrix products, scores(): lax.dot_general(rows, weights, (((1,), (1,)), ((), ())), preferred_elemen...  10.2 us
    reduce_sum x2, other arithmetic, body(): jnp.sum(teacher_exp * row_scale[:, None], axis=0)  8.01 us
    convert_element_type x1, other arithmetic, body(): grad_logits = ((prob - target) * factor).astype(jnp.bfloat16)  7.12 us
  transfers between devices with their start and end apart: 32, of which 18 were waited for; matrix products, arithmetic and copies ran while one was open for 15% of the time, Pallas kernels for 0%

profile of v1, /device:TPU:32, one launch (start us, length us, event | category | flops | bytes accessed | tf_op | source)
XLA Modules:
  0.0 208.1 jit_solution(3812803515346828703)
XLA Ops:
  0.6 0.8 fusion.32
  1.4 0.8 fusion.33
  2.2 0.7 broadcast_in_dim.23
  2.9 11.4 %all-to-all-start.2 = ((bf16[32,16,256]{2,1,0:T(8,128)(2,1)}), bf16[32,16,256]{2,1,0:T(8,128)(2,1)S(1)}, u32[]{:S(2)}, u32[]{:S(2)}) async-start(bf16[32,16,256]{2,1,0:T(8,128)(2,1)} %broadcast_in_dim.23), calls=%async_computation.2 | async-start | bytes 524288 | tf_op jit(solution)/shard_map/all_to_all | solution.py:32
  14.3 1.1 fusion.15
  15.4 1.1 fusion.16
  16.5 2.8 %collective-permute-start.8 = (bf16[512,256]{1,0:T(8,128)(2,1)S(1)}, bf16[512,256]{1,0:T(8,128)(2,1)S(1)}, u32[]{:S(2)}, u32[]{:S(2)}) collective-permute-start(bf16[512,256]{1,0:T(8,128)(2,1)S(1)} %fusion.16), channel_id=1, source_target_pairs={{0,48},{16,0},{32,16},{48,32},{1,49},{17,1},{33,17},{49,33},{2,50}... | collective-permute-start | bytes 786440 | tf_op jit(solution)/shard_map/ppermute | solution.py:27
  19.4 0.8 collective-permute-start.7
  20.2 0.9 collective-permute-start.6
  21.0 5.6 %all-to-all-done.2 = bf16[32,16,256]{2,1,0:T(8,128)(2,1)S(1)} async-done(((bf16[32,16,256]{2,1,0:T(8,128)(2,1)}), bf16[32,16,256]{2,1,0:T(8,128)(2,1)S(1)}, u32[]{:S(2)}, u32[]{:S(2)}) %all-to-all-start.2) | async-done | bytes 262176 | tf_op jit(solution)/shard_map/all_to_all | solution.py:32
  26.6 1.1 copy.8
  27.8 2.2 %collective-permute-done.8 = bf16[512,256]{1,0:T(8,128)(2,1)S(1)} collective-permute-done((bf16[512,256]{1,0:T(8,128)(2,1)S(1)}, bf16[512,256]{1,0:T(8,128)(2,1)S(1)}, u32[]{:S(2)}, u32[]{:S(2)}) %collective-permute-start.8) | collective-permute-done | bytes 262176 | tf_op jit(solution)/shard_map/ppermute | solution.py:27
  30.1 3.6 %collective-permute-done.6 = bf16[512,256]{1,0:T(8,128)(2,1)S(1)} collective-permute-done((bf16[512,256]{1,0:T(8,128)(2,1)S(1)}, bf16[512,256]{1,0:T(8,128)(2,1)S(1)}, u32[]{:S(2)}, u32[]{:S(2)}) %collective-permute-start.6) | collective-permute-done | bytes 262176 | tf_op jit(solution)/shard_map/ppermute | solution.py:27
  33.7 6.0 %fusion.53 = (f32[2048]{0:T(1024)S(1)}, f32[1024,2048]{1,0:T(8,128)}) fusion(bf16[512,256]{1,0:T(8,128)(2,1)S(1)} %collective-permute-done.8, bf16[512,256]{1,0:T(8,128)(2,1)S(1)} %collective-permute-done.7, bf16[512,256]{1,0:T(8,128)(2,1)S(1)} %collective-permute-done.6, bf16[512,256]{1,0:T(8,128)(2,1)S(1)} %fusion.16, ...), kind=kOutput, calls=%fused_computation.99 | convolution fusion | flops 1083176960 | bytes 9969664 | tf_op jit(solution)/shard_map/dot_general | solution.py:20
  39.8 0.7 collective-permute-start.11
  40.5 1.5 collective-permute-start.9
  42.0 0.9 collective-permute-start.10
  42.9 0.6 collective-permute-done.11
  43.5 1.9 collective-permute-done.9
  45.4 1.8 collective-permute-done.10
  47.2 4.0 %multiply_reduce_fusion.3 = f32[1024]{0:T(1024)S(1)} fusion(f32[1024,2048]{1,0:T(8,128)} %get-tuple-element.40, f32[2048]{0:T(1024)S(1)} %bitcast.42), kind=kLoop, calls=%fused_computation.4 | loop fusion | flops 4193280 | bytes 8400896 | tf_op jit(solution)/shard_map/reduce_sum | solution.py:81
  51.5 1.0 collective-permute-done.12
  52.5 0.7 broadcast_in_dim.25
  53.2 9.8 %all-to-all-start.3 = ((f32[32,8,128]{2,1,0:T(8,128)}), f32[32,8,128]{2,1,0:T(8,128)S(1)}, u32[]{:S(2)}, u32[]{:S(2)}) async-start(f32[32,8,128]{2,1,0:T(8,128)} %broadcast_in_dim.25), calls=%async_computation.3 | async-start | bytes 262144 | tf_op jit(solution)/shard_map/all_to_all | solution.py:32
  63.1 9.9 %all-to-all-done.3 = f32[32,8,128]{2,1,0:T(8,128)S(1)} async-done(((f32[32,8,128]{2,1,0:T(8,128)}), f32[32,8,128]{2,1,0:T(8,128)S(1)}, u32[]{:S(2)}, u32[]{:S(2)}) %all-to-all-start.3) | async-done | bytes 131104 | tf_op jit(solution)/shard_map/all_to_all | solution.py:32
  73.0 0.7 broadcast_in_dim.20
  73.8 4.4 %all-to-all-start = ((bf16[32,16,256]{2,1,0:T(8,128)(2,1)}), bf16[32,16,256]{2,1,0:T(8,128)(2,1)S(1)}, u32[]{:S(2)}, u32[]{:S(2)}) async-start(bf16[32,16,256]{2,1,0:T(8,128)(2,1)} %broadcast_in_dim.20), calls=%async_computation | async-start | bytes 524288 | tf_op jit(solution)/shard_map/all_to_all | solution.py:32
  78.2 4.0 %multiply_reduce_fusion.2 = f32[2048]{0:T(1024)S(1)} fusion(f32[1024,2048]{1,0:T(8,128)} %get-tuple-element.40, f32[1024]{0:T(1024)S(1)} %divide_bitcast_fusion.5), kind=kLoop, calls=%fused_computation.3 | loop fusion | flops 4192256 | bytes 8400896 | tf_op jit(solution)/shard_map/reduce_sum | solution.py:80
  82.3 1.9 collective-permute-start.15
  84.7 1.4 collective-permute-start.14
  86.1 1.8 collective-permute-start.3
  87.9 2.9 %collective-permute-start.2 = (bf16[512,256]{0,1:T(8,128)(2,1)S(1)}, bf16[512,256]{0,1:T(8,128)(2,1)S(1)}, u32[]{:S(2)}, u32[]{:S(2)}) collective-permute-start(bf16[512,256]{0,1:T(8,128)(2,1)S(1)} %fusion.10), channel_id=1, source_target_pairs={{0,32},{16,48},{32,0},{48,16},{1,33},{17,49},{33,1},{49,17},{2,34}... | collective-permute-start | bytes 786440 | tf_op jit(solution)/shard_map/ppermute | solution.py:27
  91.0 4.0 %multiply_reduce_fusion.1 = f32[1024]{0:T(1024)S(1)} fusion(f32[1024,2048]{1,0:T(8,128)} %get-tuple-element.40, f32[2048]{0:T(1024)S(1)} %bitcast.43), kind=kLoop, calls=%fused_computation.2 | loop fusion | flops 4193280 | bytes 8400896 | tf_op jit(solution)/shard_map/reduce_sum | solution.py:81
  96.0 2.4 %collective-permute-done.2 = bf16[512,256]{0,1:T(8,128)(2,1)S(1)} collective-permute-done((bf16[512,256]{0,1:T(8,128)(2,1)S(1)}, bf16[512,256]{0,1:T(8,128)(2,1)S(1)}, u32[]{:S(2)}, u32[]{:S(2)}) %collective-permute-start.2) | collective-permute-done | bytes 262176 | tf_op jit(solution)/shard_map/ppermute | solution.py:27
  98.4 2.8 %collective-permute-done.1 = bf16[512,256]{0,1:T(8,128)(2,1)S(1)} collective-permute-done((bf16[512,256]{0,1:T(8,128)(2,1)S(1)}, bf16[512,256]{0,1:T(8,128)(2,1)S(1)}, u32[]{:S(2)}, u32[]{:S(2)}) %collective-permute-start.1) | collective-permute-done | bytes 262176 | tf_op jit(solution)/shard_map/ppermute | solution.py:27
  101.2 4.2 %fusion = (f32[1024]{0:T(1024)S(1)}, f32[1024,2048]{1,0:T(8,128)}) fusion(bf16[512,256]{0,1:T(8,128)(2,1)S(1)} %collective-permute-done.3, bf16[512,256]{0,1:T(8,128)(2,1)S(1)} %collective-permute-done.2, bf16[512,256]{0,1:T(8,128)(2,1)S(1)} %collective-permute-done.1, bf16[512,256]{0,1:T(8,128)(2,1)S(1)} %fusion.10, ...), kind=kOutput, calls=%fused_computation.8 | convolution fusion | flops 1083177984 | bytes 9965568 | tf_op jit(solution)/shard_map/dot_general | solution.py:20
  105.3 0.7 broadcast_in_dim.27
  106.0 9.9 %all-to-all-start.4 = ((f32[32,8,128]{2,1,0:T(8,128)}), f32[32,8,128]{2,1,0:T(8,128)S(1)}, u32[]{:S(2)}, u32[]{:S(2)}) async-start(f32[32,8,128]{2,1,0:T(8,128)} %broadcast_in_dim.27), calls=%async_computation.4 | async-start | bytes 262144 | tf_op jit(solution)/shard_map/all_to_all | solution.py:32
  116.0 9.5 %all-to-all-done.4 = f32[32,8,128]{2,1,0:T(8,128)S(1)} async-done(((f32[32,8,128]{2,1,0:T(8,128)}), f32[32,8,128]{2,1,0:T(8,128)S(1)}, u32[]{:S(2)}, u32[]{:S(2)}) %all-to-all-start.4) | async-done | bytes 131104 | tf_op jit(solution)/shard_map/all_to_all | solution.py:32
  125.6 4.0 %multiply_reduce_fusion = f32[2048]{0:T(1024)S(1)} fusion(f32[1024,2048]{1,0:T(8,128)} %get-tuple-element.40, f32[1024]{0:T(1024)S(1)} %divide_bitcast_fusion.4), kind=kLoop, calls=%fused_computation.1 | loop fusion | flops 4192256 | bytes 8400896 | tf_op jit(solution)/shard_map/reduce_sum | solution.py:80
  129.7 0.6 collective-permute-start.19
  130.4 1.5 collective-permute-start.17
  131.9 1.8 collective-permute-start.18
  133.7 0.7 broadcast_in_dim.22
  134.3 4.5 %all-to-all-start.1 = ((f32[32,8,128]{2,1,0:T(8,128)}), f32[32,8,128]{2,1,0:T(8,128)S(1)}, u32[]{:S(2)}, u32[]{:S(2)}) async-start(f32[32,8,128]{2,1,0:T(8,128)} %broadcast_in_dim.22), calls=%async_computation.1 | async-start | bytes 262144 | tf_op jit(solution)/shard_map/all_to_all | solution.py:32
  138.9 4.0 %multiply_reduce_fusion.4 = f32[1024]{0:T(1024)S(1)} fusion(f32[1024,2048]{1,0:T(8,128)} %get-tuple-element.40, f32[2048]{0:T(1024)S(1)} %bitcast.40), kind=kLoop, calls=%fused_computation.7 | loop fusion | flops 4193280 | bytes 8400896 | tf_op jit(solution)/shard_map/reduce_sum | solution.py:81
  143.0 1.2 collective-permute-done.20
  144.2 4.4 %all-to-all-done.1 = f32[32,8,128]{2,1,0:T(8,128)S(1)} async-done(((f32[32,8,128]{2,1,0:T(8,128)}), f32[32,8,128]{2,1,0:T(8,128)S(1)}, u32[]{:S(2)}, u32[]{:S(2)}) %all-to-all-start.1) | async-done | bytes 131104 | tf_op jit(solution)/shard_map/all_to_all | solution.py:32
  148.6 0.7 broadcast_in_dim.29
  149.3 5.5 %all-to-all-start.5 = ((f32[32,8,128]{2,1,0:T(8,128)}), f32[32,8,128]{2,1,0:T(8,128)S(1)}, u32[]{:S(2)}, u32[]{:S(2)}) async-start(f32[32,8,128]{2,1,0:T(8,128)} %broadcast_in_dim.29), calls=%async_computation.5 | async-start | bytes 262144 | tf_op jit(solution)/shard_map/all_to_all | solution.py:32
  154.8 10.0 %all-to-all-done.5 = f32[32,8,128]{2,1,0:T(8,128)S(1)} async-done(((f32[32,8,128]{2,1,0:T(8,128)}), f32[32,8,128]{2,1,0:T(8,128)S(1)}, u32[]{:S(2)}, u32[]{:S(2)}) %all-to-all-start.5) | async-done | bytes 131104 | tf_op jit(solution)/shard_map/all_to_all | solution.py:32
  164.8 7.1 %multiply_convert_fusion = bf16[1024,2048]{1,0:T(8,128)(2,1)S(1)} fusion(f32[1024,2048]{1,0:T(8,128)} %get-tuple-element.40, f32[1024,2048]{1,0:T(8,128)} %get-tuple-element.38, f32[1024]{0:T(1024)S(1)} %divide_bitcast_fusion.3, f32[2048]{0:T(1024)S(1)} %bitcast.41, f32[1024]{0:T(1024)S(1)} %bitcast.44), kind=kLoop, calls=%fused_computation | loop fusion | flops 14680064 | bytes 20987904 | tf_op jit(solution)/shard_map/convert_element_type | solution.py:85
  172.0 1.3 fusion.24
  173.4 1.3 fusion.22
  174.8 1.2 fusion.39
  175.9 2.0 collective-permute-start.22
  178.0 1.8 collective-permute-start.23
  179.8 0.9 slice_add_fusion.1
  180.7 4.4 %all-to-all-start.6 = ((f32[32,16,256]{2,1,0:T(8,128)}), f32[32,16,256]{2,1,0:T(8,128)S(1)}, u32[]{:S(2)}, u32[]{:S(2)}) async-start(f32[32,16,256]{2,1,0:T(8,128)} %bitcast.16), calls=%async_computation.6 | async-start | bytes 1048576 | tf_op jit(solution)/shard_map/all_to_all | solution.py:93
  185.1 16.3 %collective-permute-done.22 = f32[512,256]{0,1:T(8,128)S(1)} collective-permute-done((f32[512,256]{0,1:T(8,128)}, f32[512,256]{0,1:T(8,128)S(1)}, u32[]{:S(2)}, u32[]{:S(2)}) %collective-permute-start.22) | collective-permute-done | bytes 524320 | tf_op jit(solution)/shard_map/ppermute | solution.py:27
  201.3 3.4 %collective-permute-done.24 = f32[512,256]{0,1:T(8,128)} collective-permute-done((f32[512,256]{0,1:T(8,128)}, f32[512,256]{0,1:T(8,128)}, u32[]{:S(2)}, u32[]{:S(2)}) %collective-permute-start.24) | collective-permute-done | bytes 524320 | tf_op jit(solution)/shard_map/ppermute | solution.py:27
  204.7 1.4 fusion.11
  206.2 1.0 copy.9
  207.4 0.7 fusion.30
  (102 shorter events, 3.3 us)
Async XLA Ops:
  2.9 23.7 %all-to-all-start.2 = ((bf16[32,16,256]{2,1,0:T(8,128)(2,1)}), bf16[32,16,256]{2,1,0:T(8,128)(2,1)S(1)}, u32[]{:S(2)}, u32[]{:S(2)}) async-start(bf16[32,16,256]{2,1,0:T(8,128)(2,1)} %broadcast_in_dim.23), calls=%async_computation.2 | async-start | bytes 524288 | tf_op jit(solution)/shard_map/all_to_all | solution.py:32
  16.5 13.5 %collective-permute-start.8 = (bf16[512,256]{1,0:T(8,128)(2,1)S(1)}, bf16[512,256]{1,0:T(8,128)(2,1)S(1)}, u32[]{:S(2)}, u32[]{:S(2)}) collective-permute-start(bf16[512,256]{1,0:T(8,128)(2,1)S(1)} %fusion.16), channel_id=1, source_target_pairs={{0,48},{16,0},{32,16},{48,32},{1,49},{17,1},{33,17},{49,33},{2,50}... | collective-permute-start | bytes 786440 | tf_op jit(solution)/shard_map/ppermute | solution.py:27
  19.4 10.8 %collective-permute-start.7 = (bf16[512,256]{1,0:T(8,128)(2,1)S(1)}, bf16[512,256]{1,0:T(8,128)(2,1)S(1)}, u32[]{:S(2)}, u32[]{:S(2)}) collective-permute-start(bf16[512,256]{1,0:T(8,128)(2,1)S(1)} %fusion.16), channel_id=1, source_target_pairs={{0,32},{16,48},{32,0},{48,16},{1,33},{17,49},{33,1},{49,17},{2,34}... | collective-permute-start | bytes 786440 | tf_op jit(solution)/shard_map/ppermute | solution.py:27
  20.2 13.5 %collective-permute-start.6 = (bf16[512,256]{1,0:T(8,128)(2,1)S(1)}, bf16[512,256]{1,0:T(8,128)(2,1)S(1)}, u32[]{:S(2)}, u32[]{:S(2)}) collective-permute-start(bf16[512,256]{1,0:T(8,128)(2,1)S(1)} %fusion.16), channel_id=1, source_target_pairs={{0,16},{16,32},{32,48},{48,0},{1,17},{17,33},{33,49},{49,1},{2,18}... | collective-permute-start | bytes 786440 | tf_op jit(solution)/shard_map/ppermute | solution.py:27
  26.6 7.1 %collective-permute-start.5 = (bf16[512,256]{1,0:T(8,128)(2,1)S(1)}, bf16[512,256]{1,0:T(8,128)(2,1)S(1)}, u32[]{:S(2)}, u32[]{:S(2)}) collective-permute-start(bf16[512,256]{1,0:T(8,128)(2,1)S(1)} %bitcast.38), channel_id=1, source_target_pairs={{0,1},{1,0},{2,3},{3,2},{4,5},{5,4},{6,7},{7,6},{8,9},{9,8},{10,11... | collective-permute-start | bytes 786440 | tf_op jit(solution)/shard_map/ppermute | solution.py:27
  27.8 23.6 %copy-start = (bf16[16,256]{1,0:T(8,128)(2,1)S(1)}, bf16[16,256]{1,0:T(8,128)(2,1)}, u32[]{:S(2)}) copy-start(bf16[16,256]{1,0:T(8,128)(2,1)} %param.4) | copy-start | bytes 24580
  39.8 3.7 %collective-permute-start.11 = (f32[4,512]{1,0:T(4,128)S(1)}, f32[4,512]{1,0:T(4,128)S(1)}, u32[]{:S(2)}, u32[]{:S(2)}) collective-permute-start(f32[4,512]{1,0:T(4,128)S(1)} %pad_maximum_fusion.8), channel_id=1, source_target_pairs={{0,48},{16,0},{32,16},{48,32},{1,49},{17,1},{33,17},{49,33},{2,50}... | collective-permute-start | bytes 24584 | tf_op jit(solution)/shard_map/ppermute | solution.py:27
  40.5 4.9 %collective-permute-start.9 = (f32[4,512]{1,0:T(4,128)S(1)}, f32[4,512]{1,0:T(4,128)S(1)}, u32[]{:S(2)}, u32[]{:S(2)}) collective-permute-start(f32[4,512]{1,0:T(4,128)S(1)} %pad_maximum_fusion.6), channel_id=1, source_target_pairs={{0,16},{16,32},{32,48},{48,0},{1,17},{17,33},{33,49},{49,1},{2,18}... | collective-permute-start | bytes 24584 | tf_op jit(solution)/shard_map/ppermute | solution.py:27
  42.0 5.2 %collective-permute-start.10 = (f32[4,512]{1,0:T(4,128)S(1)}, f32[4,512]{1,0:T(4,128)S(1)}, u32[]{:S(2)}, u32[]{:S(2)}) collective-permute-start(f32[4,512]{1,0:T(4,128)S(1)} %pad_maximum_fusion.7), channel_id=1, source_target_pairs={{0,32},{16,48},{32,0},{48,16},{1,33},{17,49},{33,1},{49,17},{2,34}... | collective-permute-start | bytes 24584 | tf_op jit(solution)/shard_map/ppermute | solution.py:27
  51.3 1.3 collective-permute-start.12
  53.2 19.8 %all-to-all-start.3 = ((f32[32,8,128]{2,1,0:T(8,128)}), f32[32,8,128]{2,1,0:T(8,128)S(1)}, u32[]{:S(2)}, u32[]{:S(2)}) async-start(f32[32,8,128]{2,1,0:T(8,128)} %broadcast_in_dim.25), calls=%async_computation.3 | async-start | bytes 262144 | tf_op jit(solution)/shard_map/all_to_all | solution.py:32
  73.8 17.1 %all-to-all-start = ((bf16[32,16,256]{2,1,0:T(8,128)(2,1)}), bf16[32,16,256]{2,1,0:T(8,128)(2,1)S(1)}, u32[]{:S(2)}, u32[]{:S(2)}) async-start(bf16[32,16,256]{2,1,0:T(8,128)(2,1)} %broadcast_in_dim.20), calls=%async_computation | async-start | bytes 524288 | tf_op jit(solution)/shard_map/all_to_all | solution.py:32
  82.3 8.6 %collective-permute-start.15 = (f32[4,512]{1,0:T(4,128)S(1)}, f32[4,512]{1,0:T(4,128)S(1)}, u32[]{:S(2)}, u32[]{:S(2)}) collective-permute-start(f32[4,512]{1,0:T(4,128)S(1)} %pad_maximum_fusion.11), channel_id=1, source_target_pairs={{0,48},{16,0},{32,16},{48,32},{1,49},{17,1},{33,17},{49,33},{2,50}... | collective-permute-start | bytes 24584 | tf_op jit(solution)/shard_map/ppermute | solution.py:27
  84.2 6.7 %collective-permute-start.13 = (f32[4,512]{1,0:T(4,128)S(1)}, f32[4,512]{1,0:T(4,128)S(1)}, u32[]{:S(2)}, u32[]{:S(2)}) collective-permute-start(f32[4,512]{1,0:T(4,128)S(1)} %pad_maximum_fusion.9), channel_id=1, source_target_pairs={{0,16},{16,32},{32,48},{48,0},{1,17},{17,33},{33,49},{49,1},{2,18}... | collective-permute-start | bytes 24584 | tf_op jit(solution)/shard_map/ppermute | solution.py:27
  84.7 6.3 %collective-permute-start.14 = (f32[4,512]{1,0:T(4,128)S(1)}, f32[4,512]{1,0:T(4,128)S(1)}, u32[]{:S(2)}, u32[]{:S(2)}) collective-permute-start(f32[4,512]{1,0:T(4,128)S(1)} %pad_maximum_fusion.10), channel_id=1, source_target_pairs={{0,32},{16,48},{32,0},{48,16},{1,33},{17,49},{33,1},{49,17},{2,34}... | collective-permute-start | bytes 24584 | tf_op jit(solution)/shard_map/ppermute | solution.py:27
  86.1 9.9 %collective-permute-start.3 = (bf16[512,256]{0,1:T(8,128)(2,1)S(1)}, bf16[512,256]{0,1:T(8,128)(2,1)S(1)}, u32[]{:S(2)}, u32[]{:S(2)}) collective-permute-start(bf16[512,256]{0,1:T(8,128)(2,1)S(1)} %fusion.10), channel_id=1, source_target_pairs={{0,48},{16,0},{32,16},{48,32},{1,49},{17,1},{33,17},{49,33},{2,50}... | collective-permute-start | bytes 786440 | tf_op jit(solution)/shard_map/ppermute | solution.py:27
  87.9 10.5 %collective-permute-start.2 = (bf16[512,256]{0,1:T(8,128)(2,1)S(1)}, bf16[512,256]{0,1:T(8,128)(2,1)S(1)}, u32[]{:S(2)}, u32[]{:S(2)}) collective-permute-start(bf16[512,256]{0,1:T(8,128)(2,1)S(1)} %fusion.10), channel_id=1, source_target_pairs={{0,32},{16,48},{32,0},{48,16},{1,33},{17,49},{33,1},{49,17},{2,34}... | collective-permute-start | bytes 786440 | tf_op jit(solution)/shard_map/ppermute | solution.py:27
  90.8 10.3 %collective-permute-start.1 = (bf16[512,256]{0,1:T(8,128)(2,1)S(1)}, bf16[512,256]{0,1:T(8,128)(2,1)S(1)}, u32[]{:S(2)}, u32[]{:S(2)}) collective-permute-start(bf16[512,256]{0,1:T(8,128)(2,1)S(1)} %fusion.10), channel_id=1, source_target_pairs={{0,16},{16,32},{32,48},{48,0},{1,17},{17,33},{33,49},{49,1},{2,18}... | collective-permute-start | bytes 786440 | tf_op jit(solution)/shard_map/ppermute | solution.py:27
  90.9 10.3 %collective-permute-start = (bf16[512,256]{1,0:T(8,128)(2,1)S(1)}, bf16[512,256]{1,0:T(8,128)(2,1)S(1)}, u32[]{:S(2)}, u32[]{:S(2)}) collective-permute-start(bf16[512,256]{1,0:T(8,128)(2,1)S(1)} %bitcast.35), channel_id=1, source_target_pairs={{0,1},{1,0},{2,3},{3,2},{4,5},{5,4},{6,7},{7,6},{8,9},{9,8},{10,11... | collective-permute-start | bytes 786440 | tf_op jit(solution)/shard_map/ppermute | solution.py:27
  95.1 10.3 %collective-permute-start.16 = (f32[1024]{0:T(1024)S(1)}, f32[1024]{0:T(1024)S(1)}, u32[]{:S(2)}, u32[]{:S(2)}) collective-permute-start(f32[1024]{0:T(1024)S(1)} %pad_maximum_fusion.17), channel_id=1, source_target_pairs={{0,1},{1,0},{2,3},{3,2},{4,5},{5,4},{6,7},{7,6},{8,9},{9,8},{10,11... | collective-permute-start | bytes 12296 | tf_op jit(solution)/shard_map/ppermute | solution.py:27
  101.2 28.5 %copy-start.1 = (bf16[512,256]{1,0:T(8,128)(2,1)}, bf16[512,256]{1,0:T(8,128)(2,1)S(1)}, u32[]{:S(2)}) copy-start(bf16[512,256]{1,0:T(8,128)(2,1)S(1)} %collective-permute-done) | copy-start | bytes 786436
  106.0 19.5 %all-to-all-start.4 = ((f32[32,8,128]{2,1,0:T(8,128)}), f32[32,8,128]{2,1,0:T(8,128)S(1)}, u32[]{:S(2)}, u32[]{:S(2)}) async-start(f32[32,8,128]{2,1,0:T(8,128)} %broadcast_in_dim.27), calls=%async_computation.4 | async-start | bytes 262144 | tf_op jit(solution)/shard_map/all_to_all | solution.py:32
  115.9 17.8 %collective-permute-start.4 = (f32[1024]{0:T(1024)S(1)}, f32[1024]{0:T(1024)S(1)}, u32[]{:S(2)}, u32[]{:S(2)}) collective-permute-start(f32[1024]{0:T(1024)S(1)} %pad_maximum_fusion.15), channel_id=1, source_target_pairs={{0,1},{1,0},{2,3},{3,2},{4,5},{5,4},{6,7},{7,6},{8,9},{9,8},{10,11... | collective-permute-start | bytes 12296 | tf_op jit(solution)/shard_map/ppermute | solution.py:27
  129.7 9.1 %collective-permute-start.19 = (f32[4,512]{1,0:T(4,128)S(1)}, f32[4,512]{1,0:T(4,128)S(1)}, u32[]{:S(2)}, u32[]{:S(2)}) collective-permute-start(f32[4,512]{1,0:T(4,128)S(1)} %pad_maximum_fusion.14), channel_id=1, source_target_pairs={{0,48},{16,0},{32,16},{48,32},{1,49},{17,1},{33,17},{49,33},{2,50}... | collective-permute-start | bytes 24584 | tf_op jit(solution)/shard_map/ppermute | solution.py:27
  130.4 8.5 %collective-permute-start.17 = (f32[4,512]{1,0:T(4,128)S(1)}, f32[4,512]{1,0:T(4,128)S(1)}, u32[]{:S(2)}, u32[]{:S(2)}) collective-permute-start(f32[4,512]{1,0:T(4,128)S(1)} %pad_maximum_fusion.12), channel_id=1, source_target_pairs={{0,16},{16,32},{32,48},{48,0},{1,17},{17,33},{33,49},{49,1},{2,18}... | collective-permute-start | bytes 24584 | tf_op jit(solution)/shard_map/ppermute | solution.py:27
  131.9 7.0 %collective-permute-start.18 = (f32[4,512]{1,0:T(4,128)S(1)}, f32[4,512]{1,0:T(4,128)S(1)}, u32[]{:S(2)}, u32[]{:S(2)}) collective-permute-start(f32[4,512]{1,0:T(4,128)S(1)} %pad_maximum_fusion.13), channel_id=1, source_target_pairs={{0,32},{16,48},{32,0},{48,16},{1,33},{17,49},{33,1},{49,17},{2,34}... | collective-permute-start | bytes 24584 | tf_op jit(solution)/shard_map/ppermute | solution.py:27
  134.3 14.3 %all-to-all-start.1 = ((f32[32,8,128]{2,1,0:T(8,128)}), f32[32,8,128]{2,1,0:T(8,128)S(1)}, u32[]{:S(2)}, u32[]{:S(2)}) async-start(f32[32,8,128]{2,1,0:T(8,128)} %broadcast_in_dim.22), calls=%async_computation.1 | async-start | bytes 262144 | tf_op jit(solution)/shard_map/all_to_all | solution.py:32
  142.9 1.3 collective-permute-start.20
  149.3 15.5 %all-to-all-start.5 = ((f32[32,8,128]{2,1,0:T(8,128)}), f32[32,8,128]{2,1,0:T(8,128)S(1)}, u32[]{:S(2)}, u32[]{:S(2)}) async-start(f32[32,8,128]{2,1,0:T(8,128)} %broadcast_in_dim.29), calls=%async_computation.5 | async-start | bytes 262144 | tf_op jit(solution)/shard_map/all_to_all | solution.py:32
  172.0 1.5 copy-start.2
  173.3 6.5 %collective-permute-start.21 = (f32[512,256]{1,0:T(8,128)S(1)}, f32[512,256]{1,0:T(8,128)S(1)}, u32[]{:S(2)}, u32[]{:S(2)}) collective-permute-start(f32[512,256]{1,0:T(8,128)S(1)} %slice.325), channel_id=1, source_target_pairs={{0,1},{1,0},{2,3},{3,2},{4,5},{5,4},{6,7},{7,6},{8,9},{9,8},{10,11... | collective-permute-start | bytes 1572872 | tf_op jit(solution)/shard_map/ppermute | solution.py:27
  175.9 25.4 %collective-permute-start.22 = (f32[512,256]{0,1:T(8,128)}, f32[512,256]{0,1:T(8,128)S(1)}, u32[]{:S(2)}, u32[]{:S(2)}) collective-permute-start(f32[512,256]{0,1:T(8,128)} %get-tuple-element.8), channel_id=1, source_target_pairs={{0,48},{16,0},{32,16},{48,32},{1,49},{17,1},{33,17},{49,33},{2,50}... | collective-permute-start | bytes 1572872 | tf_op jit(solution)/shard_map/ppermute | solution.py:27
  177.9 26.8 %collective-permute-start.24 = (f32[512,256]{0,1:T(8,128)}, f32[512,256]{0,1:T(8,128)}, u32[]{:S(2)}, u32[]{:S(2)}) collective-permute-start(f32[512,256]{0,1:T(8,128)} %get-tuple-element.9), channel_id=1, source_target_pairs={{0,16},{16,32},{32,48},{48,0},{1,17},{17,33},{33,49},{49,1},{2,18}... | collective-permute-start | bytes 1572872 | tf_op jit(solution)/shard_map/ppermute | solution.py:27
  178.0 26.7 %collective-permute-start.23 = (f32[512,256]{0,1:T(8,128)}, f32[512,256]{0,1:T(8,128)}, u32[]{:S(2)}, u32[]{:S(2)}) collective-permute-start(f32[512,256]{0,1:T(8,128)} %get-tuple-element.10), channel_id=1, source_target_pairs={{0,32},{16,48},{32,0},{48,16},{1,33},{17,49},{33,1},{49,17},{2,34}... | collective-permute-start | bytes 1572872 | tf_op jit(solution)/shard_map/ppermute | solution.py:27
  180.7 26.5 %all-to-all-start.6 = ((f32[32,16,256]{2,1,0:T(8,128)}), f32[32,16,256]{2,1,0:T(8,128)S(1)}, u32[]{:S(2)}, u32[]{:S(2)}) async-start(f32[32,16,256]{2,1,0:T(8,128)} %bitcast.16), calls=%async_computation.6 | async-start | bytes 1048576 | tf_op jit(solution)/shard_map/all_to_all | solution.py:93

commit v2 on v1

v2 whole, which is shorter than its diff:
```python
import functools

import jax
import jax.numpy as jnp
from jax import lax
from jax.experimental import pallas as pl
from jax.experimental.pallas import tpu as pltpu
from jax.sharding import Mesh, PartitionSpec as P

SWEEPS = 3
TEACHER_TEMP = 0.04
STUDENT_TEMP = 0.1
EPSILON = 1e-06
ROWS = ("y", "z")
STEPS = 4
LANES = 128
TILE = 256

f32 = jnp.float32
bf16 = jnp.bfloat16
VMEM = pl.BlockSpec(memory_space=pltpu.VMEM)


def inverse_norm(values):
    return lax.rsqrt(jnp.sum(values * values, axis=1, keepdims=True) + EPSILON)


def unit(raw):
    values = raw.astype(f32)
    return (values * inverse_norm(values)).astype(bf16)


def call(kernel, outs, operands, flops, name):
    return pl.pallas_call(
        kernel,
        out_shape=outs,
        in_specs=[VMEM] * len(operands),
        out_specs=jax.tree.map(lambda unused: VMEM, outs),
        compiler_params=pltpu.CompilerParams(vmem_limit_bytes=16 * 2**20),
        cost_estimate=pl.CostEstimate(flops=flops, bytes_accessed=2**20, transcendentals=0),
        name=name,
    )(*operands)


def column(values):
    return jnp.broadcast_to(values, (LANES, LANES)).T


def row_of_sums(block):
    return jnp.sum(block.T, axis=0, keepdims=True)


def lane_sum(values):
    total = values[:, :LANES]
    for at in range(LANES, values.shape[1], LANES):
        total = total + values[:, at : at + LANES]
    return total


def store_rolled(outs, block, values):
    for step, out in enumerate(outs):
        at = (block + step) % STEPS
        out[at : at + 1, :] = values


def load_features(first, own, sib, protos, feat_ref, weight_ref):
    half, block, width = own.shape[0], protos[0].shape[0], protos[0].shape[1]
    feat_ref[:half, :] = unit(own[:, first : first + width])
    feat_ref[half:, :] = unit(sib[:, first : first + width])
    for k, proto in enumerate(protos):
        weight_ref[k * block : (k + 1) * block, :] = unit(proto[...])


def scores(rows, weights):
    return lax.dot_general(rows, weights, (((1,), (1,)), ((), ())), preferred_element_type=f32)


def teacher_kernel(own, sib, p0, p1, p2, p3, exp_ref, m0, m1, m2, m3, feat_ref, weight_ref):
    load_features(0, own, sib, (p0, p1, p2, p3), feat_ref, weight_ref)
    rows, block = feat_ref.shape[0], p0.shape[0]
    for k in range(STEPS):
        cols = slice(k * block, (k + 1) * block)
        total = jnp.zeros((8, block), f32)
        for at in range(0, rows, TILE):
            r = slice(at, at + TILE)
            part = jnp.exp(scores(feat_ref[r, :], weight_ref[cols, :]) * (1.0 / TEACHER_TEMP))
            exp_ref[r, cols] = part
            total = total + jnp.sum(part.reshape(TILE // 8, 8, block), axis=0)
        store_rolled((m0, m1, m2, m3), k, jnp.sum(total, axis=0, keepdims=True))


def student_kernel(own, sib, p0, p1, p2, p3, exp_ref, sum_ref, feat_ref, weight_ref):
    width, block = p0.shape[1], p0.shape[0]
    load_features(width, own, sib, (p0, p1, p2, p3), feat_ref, weight_ref)
    rows = feat_ref.shape[0]
    for at in range(0, rows, TILE):
        r = slice(at, at + TILE)
        total = jnp.zeros((TILE, LANES), f32)
        for k in range(STEPS):
            cols = slice(k * block, (k + 1) * block)
            part = jnp.exp(scores(feat_ref[r, :], weight_ref[cols, :]) * (1.0 / STUDENT_TEMP))
            exp_ref[r, cols] = part
            total = total + lane_sum(part)
        for t in range(TILE // LANES):
            i = at // LANES + t
            sum_ref[i : i + 1, :] = row_of_sums(total[t * LANES : (t + 1) * LANES])


def column_kernel(exp_ref, mass_ref, m0, m1, m2, m3):
    scale = 1.0 / jnp.sum(mass_ref[...], axis=0)
    rows, cols = exp_ref.shape
    block = cols // STEPS
    wide = 2 * block
    for h in range(cols // wide):
        total = jnp.zeros((8, wide), f32)
        for i in range(rows // LANES):
            col = column(scale[i : i + 1, :])
            for j in range(0, LANES, 8):
                at = i * LANES + j
                factor = jnp.concatenate([col[j : j + 8, :]] * (wide // LANES), axis=1)
                total = total + exp_ref[at : at + 8, h * wide : (h + 1) * wide] * factor
        whole = jnp.sum(total, axis=0, keepdims=True)
        for b in range(2):
            store_rolled((m0, m1, m2, m3), 2 * h + b, whole[:, b * block : (b + 1) * block])


def row_kernel(exp_ref, m0, m1, m2, m3, *refs):
    extra, (out_ref, swap_ref, scale_ref) = refs[:-3], refs[-3:]
    scale = 1.0 / (m0[...] + m1[...] + m2[...] + m3[...])
    scale_ref[...] = scale
    rows, cols = exp_ref.shape
    block = cols // STEPS
    count = rows // LANES
    for i in range(count):
        total = jnp.zeros((LANES, LANES), f32)
        for at in range(0, cols, LANES):
            k, o = at // block, at % block
            r = slice(i * LANES, (i + 1) * LANES)
            total = total + exp_ref[r, at : at + LANES] * scale[k : k + 1, o : o + LANES]
        out_ref[i : i + 1, :] = row_of_sums(total)
    for ref in extra:
        out_ref[count : 2 * count, :] = ref[...]
    for at in range(0, out_ref.shape[0], count):
        swap_ref[at : at + count // 2, :] = out_ref[at + count // 2 : at + count, :]
        swap_ref[at + count // 2 : at + count, :] = out_ref[at : at + count // 2, :]


def logits_kernel(factor, exp_t, exp_s, scale_ref, mass_ref, weight_ref, grad_ref, feat_ref):
    inverse = factor / jnp.sum(mass_ref[...], axis=0)
    rows, cols = exp_t.shape
    count, block = rows // LANES, cols // STEPS
    for i in range(count):
        r = slice(i * LANES, (i + 1) * LANES)
        row = column(inverse[i : i + 1, :])
        total = column(inverse[count + i : count + i + 1, :])
        for at in range(0, cols, LANES):
            k, o = at // block, at % block
            c = slice(at, at + LANES)
            target = exp_t[r, c] * scale_ref[k : k + 1, o : o + LANES] * row
            grad_ref[r, c] = (exp_s[r, c] * total - target).astype(bf16)
    feat_ref[...] = jnp.dot(grad_ref[...], weight_ref[...], preferred_element_type=f32)


def weight_kernel(grad_ref, feat_ref, *outs):
    block = outs[0].shape[0]
    for k, out in enumerate(outs):
        out[...] = lax.dot_general(
            grad_ref[:, k * block : (k + 1) * block],
            feat_ref[...],
            (((0,), (0,)), ((), ())),
            preferred_element_type=f32,
        )


def project(raw, grads):
    values = raw.astype(f32)
    inverse = inverse_norm(values)
    unit_rows = values * inverse
    return (grads - unit_rows * jnp.sum(unit_rows * grads, axis=1, keepdims=True)) * inverse


def row_grad_kernel(raw, parts, out):
    out[...] = project(raw[...], jnp.sum(parts[...], axis=0))


def proto_grad_kernel(raw, w0, w1, w2, w3, out):
    out[...] = project(raw[...], w0[...] + w1[...] + w2[...] + w3[...])


def shift(values, axis, step):
    size = lax.axis_size(axis)
    return lax.ppermute(values, axis, [(i, (i + step) % size) for i in range(size)])


def spread(values):
    count = lax.axis_size(ROWS)
    return lax.all_to_all(
        jnp.broadcast_to(values[None], (count,) + values.shape), ROWS, 0, 0, tiled=True
    )


def gather_protos(raw):
    return [raw] + [shift(raw, "x", k) for k in range(1, STEPS)]


def share(blocks):
    return [blocks[0]] + [shift(blocks[k], "x", k) for k in range(1, STEPS)]


def share_rows(mine, swapped):
    return spread(mine + shift(swapped, "core", 1))


def body(student_rows, teacher_rows, student_protos, teacher_protos):
    own_rows, width = student_rows.shape
    own_protos = student_protos.shape[0]
    rows = own_rows * lax.axis_size(ROWS) * lax.axis_size("core")
    cols = own_protos * STEPS
    factor = own_protos * 256 / 16.0
    work = 2 * rows * cols * width

    exps = pltpu.VMEM((rows, cols), f32)
    masses = [jax.ShapeDtypeStruct((STEPS, own_protos), f32)] * STEPS
    sums = jax.ShapeDtypeStruct((rows // LANES, LANES), f32)
    feats = pltpu.VMEM((rows, width), bf16)
    weights = pltpu.VMEM((cols, width), bf16)

    teacher_blocks = gather_protos(teacher_protos)
    student_blocks = gather_protos(student_protos)
    own = spread(jnp.concatenate([teacher_rows, student_rows], axis=1)).reshape(-1, 2 * width)
    sib = shift(own, "core", 1)

    exp_t, *mass = call(
        teacher_kernel, [exps] + masses + [feats, weights], (own, sib, *teacher_blocks), work, "teacher"
    )
    mass = mass[:STEPS]
    exp_s, student_sums, student_feat, student_weight = call(
        student_kernel, [exps, sums, feats, weights], (own, sib, *student_blocks), work, "student"
    )
    for sweep in range(SWEEPS):
        last = sweep + 1 == SWEEPS
        extra = (student_sums,) if last else ()
        out = jax.ShapeDtypeStruct((rows // LANES * (1 + len(extra)), LANES), f32)
        mine, swapped, scale = call(
            row_kernel, [out, out, masses[0]], (exp_t, *share(mass), *extra), work // 8, "rows"
        )
        row_masses = share_rows(mine, swapped)
        if not last:
            mass = call(column_kernel, masses, (exp_t, row_masses), work // 8, "columns")

    grads, feat_grad = call(
        functools.partial(logits_kernel, factor),
        [pltpu.VMEM((rows, cols), bf16), jax.ShapeDtypeStruct((rows, width), f32)],
        (exp_t, exp_s, scale, row_masses, student_weight),
        work,
        "logits",
    )
    weight_parts = call(
        weight_kernel,
        [jax.ShapeDtypeStruct((own_protos, width), f32)] * STEPS,
        (grads, student_feat),
        work,
        "weights",
    )
    half = rows // 2
    feat_pair = feat_grad[:half] + shift(feat_grad[half:], "core", 1)
    feat_share = lax.all_to_all(feat_pair.reshape(-1, own_rows, width), ROWS, 0, 0, tiled=True)
    weight_share = [weight_parts[0]] + [shift(weight_parts[k], "x", -k) for k in range(1, STEPS)]
    row_grad = call(
        row_grad_kernel,
        jax.ShapeDtypeStruct((own_rows, width), f32),
        (student_rows, feat_share),
        rows * width,
        "row_grad",
    )
    proto_grad = call(
        proto_grad_kernel,
        jax.ShapeDtypeStruct((own_protos, width), f32),
        (student_protos, *weight_share),
        own_protos * width,
        "proto_grad",
    )
    return (row_grad, proto_grad)


def solution(mesh):
    fine = Mesh(mesh.devices.reshape(4, 4, 8, 2), ("y", "x", "z", "core"))
    rows = P(("y", "x", "z", "core"), None)
    protos = P(("z", "core", "y", "x"), None)
    return jax.shard_map(
        body,
        mesh=fine,
        in_specs=(rows, rows, protos, protos),
        out_specs=(rows, protos),
        check_vma=False,
    )
```

time: 210 us -> 180 us (0.86)
  blocking collectives: 0 us -> 63.6 us
  starting transfers between devices: 74.6 us -> 35.1 us
  other arithmetic: 34.9 us -> 1.59 us
  waiting for transfers between devices: 77.1 us -> 53.8 us
  Pallas kernels: 0 us -> 14 us
  matrix products: 12.8 us -> 0 us
    all_to_all x0 -> x3, blocking collectives: none -> 63.6 us  [spread(): lax.all_to_all(jnp.broadcast_to(values[None], (count,) + values.shape), R...]
    all_to_all x6 -> x1, starting transfers between devices: 45.4 us -> 4.35 us  [spread(): lax.all_to_all(jnp.broadcast_to(values[None], (count,) + values.shape), R...]
    all_to_all x6 -> x1, waiting for transfers between devices: 39.4 us -> 7.35 us  [spread(): lax.all_to_all(jnp.broadcast_to(values[None], (count,) + values.shape), R...]
    reduce_sum x16 -> x0, other arithmetic: 23.9 us -> none  [the longest x3 12.1 us: body(): jnp.sum(teacher_exp * col_scale[None, :], axis=1)]
    pallas_call x0 -> x11, Pallas kernels: none -> 14 us  [call(): pl.pallas_call(kernel, out_shape=outs, in_specs=[VMEM] * len(operands), o...]
    dot_general x4 -> x0, matrix products: 12.8 us -> none  [the longest x2 10.2 us: scores(): lax.dot_general(rows, weights, (((1,), (1,)), ((), ())), preferred_elemen...]
    convert_element_type x5 -> x0, other arithmetic: 9.1 us -> none  [the longest x1 7.12 us: body(): grad_logits = ((prob - target) * factor).astype(jnp.bfloat16)]
    ppermute x25 -> x23, waiting for transfers between devices: 37.6 us -> 46.5 us  [shift(): lax.ppermute(values, axis, [(i, (i + step) % size) for i in range(size)])]
  transfers between devices with their start and end apart: 32 -> 25, of which waited for: 18 -> 17; matrix products, arithmetic and copies ran while one was open for 15% -> 0% of each run, Pallas kernels for 0% -> 3%
where the time goes in v2:
time: 180 us; the launch traced here: 178 us
  blocking collectives  63.6 us (35%)
  waiting for transfers between devices  53.8 us (30%)
  starting transfers between devices  35.1 us (20%)
  Pallas kernels  14 us (8%)
  local copies, waits for them, and re-layouts  9.29 us (5%)
    all_to_all x3, blocking collectives, spread(): lax.all_to_all(jnp.broadcast_to(values[None], (count,) + values.shape), R...  63.6 us
    ppermute x23, waiting for transfers between devices, shift(): lax.ppermute(values, axis, [(i, (i + step) % size) for i in range(size)])  46.5 us
    ppermute x23, starting transfers between devices, shift(): lax.ppermute(values, axis, [(i, (i + step) % size) for i in range(size)])  26.2 us
    pallas_call x11, Pallas kernels, call(): pl.pallas_call(kernel, out_shape=outs, in_specs=[VMEM] * len(operands), o...  14 us
    unnamed x16, local copies, waits for them, and re-layouts  8.5 us
    all_to_all x1, waiting for transfers between devices, spread(): lax.all_to_all(jnp.broadcast_to(values[None], (count,) + values.shape), R...  7.35 us
    all_to_all x1, starting transfers between devices, body(): lax.all_to_all(feat_pair.reshape(-1, own_rows, width), ROWS, 0, 0, tiled=...  4.56 us
    all_to_all x1, starting transfers between devices, spread(): lax.all_to_all(jnp.broadcast_to(values[None], (count,) + values.shape), R...  4.35 us
  transfers between devices with their start and end apart: 25, of which 17 were waited for; matrix products, arithmetic and copies ran while one was open for 0% of the time, Pallas kernels for 3%

profile of v2, /device:TPU:32, one launch (start us, length us, event | category | flops | bytes accessed | tf_op | source)
XLA Modules:
  0.0 178.2 jit_solution(15618877788191949611)
XLA Ops:
  0.6 0.7 pad_maximum_fusion
  1.3 0.1 broadcast_in_dim.8
  1.4 28.8 %all_to_all.25 = bf16[32,16,512]{2,1,0:T(8,128)(2,1)S(1)} all-to-all(bf16[32,16,512]{2,1,0:T(8,128)(2,1)S(1)} %broadcast_in_dim.8), channel_id=1, replica_groups=mesh['y'=4,'x'=4,'z'=8,'core'=2] {'y','z'}, dimensions={0} | all-to-all | bytes 1048576 | tf_op jit(solution)/shard_map/all_to_all | solution.py:197
  30.2 0.0 collective-permute-start
  30.2 3.0 %collective-permute-start.2 = (bf16[512,256]{1,0:T(8,128)(2,1)}, bf16[512,256]{1,0:T(8,128)(2,1)S(1)}, u32[]{:S(2)}, u32[]{:S(2)}) collective-permute-start(bf16[512,256]{1,0:T(8,128)(2,1)} %p0.2), channel_id=1, source_target_pairs={{0,32},{16,48},{32,0},{48,16},{1,33},{17,49},{33,1},{49,17},{2,34}... | collective-permute-start | bytes 786440 | tf_op jit(solution)/shard_map/ppermute | solution.py:192
  33.2 0.6 collective-permute-start.1
  33.8 2.6 %collective-permute-start.3 = (bf16[512,256]{1,0:T(8,128)(2,1)}, bf16[512,256]{1,0:T(8,128)(2,1)S(1)}, u32[]{:S(2)}, u32[]{:S(2)}) collective-permute-start(bf16[512,256]{1,0:T(8,128)(2,1)} %p0.2), channel_id=1, source_target_pairs={{0,48},{16,0},{32,16},{48,32},{1,49},{17,1},{33,17},{49,33},{2,50}... | collective-permute-start | bytes 786440 | tf_op jit(solution)/shard_map/ppermute | solution.py:192
  36.4 4.6 %collective-permute-done.2.p2 = bf16[512,256]{1,0:T(8,128)(2,1)S(1)} collective-permute-done((bf16[512,256]{1,0:T(8,128)(2,1)}, bf16[512,256]{1,0:T(8,128)(2,1)S(1)}, u32[]{:S(2)}, u32[]{:S(2)}) %collective-permute-start.2) | collective-permute-done | bytes 262176 | tf_op jit(solution)/shard_map/ppermute | solution.py:192
  41.0 5.2 %collective-permute-done.1.p1 = bf16[512,256]{1,0:T(8,128)(2,1)S(1)} collective-permute-done((bf16[512,256]{1,0:T(8,128)(2,1)}, bf16[512,256]{1,0:T(8,128)(2,1)S(1)}, u32[]{:S(2)}, u32[]{:S(2)}) %collective-permute-start.1) | collective-permute-done | bytes 262176 | tf_op jit(solution)/shard_map/ppermute | solution.py:192
  46.2 0.1 collective-permute-done.3.p3
  46.4 0.9 copy-done.7
  47.3 2.5 %teacher.1 = (f32[1024,2048]{1,0:T(8,128)S(1)}, f32[4,512]{1,0:T(4,128)S(1)}, f32[4,512]{1,0:T(4,128)S(1)}, f32[4,512]{1,0:T(4,128)S(1)}, f32[4,512]{1,0:T(4,128...) custom-call(bf16[512,512]{1,0:T(8,128)(2,1)S(1)} %bitcast.3, bf16[512,512]{1,0:T(8,128)(2,1)S(1)} %collective-permute-done.sib, ...), custom_call_target="tpu_custom_call" | custom-call | flops 1073741824 | bytes 1048576 | tf_op jit(solution)/shard_map/teacher/pallas_call | solution.py:34
  49.8 1.5 collective-permute-start.7
  51.3 2.6 %collective-permute-start.8 = (f32[4,512]{1,0:T(4,128)S(1)}, f32[4,512]{1,0:T(4,128)S(1)}, u32[]{:S(2)}, u32[]{:S(2)}) collective-permute-start(f32[4,512]{1,0:T(4,128)S(1)} %get-tuple-element.36), channel_id=1, source_target_pairs={{0,32},{16,48},{32,0},{48,16},{1,33},{17,49},{33,1},{49,17},{2,34}... | collective-permute-start | bytes 24584 | tf_op jit(solution)/shard_map/ppermute | solution.py:192
  53.9 0.6 collective-permute-start.9
  54.5 0.2 collective-permute-done.7.m1
  54.7 1.7 collective-permute-done.8.m2
  56.4 1.1 collective-permute-done.9.m3
  57.6 0.7 rows.3
  58.3 0.0 collective-permute-start.10
  58.3 1.2 collective-permute-done.10
  59.5 14.7 %all_to_all.26.mass_ref = f32[32,8,128]{2,1,0:T(8,128)S(1)} all-to-all(f32[32,8,128]{2,1,0:T(8,128)S(1)} %broadcast_in_dim.9), channel_id=1, replica_groups=mesh['y'=4,'x'=4,'z'=8,'core'=2] {'y','z'}, dimensions={0} | all-to-all | bytes 262144 | tf_op jit(solution)/shard_map/all_to_all | solution.py:197
  74.2 0.7 columns.2
  74.9 0.1 collective-permute-start.11
  75.0 3.3 %collective-permute-start.12 = (f32[4,512]{1,0:T(4,128)S(1)}, f32[4,512]{1,0:T(4,128)S(1)}, u32[]{:S(2)}, u32[]{:S(2)}) collective-permute-start(f32[4,512]{1,0:T(4,128)S(1)} %get-tuple-element.42), channel_id=1, source_target_pairs={{0,32},{16,48},{32,0},{48,16},{1,33},{17,49},{33,1},{49,17},{2,34}... | collective-permute-start | bytes 24584 | tf_op jit(solution)/shard_map/ppermute | solution.py:192
  78.2 0.9 collective-permute-start.13
  79.1 0.7 collective-permute-done.11.m1
  79.8 0.4 collective-permute-done.12.m2
  80.2 1.7 collective-permute-done.13.m3
  81.9 0.7 rows.4
  82.6 0.0 collective-permute-start.14
  82.6 1.2 collective-permute-done.14
  83.8 0.7 broadcast_in_dim.10
  84.5 4.3 %all-to-all-start.2 = ((f32[32,8,128]{2,1,0:T(8,128)}), f32[32,8,128]{2,1,0:T(8,128)S(1)}, u32[]{:S(2)}, u32[]{:S(2)}) async-start(f32[32,8,128]{2,1,0:T(8,128)} %broadcast_in_dim.10), calls=%async_computation.2 | async-start | bytes 262144 | tf_op jit(solution)/shard_map/all_to_all | solution.py:197
  88.8 2.2 %collective-permute-start.6 = (bf16[512,256]{1,0:T(8,128)(2,1)S(1)}, bf16[512,256]{1,0:T(8,128)(2,1)S(1)}, u32[]{:S(2)}, u32[]{:S(2)}) collective-permute-start(bf16[512,256]{1,0:T(8,128)(2,1)S(1)} %copy-done.5), channel_id=1, source_target_pairs={{0,48},{16,0},{32,16},{48,32},{1,49},{17,1},{33,17},{49,33},{2,50}... | collective-permute-start | bytes 786440 | tf_op jit(solution)/shard_map/ppermute | solution.py:192
  91.0 0.8 collective-permute-start.5
  91.8 0.1 collective-permute-start.4
  92.0 7.3 %all-to-all-done.2.mass_ref = f32[32,8,128]{2,1,0:T(8,128)S(1)} async-done(((f32[32,8,128]{2,1,0:T(8,128)}), f32[32,8,128]{2,1,0:T(8,128)S(1)}, u32[]{:S(2)}, u32[]{:S(2)}) %all-to-all-start.2) | async-done | bytes 131104 | tf_op jit(solution)/shard_map/all_to_all | solution.py:197
  99.3 3.4 %copy-done.1 = f32[1024,2048]{1,0:T(8,128)S(1)} copy-done((f32[1024,2048]{1,0:T(8,128)S(1)}, f32[1024,2048]{1,0:T(8,128)}, u32[]{:S(2)}) %copy-start.1) | copy-done | bytes 8388632
  102.7 0.7 columns.3
  103.4 0.9 collective-permute-start.15
  104.3 2.7 %collective-permute-start.16 = (f32[4,512]{1,0:T(4,128)S(1)}, f32[4,512]{1,0:T(4,128)S(1)}, u32[]{:S(2)}, u32[]{:S(2)}) collective-permute-start(f32[4,512]{1,0:T(4,128)S(1)} %get-tuple-element.48), channel_id=1, source_target_pairs={{0,32},{16,48},{32,0},{48,16},{1,33},{17,49},{33,1},{49,17},{2,34}... | collective-permute-start | bytes 24584 | tf_op jit(solution)/shard_map/ppermute | solution.py:192
  107.0 0.0 collective-permute-done.6.p3
  107.0 0.6 collective-permute-start.17
  107.6 2.3 %student.1 = (f32[1024,2048]{1,0:T(8,128)S(1)}, f32[8,128]{1,0:T(8,128)S(1)}, bf16[1024,256]{1,0:T(8,128)(2,1)S(1)}, bf16[2048,256]{1,0:T(8,128)(2,1)S(1)}) custom-call(bf16[512,512]{1,0:T(8,128)(2,1)S(1)} %bitcast.4, bf16[512,512]{1,0:T(8,128)(2,1)S(1)} %collective-permute-done.sib, bf16[512,256]{1,0:T(8,128)(2,1)S(1)} %copy-done.5, ...), custom_call_target="tpu_custom_call" | custom-call | flops 1073741824 | bytes 1048576 | tf_op jit(solution)/shard_map/student/pallas_call | solution.py:34
  110.0 0.7 collective-permute-done.17.m3
  110.7 0.6 rows.5
  111.3 0.1 collective-permute-start.18
  111.4 1.2 collective-permute-done.18
  112.6 20.1 %all_to_all.27.mass_ref = f32[32,16,128]{2,1,0:T(8,128)S(1)} all-to-all(f32[32,16,128]{2,1,0:T(8,128)S(1)} %broadcast_in_dim.11), channel_id=1, replica_groups=mesh['y'=4,'x'=4,'z'=8,'core'=2] {'y','z'}, dimensions={0} | all-to-all | bytes 524288 | tf_op jit(solution)/shard_map/all_to_all | solution.py:197
  132.7 2.5 %logits.1 = (bf16[1024,2048]{1,0:T(8,128)(2,1)S(1)}, f32[1024,256]{1,0:T(8,128)S(1)}) custom-call(f32[1024,2048]{1,0:T(8,128)S(1)} %copy-done.2, f32[1024,2048]{1,0:T(8,128)S(1)} %get-tuple-element.33.exp_s, f32[4,512]{1,0:T(4,128)S(1)} %get-tuple-element.51.scale_ref, f32[32,16,128]{2,1,0:T(8,128)S(1)} %all_to_all.27.mass_ref, ...), custom_call_target="tpu_custom_call" | custom-call | flops 1073741824 | bytes 1048576 | tf_op jit(solution)/shard_map/logits/pallas_call | solution.py:34
  135.2 2.0 %copy-done.3 = bf16[1024,2048]{1,0:T(8,128)(2,1)} copy-done((bf16[1024,2048]{1,0:T(8,128)(2,1)}, bf16[1024,2048]{1,0:T(8,128)(2,1)S(1)}, u32[]{:S(2)}) %copy-start.3) | copy-done | bytes 4194328
  137.2 0.1 collective-permute-start.19
  137.3 1.9 %collective-permute-done.19 = f32[512,256]{1,0:T(8,128)S(1)} collective-permute-done((f32[512,256]{1,0:T(8,128)S(1)}, f32[512,256]{1,0:T(8,128)S(1)}, u32[]{:S(2)}, u32[]{:S(2)}) %collective-permute-start.19) | collective-permute-done | bytes 524320 | tf_op jit(solution)/shard_map/ppermute | solution.py:192
  139.2 0.9 slice_add_fusion
  140.1 4.6 %all-to-all-start.4 = ((f32[32,16,256]{2,1,0:T(8,128)}), f32[32,16,256]{2,1,0:T(8,128)S(1)}, u32[]{:S(2)}, u32[]{:S(2)}) async-start(f32[32,16,256]{2,1,0:T(8,128)} %bitcast.1), calls=%async_computation.4 | async-start | bytes 1048576 | tf_op jit(solution)/shard_map/all_to_all | solution.py:267
  144.7 2.2 %copy-done.4 = bf16[1024,2048]{1,0:T(8,128)(2,1)S(1)} copy-done((bf16[1024,2048]{1,0:T(8,128)(2,1)S(1)}, bf16[1024,2048]{1,0:T(8,128)(2,1)}, u32[]{:S(2)}) %copy-start.4) | copy-done | bytes 4194328
  146.9 1.3 weights.1
  148.2 2.5 %collective-permute-start.20 = (f32[512,256]{1,0:T(8,128)S(1)}, f32[512,256]{1,0:T(8,128)S(1)}, u32[]{:S(2)}, u32[]{:S(2)}) collective-permute-start(f32[512,256]{1,0:T(8,128)S(1)} %get-tuple-element.59), channel_id=1, source_target_pairs={{0,48},{16,0},{32,16},{48,32},{1,49},{17,1},{33,17},{49,33},{2,50}... | collective-permute-start | bytes 1572872 | tf_op jit(solution)/shard_map/ppermute | solution.py:192
  150.7 1.0 collective-permute-start.22
  151.7 21.2 %collective-permute-done.20.w1 = f32[512,256]{1,0:T(8,128)S(1)} collective-permute-done((f32[512,256]{1,0:T(8,128)S(1)}, f32[512,256]{1,0:T(8,128)S(1)}, u32[]{:S(2)}, u32[]{:S(2)}) %collective-permute-start.20) | collective-permute-done | bytes 524320 | tf_op jit(solution)/shard_map/ppermute | solution.py:192
  172.9 3.4 %collective-permute-done.22.w3 = f32[512,256]{1,0:T(8,128)S(1)} collective-permute-done((f32[512,256]{1,0:T(8,128)S(1)}, f32[512,256]{1,0:T(8,128)S(1)}, u32[]{:S(2)}, u32[]{:S(2)}) %collective-permute-start.22) | collective-permute-done | bytes 524320 | tf_op jit(solution)/shard_map/ppermute | solution.py:192
  176.3 1.1 proto_grad.1
  177.4 0.8 row_grad.1
  (26 shorter events, 0.1 us)
Async XLA Ops:
  30.2 16.2 %collective-permute-start = (bf16[512,512]{1,0:T(8,128)(2,1)S(1)}, bf16[512,512]{1,0:T(8,128)(2,1)S(1)}, u32[]{:S(2)}, u32[]{:S(2)}) collective-permute-start(bf16[512,512]{1,0:T(8,128)(2,1)S(1)} %bitcast.2), channel_id=1, source_target_pairs={{0,1},{1,0},{2,3},{3,2},{4,5},{5,4},{6,7},{7,6},{8,9},{9,8},{10,11... | collective-permute-start | bytes 1572872 | tf_op jit(solution)/shard_map/ppermute | solution.py:192
  30.2 10.9 %collective-permute-start.2 = (bf16[512,256]{1,0:T(8,128)(2,1)}, bf16[512,256]{1,0:T(8,128)(2,1)S(1)}, u32[]{:S(2)}, u32[]{:S(2)}) collective-permute-start(bf16[512,256]{1,0:T(8,128)(2,1)} %p0.2), channel_id=1, source_target_pairs={{0,32},{16,48},{32,0},{48,16},{1,33},{17,49},{33,1},{49,17},{2,34}... | collective-permute-start | bytes 786440 | tf_op jit(solution)/shard_map/ppermute | solution.py:192
  33.2 13.0 %collective-permute-start.1 = (bf16[512,256]{1,0:T(8,128)(2,1)}, bf16[512,256]{1,0:T(8,128)(2,1)S(1)}, u32[]{:S(2)}, u32[]{:S(2)}) collective-permute-start(bf16[512,256]{1,0:T(8,128)(2,1)} %p0.2), channel_id=1, source_target_pairs={{0,16},{16,32},{32,48},{48,0},{1,17},{17,33},{33,49},{49,1},{2,18}... | collective-permute-start | bytes 786440 | tf_op jit(solution)/shard_map/ppermute | solution.py:192
  33.8 12.6 %collective-permute-start.3 = (bf16[512,256]{1,0:T(8,128)(2,1)}, bf16[512,256]{1,0:T(8,128)(2,1)S(1)}, u32[]{:S(2)}, u32[]{:S(2)}) collective-permute-start(bf16[512,256]{1,0:T(8,128)(2,1)} %p0.2), channel_id=1, source_target_pairs={{0,48},{16,0},{32,16},{48,32},{1,49},{17,1},{33,17},{49,33},{2,50}... | collective-permute-start | bytes 786440 | tf_op jit(solution)/shard_map/ppermute | solution.py:192
  46.4 1.0 copy-start.7
  49.8 32.1 %copy-start = (f32[1024,2048]{1,0:T(8,128)}, f32[1024,2048]{1,0:T(8,128)S(1)}, u32[]{:S(2)}) copy-start(f32[1024,2048]{1,0:T(8,128)S(1)} %get-tuple-element.32.exp_ref.exp_t) | copy-start | bytes 25165828
  49.8 4.9 %collective-permute-start.7 = (f32[4,512]{1,0:T(4,128)S(1)}, f32[4,512]{1,0:T(4,128)S(1)}, u32[]{:S(2)}, u32[]{:S(2)}) collective-permute-start(f32[4,512]{1,0:T(4,128)S(1)} %get-tuple-element.35), channel_id=1, source_target_pairs={{0,16},{16,32},{32,48},{48,0},{1,17},{17,33},{33,49},{49,1},{2,18}... | collective-permute-start | bytes 24584 | tf_op jit(solution)/shard_map/ppermute | solution.py:192
  51.3 5.2 %collective-permute-start.8 = (f32[4,512]{1,0:T(4,128)S(1)}, f32[4,512]{1,0:T(4,128)S(1)}, u32[]{:S(2)}, u32[]{:S(2)}) collective-permute-start(f32[4,512]{1,0:T(4,128)S(1)} %get-tuple-element.36), channel_id=1, source_target_pairs={{0,32},{16,48},{32,0},{48,16},{1,33},{17,49},{33,1},{49,17},{2,34}... | collective-permute-start | bytes 24584 | tf_op jit(solution)/shard_map/ppermute | solution.py:192
  53.9 3.7 %collective-permute-start.9 = (f32[4,512]{1,0:T(4,128)S(1)}, f32[4,512]{1,0:T(4,128)S(1)}, u32[]{:S(2)}, u32[]{:S(2)}) collective-permute-start(f32[4,512]{1,0:T(4,128)S(1)} %get-tuple-element.37), channel_id=1, source_target_pairs={{0,48},{16,0},{32,16},{48,32},{1,49},{17,1},{33,17},{49,33},{2,50}... | collective-permute-start | bytes 24584 | tf_op jit(solution)/shard_map/ppermute | solution.py:192
  58.3 1.2 collective-permute-start.10
  74.2 14.7 %copy-start.5 = (bf16[512,256]{1,0:T(8,128)(2,1)S(1)}, bf16[512,256]{1,0:T(8,128)(2,1)}, u32[]{:S(2)}) copy-start(bf16[512,256]{1,0:T(8,128)(2,1)} %raw.3) | copy-start | bytes 786436
  74.9 4.9 %collective-permute-start.11 = (f32[4,512]{1,0:T(4,128)S(1)}, f32[4,512]{1,0:T(4,128)S(1)}, u32[]{:S(2)}, u32[]{:S(2)}) collective-permute-start(f32[4,512]{1,0:T(4,128)S(1)} %get-tuple-element.41), channel_id=1, source_target_pairs={{0,16},{16,32},{32,48},{48,0},{1,17},{17,33},{33,49},{49,1},{2,18}... | collective-permute-start | bytes 24584 | tf_op jit(solution)/shard_map/ppermute | solution.py:192
  75.0 5.2 %collective-permute-start.12 = (f32[4,512]{1,0:T(4,128)S(1)}, f32[4,512]{1,0:T(4,128)S(1)}, u32[]{:S(2)}, u32[]{:S(2)}) collective-permute-start(f32[4,512]{1,0:T(4,128)S(1)} %get-tuple-element.42), channel_id=1, source_target_pairs={{0,32},{16,48},{32,0},{48,16},{1,33},{17,49},{33,1},{49,17},{2,34}... | collective-permute-start | bytes 24584 | tf_op jit(solution)/shard_map/ppermute | solution.py:192
  78.2 3.7 %collective-permute-start.13 = (f32[4,512]{1,0:T(4,128)S(1)}, f32[4,512]{1,0:T(4,128)S(1)}, u32[]{:S(2)}, u32[]{:S(2)}) collective-permute-start(f32[4,512]{1,0:T(4,128)S(1)} %get-tuple-element.43), channel_id=1, source_target_pairs={{0,48},{16,0},{32,16},{48,32},{1,49},{17,1},{33,17},{49,33},{2,50}... | collective-permute-start | bytes 24584 | tf_op jit(solution)/shard_map/ppermute | solution.py:192
  82.6 1.2 collective-permute-start.14
  84.5 14.8 %all-to-all-start.2 = ((f32[32,8,128]{2,1,0:T(8,128)}), f32[32,8,128]{2,1,0:T(8,128)S(1)}, u32[]{:S(2)}, u32[]{:S(2)}) async-start(f32[32,8,128]{2,1,0:T(8,128)} %broadcast_in_dim.10), calls=%async_computation.2 | async-start | bytes 262144 | tf_op jit(solution)/shard_map/all_to_all | solution.py:197
  88.8 18.2 %collective-permute-start.6 = (bf16[512,256]{1,0:T(8,128)(2,1)S(1)}, bf16[512,256]{1,0:T(8,128)(2,1)S(1)}, u32[]{:S(2)}, u32[]{:S(2)}) collective-permute-start(bf16[512,256]{1,0:T(8,128)(2,1)S(1)} %copy-done.5), channel_id=1, source_target_pairs={{0,48},{16,0},{32,16},{48,32},{1,49},{17,1},{33,17},{49,33},{2,50}... | collective-permute-start | bytes 786440 | tf_op jit(solution)/shard_map/ppermute | solution.py:192
  91.0 16.6 %collective-permute-start.5 = (bf16[512,256]{1,0:T(8,128)(2,1)S(1)}, bf16[512,256]{1,0:T(8,128)(2,1)S(1)}, u32[]{:S(2)}, u32[]{:S(2)}) collective-permute-start(bf16[512,256]{1,0:T(8,128)(2,1)S(1)} %copy-done.5), channel_id=1, source_target_pairs={{0,32},{16,48},{32,0},{48,16},{1,33},{17,49},{33,1},{49,17},{2,34}... | collective-permute-start | bytes 786440 | tf_op jit(solution)/shard_map/ppermute | solution.py:192
  91.8 15.8 %collective-permute-start.4 = (bf16[512,256]{1,0:T(8,128)(2,1)S(1)}, bf16[512,256]{1,0:T(8,128)(2,1)S(1)}, u32[]{:S(2)}, u32[]{:S(2)}) collective-permute-start(bf16[512,256]{1,0:T(8,128)(2,1)S(1)} %copy-done.5), channel_id=1, source_target_pairs={{0,16},{16,32},{32,48},{48,0},{1,17},{17,33},{33,49},{49,1},{2,18}... | collective-permute-start | bytes 786440 | tf_op jit(solution)/shard_map/ppermute | solution.py:192
  99.3 3.4 %copy-start.1 = (f32[1024,2048]{1,0:T(8,128)S(1)}, f32[1024,2048]{1,0:T(8,128)}, u32[]{:S(2)}) copy-start(f32[1024,2048]{1,0:T(8,128)} %copy-done) | copy-start | bytes 25165828
  102.7 8.0 %copy-start.2 = (f32[1024,2048]{1,0:T(8,128)S(1)}, f32[1024,2048]{1,0:T(8,128)}, u32[]{:S(2)}) copy-start(f32[1024,2048]{1,0:T(8,128)} %copy-done) | copy-start | bytes 25165828
  103.4 6.6 %collective-permute-start.15 = (f32[4,512]{1,0:T(4,128)S(1)}, f32[4,512]{1,0:T(4,128)S(1)}, u32[]{:S(2)}, u32[]{:S(2)}) collective-permute-start(f32[4,512]{1,0:T(4,128)S(1)} %get-tuple-element.47), channel_id=1, source_target_pairs={{0,16},{16,32},{32,48},{48,0},{1,17},{17,33},{33,49},{49,1},{2,18}... | collective-permute-start | bytes 24584 | tf_op jit(solution)/shard_map/ppermute | solution.py:192
  104.3 5.7 %collective-permute-start.16 = (f32[4,512]{1,0:T(4,128)S(1)}, f32[4,512]{1,0:T(4,128)S(1)}, u32[]{:S(2)}, u32[]{:S(2)}) collective-permute-start(f32[4,512]{1,0:T(4,128)S(1)} %get-tuple-element.48), channel_id=1, source_target_pairs={{0,32},{16,48},{32,0},{48,16},{1,33},{17,49},{33,1},{49,17},{2,34}... | collective-permute-start | bytes 24584 | tf_op jit(solution)/shard_map/ppermute | solution.py:192
  107.0 3.7 %collective-permute-start.17 = (f32[4,512]{1,0:T(4,128)S(1)}, f32[4,512]{1,0:T(4,128)S(1)}, u32[]{:S(2)}, u32[]{:S(2)}) collective-permute-start(f32[4,512]{1,0:T(4,128)S(1)} %get-tuple-element.49), channel_id=1, source_target_pairs={{0,48},{16,0},{32,16},{48,32},{1,49},{17,1},{33,17},{49,33},{2,50}... | collective-permute-start | bytes 24584 | tf_op jit(solution)/shard_map/ppermute | solution.py:192
  111.3 1.3 collective-permute-start.18
  135.2 2.0 %copy-start.3 = (bf16[1024,2048]{1,0:T(8,128)(2,1)}, bf16[1024,2048]{1,0:T(8,128)(2,1)S(1)}, u32[]{:S(2)}) copy-start(bf16[1024,2048]{1,0:T(8,128)(2,1)S(1)} %get-tuple-element.56.grad_ref) | copy-start | bytes 12582916
  137.2 40.2 %copy-start.6 = (bf16[16,256]{1,0:T(8,128)(2,1)S(1)}, bf16[16,256]{1,0:T(8,128)(2,1)}, u32[]{:S(2)}) copy-start(bf16[16,256]{1,0:T(8,128)(2,1)} %raw.2) | copy-start | bytes 24580
  137.2 2.0 %collective-permute-start.19 = (f32[512,256]{1,0:T(8,128)S(1)}, f32[512,256]{1,0:T(8,128)S(1)}, u32[]{:S(2)}, u32[]{:S(2)}) collective-permute-start(f32[512,256]{1,0:T(8,128)S(1)} %slice.7), channel_id=1, source_target_pairs={{0,1},{1,0},{2,3},{3,2},{4,5},{5,4},{6,7},{7,6},{8,9},{9,8},{10,11... | collective-permute-start | bytes 1572872 | tf_op jit(solution)/shard_map/ppermute | solution.py:192
  140.1 37.3 %all-to-all-start.4 = ((f32[32,16,256]{2,1,0:T(8,128)}), f32[32,16,256]{2,1,0:T(8,128)S(1)}, u32[]{:S(2)}, u32[]{:S(2)}) async-start(f32[32,16,256]{2,1,0:T(8,128)} %bitcast.1), calls=%async_computation.4 | async-start | bytes 1048576 | tf_op jit(solution)/shard_map/all_to_all | solution.py:267
  144.7 2.2 %copy-start.4 = (bf16[1024,2048]{1,0:T(8,128)(2,1)S(1)}, bf16[1024,2048]{1,0:T(8,128)(2,1)}, u32[]{:S(2)}) copy-start(bf16[1024,2048]{1,0:T(8,128)(2,1)} %copy-done.3) | copy-start | bytes 12582916
  148.2 24.7 %collective-permute-start.20 = (f32[512,256]{1,0:T(8,128)S(1)}, f32[512,256]{1,0:T(8,128)S(1)}, u32[]{:S(2)}, u32[]{:S(2)}) collective-permute-start(f32[512,256]{1,0:T(8,128)S(1)} %get-tuple-element.59), channel_id=1, source_target_pairs={{0,48},{16,0},{32,16},{48,32},{1,49},{17,1},{33,17},{49,33},{2,50}... | collective-permute-start | bytes 1572872 | tf_op jit(solution)/shard_map/ppermute | solution.py:192
  150.7 22.2 %collective-permute-start.21 = (f32[512,256]{1,0:T(8,128)S(1)}, f32[512,256]{1,0:T(8,128)S(1)}, u32[]{:S(2)}, u32[]{:S(2)}) collective-permute-start(f32[512,256]{1,0:T(8,128)S(1)} %get-tuple-element.60), channel_id=1, source_target_pairs={{0,32},{16,48},{32,0},{48,16},{1,33},{17,49},{33,1},{49,17},{2,34}... | collective-permute-start | bytes 1572872 | tf_op jit(solution)/shard_map/ppermute | solution.py:192
  150.7 25.6 %collective-permute-start.22 = (f32[512,256]{1,0:T(8,128)S(1)}, f32[512,256]{1,0:T(8,128)S(1)}, u32[]{:S(2)}, u32[]{:S(2)}) collective-permute-start(f32[512,256]{1,0:T(8,128)S(1)} %get-tuple-element.61), channel_id=1, source_target_pairs={{0,16},{16,32},{32,48},{48,0},{1,17},{17,33},{33,49},{49,1},{2,18}... | collective-permute-start | bytes 1572872 | tf_op jit(solution)/shard_map/ppermute | solution.py:192

commit v3 on v2

--- a/solution.py
+++ b/solution.py
@@ -30,16 +30,18 @@
     return (values * inverse_norm(values)).astype(bf16)
 
 
-def call(kernel, outs, operands, flops, name):
+def call(kernel, outs, operands, flops, name, scratch=(), after=(), where=VMEM):
+    count = len(after)
     return pl.pallas_call(
-        kernel,
+        lambda *refs: kernel(*refs[count:]),
         out_shape=outs,
-        in_specs=[VMEM] * len(operands),
+        in_specs=[pl.BlockSpec(memory_space=pl.ANY)] * count + [where] * len(operands),
         out_specs=jax.tree.map(lambda unused: VMEM, outs),
-        compiler_params=pltpu.CompilerParams(vmem_limit_bytes=16 * 2**20),
+        scratch_shapes=scratch,
+        compiler_params=pltpu.CompilerParams(vmem_limit_bytes=8 * 2**20),
         cost_estimate=pl.CostEstimate(flops=flops, bytes_accessed=2**20, transcendentals=0),
         name=name,
-    )(*operands)
+    )(*after, *operands)
 
 
 def column(values):
@@ -63,21 +65,38 @@
         out[at : at + 1, :] = values
 
 
-def load_features(first, own, sib, protos, feat_ref, weight_ref):
-    half, block, width = own.shape[0], protos[0].shape[0], protos[0].shape[1]
+def pack_kernel(first, second, out, held, arrived):
+    copies = [
+        pltpu.make_async_copy(ref, held.at[k], arrived.at[k]) for k, ref in enumerate((first, second))
+    ]
+    for copy in copies:
+        copy.start()
+    for copy in copies:
+        copy.wait()
+    packed = jnp.concatenate([held[0], held[1]], axis=1)
+    for peer in range(out.shape[0]):
+        out[peer] = packed
+
+
+def unit_kernel(*refs):
+    out, block = refs[-1], refs[0].shape[0]
+    for k, ref in enumerate(refs[:-1]):
+        out[k * block : (k + 1) * block, :] = unit(ref[...])
+
+
+def load_features(first, own, sib, feat_ref):
+    half, width = own.shape[0], feat_ref.shape[1]
     feat_ref[:half, :] = unit(own[:, first : first + width])
     feat_ref[half:, :] = unit(sib[:, first : first + width])
-    for k, proto in enumerate(protos):
-        weight_ref[k * block : (k + 1) * block, :] = unit(proto[...])
 
 
 def scores(rows, weights):
     return lax.dot_general(rows, weights, (((1,), (1,)), ((), ())), preferred_element_type=f32)
 
 
-def teacher_kernel(own, sib, p0, p1, p2, p3, exp_ref, m0, m1, m2, m3, feat_ref, weight_ref):
-    load_features(0, own, sib, (p0, p1, p2, p3), feat_ref, weight_ref)
-    rows, block = feat_ref.shape[0], p0.shape[0]
+def teacher_kernel(own, sib, weight_ref, exp_ref, m0, m1, m2, m3, feat_ref):
+    load_features(0, own, sib, feat_ref)
+    rows, block = feat_ref.shape[0], weight_ref.shape[0] // STEPS
     for k in range(STEPS):
         cols = slice(k * block, (k + 1) * block)
         total = jnp.zeros((8, block), f32)
@@ -89,10 +108,9 @@
         store_rolled((m0, m1, m2, m3), k, jnp.sum(total, axis=0, keepdims=True))
 
 
-def student_kernel(own, sib, p0, p1, p2, p3, exp_ref, sum_ref, feat_ref, weight_ref):
-    width, block = p0.shape[1], p0.shape[0]
-    load_features(width, own, sib, (p0, p1, p2, p3), feat_ref, weight_ref)
-    rows = feat_ref.shape[0]
+def student_kernel(own, sib, weight_ref, exp_ref, sum_ref, feat_ref):
+    load_features(feat_ref.shape[1], own, sib, feat_ref)
+    rows, block = feat_ref.shape[0], weight_ref.shape[0] // STEPS
     for at in range(0, rows, TILE):
         r = slice(at, at + TILE)
         total = jnp.zeros((TILE, LANES), f32)
@@ -145,31 +163,45 @@
         swap_ref[at + count // 2 : at + count, :] = out_ref[at : at + count // 2, :]
 
 
-def logits_kernel(factor, exp_t, exp_s, scale_ref, mass_ref, weight_ref, grad_ref, feat_ref):
+def grads_kernel(
+    factor, exp_t, exp_s, scale_ref, mass_ref, feat_ref, weight_ref, feat_out, w0, w1, w2a, w2b, w3, grad_ref
+):
     inverse = factor / jnp.sum(mass_ref[...], axis=0)
     rows, cols = exp_t.shape
     count, block = rows // LANES, cols // STEPS
-    for i in range(count):
-        r = slice(i * LANES, (i + 1) * LANES)
-        row = column(inverse[i : i + 1, :])
-        total = column(inverse[count + i : count + i + 1, :])
-        for at in range(0, cols, LANES):
-            k, o = at // block, at % block
-            c = slice(at, at + LANES)
-            target = exp_t[r, c] * scale_ref[k : k + 1, o : o + LANES] * row
-            grad_ref[r, c] = (exp_s[r, c] * total - target).astype(bf16)
-    feat_ref[...] = jnp.dot(grad_ref[...], weight_ref[...], preferred_element_type=f32)
-
-
-def weight_kernel(grad_ref, feat_ref, *outs):
-    block = outs[0].shape[0]
-    for k, out in enumerate(outs):
-        out[...] = lax.dot_general(
-            grad_ref[:, k * block : (k + 1) * block],
-            feat_ref[...],
-            (((0,), (0,)), ((), ())),
-            preferred_element_type=f32,
-        )
+    row = [column(inverse[i : i + 1, :]) for i in range(count)]
+    total = [column(inverse[count + i : count + i + 1, :]) for i in range(count)]
+    for k, outs in enumerate(((w0,), (w1,), (w2a, w2b), (w3,))):
+        for i in range(count):
+            r = slice(i * LANES, (i + 1) * LANES)
+            for o in range(0, block, LANES):
+                c = slice(k * block + o, k * block + o + LANES)
+                target = exp_t[r, c] * scale_ref[k : k + 1, o : o + LANES] * row[i]
+                grad_ref[r, c] = (exp_s[r, c] * total[i] - target).astype(bf16)
+        at = k * block
+        for out in outs:
+            size = out.shape[0]
+            out[...] = lax.dot_general(
+                grad_ref[:, at : at + size],
+                feat_ref[...],
+                (((0,), (0,)), ((), ())),
+                preferred_element_type=f32,
+            )
+            at += size
+    feat_out[...] = jnp.dot(grad_ref[...], weight_ref[...], preferred_element_type=f32)
+
+
+def pair_kernel(mine, other, out):
+    half = other.shape[0]
+    out[...] = (mine[:half, :] + other[...]).reshape(out.shape)
+
+
+def relay_kernel(forward, back, upper, lower, forward_out, back_out):
+    half = upper.shape[0]
+    forward_out[:half, :] = forward[:half, :] + upper[...]
+    forward_out[half:, :] = forward[half:, :]
+    back_out[:half, :] = back[:half, :]
+    back_out[half:, :] = back[half:, :] + lower[...]
 
 
 def project(raw, grads):
@@ -183,8 +215,8 @@
     out[...] = project(raw[...], jnp.sum(parts[...], axis=0))
 
 
-def proto_grad_kernel(raw, w0, w1, w2, w3, out):
-    out[...] = project(raw[...], w0[...] + w1[...] + w2[...] + w3[...])
+def proto_grad_kernel(raw, mine, before, after, out):
+    out[...] = project(raw[...], mine[...] + before[...] + after[...])
 
 
 def shift(values, axis, step):
@@ -225,60 +257,89 @@
     feats = pltpu.VMEM((rows, width), bf16)
     weights = pltpu.VMEM((cols, width), bf16)
 
+    peers = lax.axis_size(ROWS)
+    packed = call(
+        pack_kernel,
+        jax.ShapeDtypeStruct((peers, own_rows, 2 * width), bf16),
+        (teacher_rows, student_rows),
+        0,
+        "pack",
+        [pltpu.VMEM((2, own_rows, width), bf16), pltpu.SemaphoreType.DMA((2,))],
+        where=pl.BlockSpec(memory_space=pltpu.HBM),
+    )
+    own = lax.all_to_all(packed, ROWS, 0, 0, tiled=True).reshape(-1, 2 * width)
     teacher_blocks = gather_protos(teacher_protos)
-    student_blocks = gather_protos(student_protos)
-    own = spread(jnp.concatenate([teacher_rows, student_rows], axis=1)).reshape(-1, 2 * width)
+    teacher_weight = call(unit_kernel, weights, teacher_blocks, 100 * work, "teacher_units")
+    student_protos, teacher_blocks[1] = lax.optimization_barrier((student_protos, teacher_blocks[1]))
+    student_weight = call(unit_kernel, weights, gather_protos(student_protos), 0, "student_units")
+    own, teacher_weight, student_weight = lax.optimization_barrier(
+        (own, teacher_weight, student_weight)
+    )
     sib = shift(own, "core", 1)
 
     exp_t, *mass = call(
-        teacher_kernel, [exps] + masses + [feats, weights], (own, sib, *teacher_blocks), work, "teacher"
-    )
-    mass = mass[:STEPS]
-    exp_s, student_sums, student_feat, student_weight = call(
-        student_kernel, [exps, sums, feats, weights], (own, sib, *student_blocks), work, "student"
+        teacher_kernel, [exps] + masses + [feats], (own, sib, teacher_weight), work, "teacher"
+    )
+    mass = share(mass[:STEPS])
+    exp_s, student_sums, student_feat = call(
+        student_kernel, [exps, sums, feats], (own, sib, student_weight), work, "student"
     )
     for sweep in range(SWEEPS):
         last = sweep + 1 == SWEEPS
         extra = (student_sums,) if last else ()
         out = jax.ShapeDtypeStruct((rows // LANES * (1 + len(extra)), LANES), f32)
         mine, swapped, scale = call(
-            row_kernel, [out, out, masses[0]], (exp_t, *share(mass), *extra), work // 8, "rows"
+            row_kernel,
+            [out, out, masses[0]],
+            (exp_t, *mass, *extra),
+            work // 8,
+            "rows",
         )
         row_masses = share_rows(mine, swapped)
         if not last:
-            mass = call(column_kernel, masses, (exp_t, row_masses), work // 8, "columns")
-
-    grads, feat_grad = call(
-        functools.partial(logits_kernel, factor),
-        [pltpu.VMEM((rows, cols), bf16), jax.ShapeDtypeStruct((rows, width), f32)],
-        (exp_t, exp_s, scale, row_masses, student_weight),
-        work,
-        "logits",
-    )
-    weight_parts = call(
-        weight_kernel,
-        [jax.ShapeDtypeStruct((own_protos, width), f32)] * STEPS,
-        (grads, student_feat),
-        work,
-        "weights",
+            mass = share(call(column_kernel, masses, (exp_t, row_masses), work // 8, "columns"))
+
+    feat_grad, *weight_parts = call(
+        functools.partial(grads_kernel, factor),
+        [
+            jax.ShapeDtypeStruct((size, width), f32)
+            for size in (rows, own_protos, own_protos, own_protos // 2, own_protos // 2, own_protos)
+        ],
+        (exp_t, exp_s, scale, row_masses, student_feat, student_weight),
+        2 * work,
+        "grads",
+        [pltpu.VMEM((rows, cols), bf16)],
     )
     half = rows // 2
-    feat_pair = feat_grad[:half] + shift(feat_grad[half:], "core", 1)
-    feat_share = lax.all_to_all(feat_pair.reshape(-1, own_rows, width), ROWS, 0, 0, tiled=True)
-    weight_share = [weight_parts[0]] + [shift(weight_parts[k], "x", -k) for k in range(1, STEPS)]
+    feat_pair = call(
+        pair_kernel,
+        jax.ShapeDtypeStruct((half // own_rows, own_rows, width), f32),
+        (feat_grad, shift(feat_grad[half:], "core", 1)),
+        100 * work,
+        "pair",
+    )
+    feat_share = lax.all_to_all(feat_pair, ROWS, 0, 0, tiled=True)
+    own_part, back_part, upper_part, lower_part, forward_part = weight_parts
+    forward_part, back_part = call(
+        relay_kernel,
+        [jax.ShapeDtypeStruct((own_protos, width), f32)] * 2,
+        (forward_part, back_part, shift(upper_part, "x", 1), shift(lower_part, "x", -1)),
+        100 * work,
+        "relay",
+    )
+    proto_grad = call(
+        proto_grad_kernel,
+        jax.ShapeDtypeStruct((own_protos, width), f32),
+        (student_protos, own_part, shift(forward_part, "x", 1), shift(back_part, "x", -1)),
+        0,
+        "proto_grad",
+    )
     row_grad = call(
         row_grad_kernel,
         jax.ShapeDtypeStruct((own_rows, width), f32),
         (student_rows, feat_share),
-        rows * width,
+        0,
         "row_grad",
-    )
-    proto_grad = call(
-        proto_grad_kernel,
-        jax.ShapeDtypeStruct((own_protos, width), f32),
-        (student_protos, *weight_share),
-        own_protos * width,
-        "proto_grad",
     )
     return (row_grad, proto_grad)
 

time: 180 us -> 150 us (0.83)
  waiting for transfers between devices: 53.8 us -> 37.2 us
  blocking collectives: 63.6 us -> 48.8 us
  starting transfers between devices: 35.1 us -> 43.5 us
  local copies, waits for them, and re-layouts: 9.29 us -> 2.44 us
  Pallas kernels: 14 us -> 16.5 us
    all_to_all x3, blocking collectives: 63.6 us -> 48.8 us  [spread(): lax.all_to_all(jnp.broadcast_to(values[None], (count,) + values.shape), R...]
    ppermute x23 -> x24, waiting for transfers between devices: 46.5 us -> 34.4 us  [shift(): lax.ppermute(values, axis, [(i, (i + step) % size) for i in range(size)])]
    all_to_all x2, starting transfers between devices: 8.91 us -> 15.9 us  [the longest x1 11.4 us: body(): own = lax.all_to_all(packed, ROWS, 0, 0, tiled=True).reshape(-1, 2 * width)]
    unnamed x16 -> x12, local copies, waits for them, and re-layouts: 8.5 us -> 2.35 us
    all_to_all x2, waiting for transfers between devices: 7.35 us -> 2.74 us  [the longest x1 2.21 us: body(): own = lax.all_to_all(packed, ROWS, 0, 0, tiled=True).reshape(-1, 2 * width)]
    pallas_call x11 -> x15, Pallas kernels: 14 us -> 16.5 us  [call(): pl.pallas_call(lambda *refs: kernel(*refs[count:]), out_shape=outs, in_sp...]
    ppermute x23 -> x24, starting transfers between devices: 26.2 us -> 27.5 us  [shift(): lax.ppermute(values, axis, [(i, (i + step) % size) for i in range(size)])]
  transfers between devices with their start and end apart: 25 -> 26, of which waited for: 17 -> 18; matrix products, arithmetic and copies ran while one was open for 0% -> 0% of each run, Pallas kernels for 3% -> 4%
where the time goes in v3:
time: 150 us; the launch traced here: 149 us
  blocking collectives  48.8 us (33%)
  starting transfers between devices  43.5 us (29%)
  waiting for transfers between devices  37.2 us (25%)
  Pallas kernels  16.5 us (11%)
  local copies, waits for them, and re-layouts  2.44 us (2%)
    all_to_all x3, blocking collectives, spread(): lax.all_to_all(jnp.broadcast_to(values[None], (count,) + values.shape), R...  48.8 us
    ppermute x24, waiting for transfers between devices, shift(): lax.ppermute(values, axis, [(i, (i + step) % size) for i in range(size)])  34.4 us
    ppermute x24, starting transfers between devices, shift(): lax.ppermute(values, axis, [(i, (i + step) % size) for i in range(size)])  27.5 us
    pallas_call x15, Pallas kernels, call(): pl.pallas_call(lambda *refs: kernel(*refs[count:]), out_shape=outs, in_sp...  16.5 us
    all_to_all x1, starting transfers between devices, body(): own = lax.all_to_all(packed, ROWS, 0, 0, tiled=True).reshape(-1, 2 * width)  11.4 us
    all_to_all x1, starting transfers between devices, body(): feat_share = lax.all_to_all(feat_pair, ROWS, 0, 0, tiled=True)  4.56 us
  transfers between devices with their start and end apart: 26, of which 18 were waited for; matrix products, arithmetic and copies ran while one was open for 0% of the time, Pallas kernels for 4%

profile of v3, /device:TPU:32, one launch (start us, length us, event | category | flops | bytes accessed | tf_op | source)
XLA Modules:
  0.0 149.2 jit_solution(9833820940113664428)
XLA Ops:
  0.6 1.6 %collective-permute-start = (bf16[512,256]{1,0:T(8,128)(2,1)}, bf16[512,256]{1,0:T(8,128)(2,1)S(1)}, u32[]{:S(2)}, u32[]{:S(2)}) collective-permute-start(bf16[512,256]{1,0:T(8,128)(2,1)} %refs_0_.4), channel_id=1, source_target_pairs={{0,16},{16,32},{32,48},{48,0},{1,17},{17,33},{33,49},{49,1},{2,18}... | collective-permute-start | bytes 786440 | tf_op jit(solution)/shard_map/ppermute | solution.py:224
  2.2 2.7 %collective-permute-start.1 = (bf16[512,256]{1,0:T(8,128)(2,1)}, bf16[512,256]{1,0:T(8,128)(2,1)S(1)}, u32[]{:S(2)}, u32[]{:S(2)}) collective-permute-start(bf16[512,256]{1,0:T(8,128)(2,1)} %refs_0_.4), channel_id=1, source_target_pairs={{0,32},{16,48},{32,0},{48,16},{1,33},{17,49},{33,1},{49,17},{2,34}... | collective-permute-start | bytes 786440 | tf_op jit(solution)/shard_map/ppermute | solution.py:224
  4.9 1.4 collective-permute-start.2
  6.4 0.7 copy-done.2
  7.1 0.7 copy-done.4
  7.8 0.9 pack.1
  8.6 11.4 %all-to-all-start = ((bf16[32,16,512]{2,1,0:T(8,128)(2,1)}), bf16[32,16,512]{2,1,0:T(8,128)(2,1)S(1)}, u32[]{:S(2)}, u32[]{:S(2)}) async-start(bf16[32,16,512]{2,1,0:T(8,128)(2,1)} %pack.1), calls=%async_computation | async-start | bytes 1048576 | tf_op jit(solution)/shard_map/all_to_all | solution.py:270
  20.0 0.0 copy-start
  20.0 0.1 collective-permute-start.5
  20.1 2.6 %collective-permute-start.4 = (bf16[512,256]{1,0:T(8,128)(2,1)}, bf16[512,256]{1,0:T(8,128)(2,1)S(1)}, u32[]{:S(2)}, u32[]{:S(2)}) collective-permute-start(bf16[512,256]{1,0:T(8,128)(2,1)} %refs_0_.7), channel_id=1, source_target_pairs={{0,32},{16,48},{32,0},{48,16},{1,33},{17,49},{33,1},{49,17},{2,34}... | collective-permute-start | bytes 786440 | tf_op jit(solution)/shard_map/ppermute | solution.py:224
  22.8 0.0 copy-start.5
  22.8 0.9 copy-done.5
  23.7 0.4 teacher_units.1.refs_2_
  24.1 5.4 %collective-permute-done.5.refs_3_ = bf16[512,256]{1,0:T(8,128)(2,1)S(1)} collective-permute-done((bf16[512,256]{1,0:T(8,128)(2,1)}, bf16[512,256]{1,0:T(8,128)(2,1)S(1)}, u32[]{:S(2)}, u32[]{:S(2)}) %collective-permute-start.5) | collective-permute-done | bytes 262176 | tf_op jit(solution)/shard_map/ppermute | solution.py:224
  29.6 1.6 %collective-permute-done.4.refs_2_ = bf16[512,256]{1,0:T(8,128)(2,1)S(1)} collective-permute-done((bf16[512,256]{1,0:T(8,128)(2,1)}, bf16[512,256]{1,0:T(8,128)(2,1)S(1)}, u32[]{:S(2)}, u32[]{:S(2)}) %collective-permute-start.4) | collective-permute-done | bytes 262176 | tf_op jit(solution)/shard_map/ppermute | solution.py:224
  31.2 3.0 %collective-permute-done.3.refs_1_ = bf16[512,256]{1,0:T(8,128)(2,1)S(1)} collective-permute-done((bf16[512,256]{1,0:T(8,128)(2,1)}, bf16[512,256]{1,0:T(8,128)(2,1)S(1)}, u32[]{:S(2)}, u32[]{:S(2)}) %collective-permute-start.3) | collective-permute-done | bytes 262176 | tf_op jit(solution)/shard_map/ppermute | solution.py:224
  34.2 0.4 student_units.1.refs_2_.refs_5_
  34.6 2.2 %all-to-all-done = bf16[32,16,512]{2,1,0:T(8,128)(2,1)S(1)} async-done(((bf16[32,16,512]{2,1,0:T(8,128)(2,1)}), bf16[32,16,512]{2,1,0:T(8,128)(2,1)S(1)}, u32[]{:S(2)}, u32[]{:S(2)}) %all-to-all-start) | async-done | bytes 524320 | tf_op jit(solution)/shard_map/all_to_all | solution.py:270
  36.8 1.9 %collective-permute-done.6.refs_1_ = bf16[512,512]{1,0:T(8,128)(2,1)S(1)} collective-permute-done((bf16[512,512]{1,0:T(8,128)(2,1)S(1)}, bf16[512,512]{1,0:T(8,128)(2,1)S(1)}, u32[]{:S(2)}, u32[]{:S(2)}) %collective-permute-start.6) | collective-permute-done | bytes 524320 | tf_op jit(solution)/shard_map/ppermute | solution.py:224
  38.7 2.2 %teacher.1 = (f32[1024,2048]{1,0:T(8,128)S(1)}, f32[4,512]{1,0:T(4,128)S(1)}, f32[4,512]{1,0:T(4,128)S(1)}, f32[4,512]{1,0:T(4,128)S(1)}, f32[4,512]{1,0:T(4,128)S(1)}, /*index=5*/bf16[1024,256]{1,0:T(8,128)(2,1)}) custom-call(bf16[512,512]{1,0:T(8,128)(2,1)S(1)} %bitcast.2, bf16[512,512]{1,0:T(8,128)(2,1)S(1)} %collective-permute-done.6.refs_1_, ...), custom_call_target="tpu_custom_call" | custom-call | flops 1073741824 | bytes 1048576 | tf_op jit(solution)/shard_map/teacher/pallas_call | solution.py:35
  40.9 0.6 collective-permute-start.7
  41.5 1.1 collective-permute-start.8
  42.6 1.5 %collective-permute-start.9 = (f32[4,512]{1,0:T(4,128)S(1)}, f32[4,512]{1,0:T(4,128)S(1)}, u32[]{:S(2)}, u32[]{:S(2)}) collective-permute-start(f32[4,512]{1,0:T(4,128)S(1)} %get-tuple-element.46), channel_id=1, source_target_pairs={{0,48},{16,0},{32,16},{48,32},{1,49},{17,1},{33,17},{49,33},{2,50}... | collective-permute-start | bytes 24584 | tf_op jit(solution)/shard_map/ppermute | solution.py:224
  44.2 1.6 %collective-permute-done.7.refs_2_ = f32[4,512]{1,0:T(4,128)S(1)} collective-permute-done((f32[4,512]{1,0:T(4,128)S(1)}, f32[4,512]{1,0:T(4,128)S(1)}, u32[]{:S(2)}, u32[]{:S(2)}) %collective-permute-start.7) | collective-permute-done | bytes 8224 | tf_op jit(solution)/shard_map/ppermute | solution.py:224
  45.8 0.9 collective-permute-done.8.refs_3_
  46.7 0.1 collective-permute-done.9.refs_4_
  46.7 0.7 rows.3
  47.5 0.0 collective-permute-start.10
  47.5 1.2 collective-permute-done.10
  48.6 17.9 %all_to_all.25.refs_1_ = f32[32,8,128]{2,1,0:T(8,128)S(1)} all-to-all(f32[32,8,128]{2,1,0:T(8,128)S(1)} %broadcast_in_dim.6), channel_id=1, replica_groups=mesh['y'=4,'x'=4,'z'=8,'core'=2] {'y','z'}, dimensions={0} | all-to-all | bytes 262144 | tf_op jit(solution)/shard_map/all_to_all | solution.py:229
  66.5 0.7 columns.2
  67.3 1.8 %collective-permute-start.11 = (f32[4,512]{1,0:T(4,128)S(1)}, f32[4,512]{1,0:T(4,128)S(1)}, u32[]{:S(2)}, u32[]{:S(2)}) collective-permute-start(f32[4,512]{1,0:T(4,128)S(1)} %get-tuple-element.50), channel_id=1, source_target_pairs={{0,16},{16,32},{32,48},{48,0},{1,17},{17,33},{33,49},{49,1},{2,18}... | collective-permute-start | bytes 24584 | tf_op jit(solution)/shard_map/ppermute | solution.py:224
  69.1 3.0 %collective-permute-start.12 = (f32[4,512]{1,0:T(4,128)S(1)}, f32[4,512]{1,0:T(4,128)S(1)}, u32[]{:S(2)}, u32[]{:S(2)}) collective-permute-start(f32[4,512]{1,0:T(4,128)S(1)} %get-tuple-element.51), channel_id=1, source_target_pairs={{0,32},{16,48},{32,0},{48,16},{1,33},{17,49},{33,1},{49,17},{2,34}... | collective-permute-start | bytes 24584 | tf_op jit(solution)/shard_map/ppermute | solution.py:224
  72.0 0.3 collective-permute-done.11.refs_2_
  72.4 1.9 %collective-permute-done.12.refs_3_ = f32[4,512]{1,0:T(4,128)S(1)} collective-permute-done((f32[4,512]{1,0:T(4,128)S(1)}, f32[4,512]{1,0:T(4,128)S(1)}, u32[]{:S(2)}, u32[]{:S(2)}) %collective-permute-start.12) | collective-permute-done | bytes 8224 | tf_op jit(solution)/shard_map/ppermute | solution.py:224
  74.2 1.5 collective-permute-done.13.refs_4_
  75.7 0.7 rows.4
  76.4 1.2 collective-permute-done.14
  77.6 14.2 %all_to_all.26.refs_1_ = f32[32,8,128]{2,1,0:T(8,128)S(1)} all-to-all(f32[32,8,128]{2,1,0:T(8,128)S(1)} %broadcast_in_dim.7), channel_id=1, replica_groups=mesh['y'=4,'x'=4,'z'=8,'core'=2] {'y','z'}, dimensions={0} | all-to-all | bytes 262144 | tf_op jit(solution)/shard_map/all_to_all | solution.py:229
  91.8 0.7 columns.3
  92.5 0.1 collective-permute-start.15
  92.6 2.7 %collective-permute-start.16 = (f32[4,512]{1,0:T(4,128)S(1)}, f32[4,512]{1,0:T(4,128)S(1)}, u32[]{:S(2)}, u32[]{:S(2)}) collective-permute-start(f32[4,512]{1,0:T(4,128)S(1)} %get-tuple-element.57), channel_id=1, source_target_pairs={{0,32},{16,48},{32,0},{48,16},{1,33},{17,49},{33,1},{49,17},{2,34}... | collective-permute-start | bytes 24584 | tf_op jit(solution)/shard_map/ppermute | solution.py:224
  95.3 1.5 collective-permute-start.17
  96.8 2.1 %student.1 = (f32[1024,2048]{1,0:T(8,128)S(1)}, f32[8,128]{1,0:T(8,128)S(1)}, bf16[1024,256]{1,0:T(8,128)(2,1)S(1)}) custom-call(bf16[512,512]{1,0:T(8,128)(2,1)S(1)} %bitcast.3, bf16[512,512]{1,0:T(8,128)(2,1)S(1)} %collective-permute-done.6.refs_1_, bf16[2048,256]{1,0:T(8,128)(2,1)S(1)} %student_units.1.refs_2_.refs_5_), custom_call_target="tpu_custom_call" | custom-call | flops 1073741824 | bytes 1048576 | tf_op jit(solution)/shard_map/student/pallas_call | solution.py:35
  98.8 0.0 collective-permute-done.15.refs_2_
  98.8 0.1 collective-permute-done.17.refs_4_
  98.9 0.6 rows.5
  99.6 0.1 collective-permute-start.18
  99.7 1.2 collective-permute-done.18
  100.9 16.8 %all_to_all.27.refs_3_ = f32[32,16,128]{2,1,0:T(8,128)S(1)} all-to-all(f32[32,16,128]{2,1,0:T(8,128)S(1)} %broadcast_in_dim.8), channel_id=1, replica_groups=mesh['y'=4,'x'=4,'z'=8,'core'=2] {'y','z'}, dimensions={0} | all-to-all | bytes 524288 | tf_op jit(solution)/shard_map/all_to_all | solution.py:229
  117.6 4.2 %grads.1 = (f32[1024,256]{1,0:T(8,128)S(1)}, f32[512,256]{1,0:T(8,128)S(1)}, f32[512,256]{1,0:T(8,128)S(1)}, f32[256,256]{1,0:T(8,128)S(1)}, f32[256,256]{1,0:T(8,128)S(1)}, /*index=5*/f32[512,256]{1,0:T(8,128)S(1)}) custom-call(f32[1024,2048]{1,0:T(8,128)S(1)} %get-tuple-element.40.refs_0_, f32[1024,2048]{1,0:T(8,128)S(1)} %get-tuple-element.42.refs_1_, ...), custom_call_target="tpu_custom_call" | custom-call | flops 2147483648 | bytes 1048576 | tf_op jit(solution)/shard_map/grads/pallas_call | solution.py:35
  121.9 0.1 collective-permute-start.19
  122.0 1.5 %collective-permute-start.20 = (f32[256,256]{1,0:T(8,128)S(1)}, f32[256,256]{1,0:T(8,128)S(1)}, u32[]{:S(2)}, u32[]{:S(2)}) collective-permute-start(f32[256,256]{1,0:T(8,128)S(1)} %get-tuple-element.68), channel_id=1, source_target_pairs={{0,16},{16,32},{32,48},{48,0},{1,17},{17,33},{33,49},{49,1},{2,18}... | collective-permute-start | bytes 786440 | tf_op jit(solution)/shard_map/ppermute | solution.py:224
  123.5 1.8 %collective-permute-start.21 = (f32[256,256]{1,0:T(8,128)S(1)}, f32[256,256]{1,0:T(8,128)S(1)}, u32[]{:S(2)}, u32[]{:S(2)}) collective-permute-start(f32[256,256]{1,0:T(8,128)S(1)} %get-tuple-element.69), channel_id=1, source_target_pairs={{0,48},{16,0},{32,16},{48,32},{1,49},{17,1},{33,17},{49,33},{2,50}... | collective-permute-start | bytes 786440 | tf_op jit(solution)/shard_map/ppermute | solution.py:224
  125.3 0.8 pair.1
  126.2 4.6 %all-to-all-start.4 = ((f32[32,16,256]{2,1,0:T(8,128)}), f32[32,16,256]{2,1,0:T(8,128)S(1)}, u32[]{:S(2)}, u32[]{:S(2)}) async-start(f32[32,16,256]{2,1,0:T(8,128)} %pair.1), calls=%async_computation.4 | async-start | bytes 1048576 | tf_op jit(solution)/shard_map/all_to_all | solution.py:321
  130.7 1.2 collective-permute-done.20.refs_2_
  131.9 0.1 relay.1
  132.0 0.9 collective-permute-start.22
  133.0 2.4 %collective-permute-start.23 = (f32[512,256]{1,0:T(8,128)S(1)}, f32[512,256]{1,0:T(8,128)S(1)}, u32[]{:S(2)}, u32[]{:S(2)}) collective-permute-start(f32[512,256]{1,0:T(8,128)S(1)} %get-tuple-element.71), channel_id=1, source_target_pairs={{0,48},{16,0},{32,16},{48,32},{1,49},{17,1},{33,17},{49,33},{2,50}... | collective-permute-start | bytes 1572872 | tf_op jit(solution)/shard_map/ppermute | solution.py:224
  135.4 11.4 %collective-permute-done.22.refs_2_ = f32[512,256]{1,0:T(8,128)S(1)} collective-permute-done((f32[512,256]{1,0:T(8,128)S(1)}, f32[512,256]{1,0:T(8,128)S(1)}, u32[]{:S(2)}, u32[]{:S(2)}) %collective-permute-start.22) | collective-permute-done | bytes 524320 | tf_op jit(solution)/shard_map/ppermute | solution.py:224
  146.8 1.0 proto_grad.1
  147.9 0.5 all-to-all-done.4.refs_1_
  148.4 0.8 row_grad.1
  (25 shorter events, 0.1 us)
Async XLA Ops:
  0.6 19.4 %collective-permute-start = (bf16[512,256]{1,0:T(8,128)(2,1)}, bf16[512,256]{1,0:T(8,128)(2,1)S(1)}, u32[]{:S(2)}, u32[]{:S(2)}) collective-permute-start(bf16[512,256]{1,0:T(8,128)(2,1)} %refs_0_.4), channel_id=1, source_target_pairs={{0,16},{16,32},{32,48},{48,0},{1,17},{17,33},{33,49},{49,1},{2,18}... | collective-permute-start | bytes 786440 | tf_op jit(solution)/shard_map/ppermute | solution.py:224
  2.2 20.6 %collective-permute-start.1 = (bf16[512,256]{1,0:T(8,128)(2,1)}, bf16[512,256]{1,0:T(8,128)(2,1)S(1)}, u32[]{:S(2)}, u32[]{:S(2)}) collective-permute-start(bf16[512,256]{1,0:T(8,128)(2,1)} %refs_0_.4), channel_id=1, source_target_pairs={{0,32},{16,48},{32,0},{48,16},{1,33},{17,49},{33,1},{49,17},{2,34}... | collective-permute-start | bytes 786440 | tf_op jit(solution)/shard_map/ppermute | solution.py:224
  4.9 17.9 %collective-permute-start.2 = (bf16[512,256]{1,0:T(8,128)(2,1)}, bf16[512,256]{1,0:T(8,128)(2,1)S(1)}, u32[]{:S(2)}, u32[]{:S(2)}) collective-permute-start(bf16[512,256]{1,0:T(8,128)(2,1)} %refs_0_.4), channel_id=1, source_target_pairs={{0,48},{16,0},{32,16},{48,32},{1,49},{17,1},{33,17},{49,33},{2,50}... | collective-permute-start | bytes 786440 | tf_op jit(solution)/shard_map/ppermute | solution.py:224
  6.4 0.7 copy-start.2
  7.1 0.7 copy-start.4
  8.6 28.2 %all-to-all-start = ((bf16[32,16,512]{2,1,0:T(8,128)(2,1)}), bf16[32,16,512]{2,1,0:T(8,128)(2,1)S(1)}, u32[]{:S(2)}, u32[]{:S(2)}) async-start(bf16[32,16,512]{2,1,0:T(8,128)(2,1)} %pack.1), calls=%async_computation | async-start | bytes 1048576 | tf_op jit(solution)/shard_map/all_to_all | solution.py:270
  20.0 14.2 %copy-start = (bf16[512,256]{1,0:T(8,128)(2,1)S(1)}, bf16[512,256]{1,0:T(8,128)(2,1)}, u32[]{:S(2)}) copy-start(bf16[512,256]{1,0:T(8,128)(2,1)} %refs_0_.7) | copy-start | bytes 786436
  20.0 9.5 %collective-permute-start.5 = (bf16[512,256]{1,0:T(8,128)(2,1)}, bf16[512,256]{1,0:T(8,128)(2,1)S(1)}, u32[]{:S(2)}, u32[]{:S(2)}) collective-permute-start(bf16[512,256]{1,0:T(8,128)(2,1)} %refs_0_.7), channel_id=1, source_target_pairs={{0,48},{16,0},{32,16},{48,32},{1,49},{17,1},{33,17},{49,33},{2,50}... | collective-permute-start | bytes 786440 | tf_op jit(solution)/shard_map/ppermute | solution.py:224
  20.1 11.0 %collective-permute-start.4 = (bf16[512,256]{1,0:T(8,128)(2,1)}, bf16[512,256]{1,0:T(8,128)(2,1)S(1)}, u32[]{:S(2)}, u32[]{:S(2)}) collective-permute-start(bf16[512,256]{1,0:T(8,128)(2,1)} %refs_0_.7), channel_id=1, source_target_pairs={{0,32},{16,48},{32,0},{48,16},{1,33},{17,49},{33,1},{49,17},{2,34}... | collective-permute-start | bytes 786440 | tf_op jit(solution)/shard_map/ppermute | solution.py:224
  22.8 11.4 %collective-permute-start.3 = (bf16[512,256]{1,0:T(8,128)(2,1)}, bf16[512,256]{1,0:T(8,128)(2,1)S(1)}, u32[]{:S(2)}, u32[]{:S(2)}) collective-permute-start(bf16[512,256]{1,0:T(8,128)(2,1)} %refs_0_.7), channel_id=1, source_target_pairs={{0,16},{16,32},{32,48},{48,0},{1,17},{17,33},{33,49},{49,1},{2,18}... | collective-permute-start | bytes 786440 | tf_op jit(solution)/shard_map/ppermute | solution.py:224
  22.8 1.0 copy-start.5
  36.8 1.9 %collective-permute-start.6 = (bf16[512,512]{1,0:T(8,128)(2,1)S(1)}, bf16[512,512]{1,0:T(8,128)(2,1)S(1)}, u32[]{:S(2)}, u32[]{:S(2)}) collective-permute-start(bf16[512,512]{1,0:T(8,128)(2,1)S(1)} %bitcast.1), channel_id=1, source_target_pairs={{0,1},{1,0},{2,3},{3,2},{4,5},{5,4},{6,7},{7,6},{8,9},{9,8},{10,11... | collective-permute-start | bytes 1572872 | tf_op jit(solution)/shard_map/ppermute | solution.py:224
  40.9 4.9 %collective-permute-start.7 = (f32[4,512]{1,0:T(4,128)S(1)}, f32[4,512]{1,0:T(4,128)S(1)}, u32[]{:S(2)}, u32[]{:S(2)}) collective-permute-start(f32[4,512]{1,0:T(4,128)S(1)} %get-tuple-element.44), channel_id=1, source_target_pairs={{0,16},{16,32},{32,48},{48,0},{1,17},{17,33},{33,49},{49,1},{2,18}... | collective-permute-start | bytes 24584 | tf_op jit(solution)/shard_map/ppermute | solution.py:224
  41.5 5.2 %collective-permute-start.8 = (f32[4,512]{1,0:T(4,128)S(1)}, f32[4,512]{1,0:T(4,128)S(1)}, u32[]{:S(2)}, u32[]{:S(2)}) collective-permute-start(f32[4,512]{1,0:T(4,128)S(1)} %get-tuple-element.45), channel_id=1, source_target_pairs={{0,32},{16,48},{32,0},{48,16},{1,33},{17,49},{33,1},{49,17},{2,34}... | collective-permute-start | bytes 24584 | tf_op jit(solution)/shard_map/ppermute | solution.py:224
  42.6 4.1 %collective-permute-start.9 = (f32[4,512]{1,0:T(4,128)S(1)}, f32[4,512]{1,0:T(4,128)S(1)}, u32[]{:S(2)}, u32[]{:S(2)}) collective-permute-start(f32[4,512]{1,0:T(4,128)S(1)} %get-tuple-element.46), channel_id=1, source_target_pairs={{0,48},{16,0},{32,16},{48,32},{1,49},{17,1},{33,17},{49,33},{2,50}... | collective-permute-start | bytes 24584 | tf_op jit(solution)/shard_map/ppermute | solution.py:224
  47.5 1.2 collective-permute-start.10
  67.3 5.1 %collective-permute-start.11 = (f32[4,512]{1,0:T(4,128)S(1)}, f32[4,512]{1,0:T(4,128)S(1)}, u32[]{:S(2)}, u32[]{:S(2)}) collective-permute-start(f32[4,512]{1,0:T(4,128)S(1)} %get-tuple-element.50), channel_id=1, source_target_pairs={{0,16},{16,32},{32,48},{48,0},{1,17},{17,33},{33,49},{49,1},{2,18}... | collective-permute-start | bytes 24584 | tf_op jit(solution)/shard_map/ppermute | solution.py:224
  69.1 5.2 %collective-permute-start.12 = (f32[4,512]{1,0:T(4,128)S(1)}, f32[4,512]{1,0:T(4,128)S(1)}, u32[]{:S(2)}, u32[]{:S(2)}) collective-permute-start(f32[4,512]{1,0:T(4,128)S(1)} %get-tuple-element.51), channel_id=1, source_target_pairs={{0,32},{16,48},{32,0},{48,16},{1,33},{17,49},{33,1},{49,17},{2,34}... | collective-permute-start | bytes 24584 | tf_op jit(solution)/shard_map/ppermute | solution.py:224
  72.0 3.7 %collective-permute-start.13 = (f32[4,512]{1,0:T(4,128)S(1)}, f32[4,512]{1,0:T(4,128)S(1)}, u32[]{:S(2)}, u32[]{:S(2)}) collective-permute-start(f32[4,512]{1,0:T(4,128)S(1)} %get-tuple-element.52), channel_id=1, source_target_pairs={{0,48},{16,0},{32,16},{48,32},{1,49},{17,1},{33,17},{49,33},{2,50}... | collective-permute-start | bytes 24584 | tf_op jit(solution)/shard_map/ppermute | solution.py:224
  76.4 1.2 collective-permute-start.14
  92.5 6.3 %collective-permute-start.15 = (f32[4,512]{1,0:T(4,128)S(1)}, f32[4,512]{1,0:T(4,128)S(1)}, u32[]{:S(2)}, u32[]{:S(2)}) collective-permute-start(f32[4,512]{1,0:T(4,128)S(1)} %get-tuple-element.56), channel_id=1, source_target_pairs={{0,16},{16,32},{32,48},{48,0},{1,17},{17,33},{33,49},{49,1},{2,18}... | collective-permute-start | bytes 24584 | tf_op jit(solution)/shard_map/ppermute | solution.py:224
  92.6 6.2 %collective-permute-start.16 = (f32[4,512]{1,0:T(4,128)S(1)}, f32[4,512]{1,0:T(4,128)S(1)}, u32[]{:S(2)}, u32[]{:S(2)}) collective-permute-start(f32[4,512]{1,0:T(4,128)S(1)} %get-tuple-element.57), channel_id=1, source_target_pairs={{0,32},{16,48},{32,0},{48,16},{1,33},{17,49},{33,1},{49,17},{2,34}... | collective-permute-start | bytes 24584 | tf_op jit(solution)/shard_map/ppermute | solution.py:224
  95.3 3.7 %collective-permute-start.17 = (f32[4,512]{1,0:T(4,128)S(1)}, f32[4,512]{1,0:T(4,128)S(1)}, u32[]{:S(2)}, u32[]{:S(2)}) collective-permute-start(f32[4,512]{1,0:T(4,128)S(1)} %get-tuple-element.58), channel_id=1, source_target_pairs={{0,48},{16,0},{32,16},{48,32},{1,49},{17,1},{33,17},{49,33},{2,50}... | collective-permute-start | bytes 24584 | tf_op jit(solution)/shard_map/ppermute | solution.py:224
  99.6 1.3 collective-permute-start.18
  121.9 3.4 %collective-permute-start.19 = (f32[512,256]{1,0:T(8,128)S(1)}, f32[512,256]{1,0:T(8,128)S(1)}, u32[]{:S(2)}, u32[]{:S(2)}) collective-permute-start(f32[512,256]{1,0:T(8,128)S(1)} %slice.3), channel_id=1, source_target_pairs={{0,1},{1,0},{2,3},{3,2},{4,5},{5,4},{6,7},{7,6},{8,9},{9,8},{10,11... | collective-permute-start | bytes 1572872 | tf_op jit(solution)/shard_map/ppermute | solution.py:224
  122.0 9.9 %collective-permute-start.20 = (f32[256,256]{1,0:T(8,128)S(1)}, f32[256,256]{1,0:T(8,128)S(1)}, u32[]{:S(2)}, u32[]{:S(2)}) collective-permute-start(f32[256,256]{1,0:T(8,128)S(1)} %get-tuple-element.68), channel_id=1, source_target_pairs={{0,16},{16,32},{32,48},{48,0},{1,17},{17,33},{33,49},{49,1},{2,18}... | collective-permute-start | bytes 786440 | tf_op jit(solution)/shard_map/ppermute | solution.py:224
  123.5 8.4 %collective-permute-start.21 = (f32[256,256]{1,0:T(8,128)S(1)}, f32[256,256]{1,0:T(8,128)S(1)}, u32[]{:S(2)}, u32[]{:S(2)}) collective-permute-start(f32[256,256]{1,0:T(8,128)S(1)} %get-tuple-element.69), channel_id=1, source_target_pairs={{0,48},{16,0},{32,16},{48,32},{1,49},{17,1},{33,17},{49,33},{2,50}... | collective-permute-start | bytes 786440 | tf_op jit(solution)/shard_map/ppermute | solution.py:224
  126.2 22.2 %all-to-all-start.4 = ((f32[32,16,256]{2,1,0:T(8,128)}), f32[32,16,256]{2,1,0:T(8,128)S(1)}, u32[]{:S(2)}, u32[]{:S(2)}) async-start(f32[32,16,256]{2,1,0:T(8,128)} %pair.1), calls=%async_computation.4 | async-start | bytes 1048576 | tf_op jit(solution)/shard_map/all_to_all | solution.py:321
  131.9 14.9 %copy-start.1 = (bf16[512,256]{1,0:T(8,128)(2,1)S(1)}, bf16[512,256]{1,0:T(8,128)(2,1)}, u32[]{:S(2)}) copy-start(bf16[512,256]{1,0:T(8,128)(2,1)} %refs_0_.7) | copy-start | bytes 786436
  131.9 16.5 %copy-start.3 = (bf16[16,256]{1,0:T(8,128)(2,1)S(1)}, bf16[16,256]{1,0:T(8,128)(2,1)}, u32[]{:S(2)}) copy-start(bf16[16,256]{1,0:T(8,128)(2,1)} %refs_0_.6) | copy-start | bytes 24580
  132.0 14.8 %collective-permute-start.22 = (f32[512,256]{1,0:T(8,128)S(1)}, f32[512,256]{1,0:T(8,128)S(1)}, u32[]{:S(2)}, u32[]{:S(2)}) collective-permute-start(f32[512,256]{1,0:T(8,128)S(1)} %get-tuple-element.70), channel_id=1, source_target_pairs={{0,16},{16,32},{32,48},{48,0},{1,17},{17,33},{33,49},{49,1},{2,18}... | collective-permute-start | bytes 1572872 | tf_op jit(solution)/shard_map/ppermute | solution.py:224
  133.0 13.8 %collective-permute-start.23 = (f32[512,256]{1,0:T(8,128)S(1)}, f32[512,256]{1,0:T(8,128)S(1)}, u32[]{:S(2)}, u32[]{:S(2)}) collective-permute-start(f32[512,256]{1,0:T(8,128)S(1)} %get-tuple-element.71), channel_id=1, source_target_pairs={{0,48},{16,0},{32,16},{48,32},{1,49},{17,1},{33,17},{49,33},{2,50}... | collective-permute-start | bytes 1572872 | tf_op jit(solution)/shard_map/ppermute | solution.py:224

commit v4 on v3

--- a/solution.py
+++ b/solution.py
@@ -78,10 +78,17 @@
         out[peer] = packed
 
 
+def halves_kernel(before, after, upper, lower):
+    half = upper.shape[0]
+    upper[...] = before[:half, :]
+    lower[...] = after[half:, :]
+
+
 def unit_kernel(*refs):
-    out, block = refs[-1], refs[0].shape[0]
-    for k, ref in enumerate(refs[:-1]):
-        out[k * block : (k + 1) * block, :] = unit(ref[...])
+    out, at = refs[-1], 0
+    for ref in refs[:-1]:
+        out[at : at + ref.shape[0], :] = unit(ref[...])
+        at += ref.shape[0]
 
 
 def load_features(first, own, sib, feat_ref):
@@ -231,8 +238,13 @@
     )
 
 
-def gather_protos(raw):
-    return [raw] + [shift(raw, "x", k) for k in range(1, STEPS)]
+def gather_protos(raw, name, flops):
+    before, after = shift(raw, "x", 1), shift(raw, "x", -1)
+    half = raw.shape[0] // 2
+    upper, lower = call(
+        halves_kernel, [jax.ShapeDtypeStruct((half, raw.shape[1]), bf16)] * 2, (before, after), flops, name
+    )
+    return [raw, before, shift(upper, "x", 1), shift(lower, "x", -1), after]
 
 
 def share(blocks):
@@ -261,26 +273,28 @@
     packed = call(
         pack_kernel,
         jax.ShapeDtypeStruct((peers, own_rows, 2 * width), bf16),
-        (teacher_rows, student_rows),
+        [pltpu.with_memory_space_constraint(r, pltpu.HBM) for r in (teacher_rows, student_rows)],
         0,
         "pack",
         [pltpu.VMEM((2, own_rows, width), bf16), pltpu.SemaphoreType.DMA((2,))],
         where=pl.BlockSpec(memory_space=pltpu.HBM),
     )
     own = lax.all_to_all(packed, ROWS, 0, 0, tiled=True).reshape(-1, 2 * width)
-    teacher_blocks = gather_protos(teacher_protos)
-    teacher_weight = call(unit_kernel, weights, teacher_blocks, 100 * work, "teacher_units")
-    student_protos, teacher_blocks[1] = lax.optimization_barrier((student_protos, teacher_blocks[1]))
-    student_weight = call(unit_kernel, weights, gather_protos(student_protos), 0, "student_units")
-    own, teacher_weight, student_weight = lax.optimization_barrier(
-        (own, teacher_weight, student_weight)
-    )
+    teacher_blocks = gather_protos(teacher_protos, "teacher_halves", 100 * work)
+    teacher_weight = call(unit_kernel, weights, teacher_blocks, 0, "teacher_units")
+    student_raw, teacher_blocks[1] = lax.optimization_barrier((student_protos, teacher_blocks[1]))
+    student_blocks = gather_protos(student_raw, "student_halves", 0)
+    own, teacher_weight, student_blocks[1], student_blocks[4] = lax.optimization_barrier(
+        (own, teacher_weight, student_blocks[1], student_blocks[4])
+    )
+    student_weight = call(unit_kernel, weights, student_blocks, 0, "student_units")
     sib = shift(own, "core", 1)
 
     exp_t, *mass = call(
         teacher_kernel, [exps] + masses + [feats], (own, sib, teacher_weight), work, "teacher"
     )
     mass = share(mass[:STEPS])
+    mass[3], student_weight = lax.optimization_barrier((mass[3], student_weight))
     exp_s, student_sums, student_feat = call(
         student_kernel, [exps, sums, feats], (own, sib, student_weight), work, "student"
     )

time: 150 us -> 147 us (0.980)
  local copies, waits for them, and re-layouts: 2.44 us -> 0.1 us
  blocking collectives: 48.8 us -> 46.6 us
  starting transfers between devices: 43.5 us -> 45.2 us
    ppermute x24 -> x26, waiting for transfers between devices: 34.4 us -> 31.3 us  [shift(): lax.ppermute(values, axis, [(i, (i + step) % size) for i in range(size)])]
    unnamed x12 -> x6, local copies, waits for them, and re-layouts: 2.35 us -> 0.02 us
    all_to_all x3, blocking collectives: 48.8 us -> 46.6 us  [spread(): lax.all_to_all(jnp.broadcast_to(values[None], (count,) + values.shape), R...]
    all_to_all x1, waiting for transfers between devices: 2.21 us -> 4.11 us  [body(): own = lax.all_to_all(packed, ROWS, 0, 0, tiled=True).reshape(-1, 2 * width)]
    ppermute x24 -> x26, starting transfers between devices: 27.5 us -> 29.3 us  [shift(): lax.ppermute(values, axis, [(i, (i + step) % size) for i in range(size)])]
    pallas_call x15 -> x17, Pallas kernels: 16.5 us -> 17.2 us  [call(): pl.pallas_call(lambda *refs: kernel(*refs[count:]), out_shape=outs, in_sp...]
  transfers between devices with their start and end apart: 26 -> 28, of which waited for: 18 -> 16; matrix products, arithmetic and copies ran while one was open for 0% -> 0% of each run, Pallas kernels for 4% -> 6%
where the time goes in v4:
time: 147 us; the launch traced here: 146 us
  blocking collectives  46.6 us (32%)
  starting transfers between devices  45.2 us (31%)
  waiting for transfers between devices  36 us (24%)
  Pallas kernels  17.2 us (12%)
    all_to_all x3, blocking collectives, spread(): lax.all_to_all(jnp.broadcast_to(values[None], (count,) + values.shape), R...  46.6 us
    ppermute x26, waiting for transfers between devices, shift(): lax.ppermute(values, axis, [(i, (i + step) % size) for i in range(size)])  31.3 us
    ppermute x26, starting transfers between devices, shift(): lax.ppermute(values, axis, [(i, (i + step) % size) for i in range(size)])  29.3 us
    pallas_call x17, Pallas kernels, call(): pl.pallas_call(lambda *refs: kernel(*refs[count:]), out_shape=outs, in_sp...  17.2 us
    all_to_all x1, starting transfers between devices, body(): own = lax.all_to_all(packed, ROWS, 0, 0, tiled=True).reshape(-1, 2 * width)  11.4 us
    all_to_all x1, starting transfers between devices, body(): feat_share = lax.all_to_all(feat_pair, ROWS, 0, 0, tiled=True)  4.57 us
    all_to_all x1, waiting for transfers between devices, body(): own = lax.all_to_all(packed, ROWS, 0, 0, tiled=True).reshape(-1, 2 * width)  4.11 us
  transfers between devices with their start and end apart: 28, of which 16 were waited for; matrix products, arithmetic and copies ran while one was open for 0% of the time, Pallas kernels for 6%

profile of v4, /device:TPU:32, one launch (start us, length us, event | category | flops | bytes accessed | tf_op | source)
XLA Modules:
  0.0 145.9 jit_solution(16574452841929877303)
XLA Ops:
  0.6 1.6 %collective-permute-start = (bf16[512,256]{1,0:T(8,128)(2,1)}, bf16[512,256]{1,0:T(8,128)(2,1)S(1)}, u32[]{:S(2)}, u32[]{:S(2)}) collective-permute-start(bf16[512,256]{1,0:T(8,128)(2,1)} %refs_0_.5), channel_id=1, source_target_pairs={{0,16},{16,32},{32,48},{48,0},{1,17},{17,33},{33,49},{49,1},{2,18}... | collective-permute-start | bytes 786440 | tf_op jit(solution)/shard_map/ppermute | solution.py:231
  2.2 1.7 %collective-permute-start.1 = (bf16[512,256]{1,0:T(8,128)(2,1)}, bf16[512,256]{1,0:T(8,128)(2,1)S(1)}, u32[]{:S(2)}, u32[]{:S(2)}) collective-permute-start(bf16[512,256]{1,0:T(8,128)(2,1)} %refs_0_.5), channel_id=1, source_target_pairs={{0,48},{16,0},{32,16},{48,32},{1,49},{17,1},{33,17},{49,33},{2,50}... | collective-permute-start | bytes 786440 | tf_op jit(solution)/shard_map/ppermute | solution.py:231
  3.9 1.6 %pack.1 = bf16[32,16,512]{2,1,0:T(8,128)(2,1)} custom-call(bf16[16,256]{1,0:T(8,128)(2,1)} %refs_0_.4, bf16[16,256]{1,0:T(8,128)(2,1)} %refs_0_.7), custom_call_target="tpu_custom_call" | custom-call | bytes 1048576 | tf_op jit(solution)/shard_map/pack/pallas_call | solution.py:35
  5.5 11.4 %all-to-all-start = ((bf16[32,16,512]{2,1,0:T(8,128)(2,1)}), bf16[32,16,512]{2,1,0:T(8,128)(2,1)S(1)}, u32[]{:S(2)}, u32[]{:S(2)}) async-start(bf16[32,16,512]{2,1,0:T(8,128)(2,1)} %pack.1), calls=%async_computation | async-start | bytes 1048576 | tf_op jit(solution)/shard_map/all_to_all | solution.py:282
  16.9 0.0 copy-start.1
  16.9 0.0 copy-start
  16.9 0.0 collective-permute-done.refs_0_.refs_1_
  16.9 1.6 %collective-permute-start.5 = (bf16[512,256]{1,0:T(8,128)(2,1)}, bf16[512,256]{1,0:T(8,128)(2,1)S(1)}, u32[]{:S(2)}, u32[]{:S(2)}) collective-permute-start(bf16[512,256]{1,0:T(8,128)(2,1)} %refs_0_.8), channel_id=1, source_target_pairs={{0,48},{16,0},{32,16},{48,32},{1,49},{17,1},{33,17},{49,33},{2,50}... | collective-permute-start | bytes 786440 | tf_op jit(solution)/shard_map/ppermute | solution.py:231
  18.6 0.5 collective-permute-start.4
  19.1 0.3 collective-permute-start.2
  19.4 3.0 %collective-permute-start.3 = (bf16[256,256]{1,0:T(8,128)(2,1)S(1)}, bf16[256,256]{1,0:T(8,128)(2,1)S(1)}, u32[]{:S(2)}, u32[]{:S(2)}) collective-permute-start(bf16[256,256]{1,0:T(8,128)(2,1)S(1)} %get-tuple-element.45), channel_id=1, source_target_pairs={{0,48},{16,0},{32,16},{48,32},{1,49},{17,1},{33,17},{49,33},{2,50}... | collective-permute-start | bytes 393224 | tf_op jit(solution)/shard_map/ppermute | solution.py:231
  22.4 7.0 %collective-permute-done.2.refs_2_ = bf16[256,256]{1,0:T(8,128)(2,1)S(1)} collective-permute-done((bf16[256,256]{1,0:T(8,128)(2,1)S(1)}, bf16[256,256]{1,0:T(8,128)(2,1)S(1)}, u32[]{:S(2)}, u32[]{:S(2)}) %collective-permute-start.2) | collective-permute-done | bytes 131104 | tf_op jit(solution)/shard_map/ppermute | solution.py:231
  29.4 0.0 collective-permute-done.3.refs_3_
  29.5 0.4 teacher_units.1.refs_2_
  29.8 0.0 collective-permute-done.5.refs_1_.refs_4_
  29.9 4.1 %all-to-all-done = bf16[32,16,512]{2,1,0:T(8,128)(2,1)S(1)} async-done(((bf16[32,16,512]{2,1,0:T(8,128)(2,1)}), bf16[32,16,512]{2,1,0:T(8,128)(2,1)S(1)}, u32[]{:S(2)}, u32[]{:S(2)}) %all-to-all-start) | async-done | bytes 524320 | tf_op jit(solution)/shard_map/all_to_all | solution.py:282
  34.0 0.4 collective-permute-start.8
  34.4 3.0 %collective-permute-start.9 = (bf16[256,256]{1,0:T(8,128)(2,1)S(1)}, bf16[256,256]{1,0:T(8,128)(2,1)S(1)}, u32[]{:S(2)}, u32[]{:S(2)}) collective-permute-start(bf16[256,256]{1,0:T(8,128)(2,1)S(1)} %get-tuple-element.53), channel_id=1, source_target_pairs={{0,48},{16,0},{32,16},{48,32},{1,49},{17,1},{33,17},{49,33},{2,50}... | collective-permute-start | bytes 393224 | tf_op jit(solution)/shard_map/ppermute | solution.py:231
  37.3 2.2 %teacher.1 = (f32[1024,2048]{1,0:T(8,128)S(1)}, f32[4,512]{1,0:T(4,128)S(1)}, f32[4,512]{1,0:T(4,128)S(1)}, f32[4,512]{1,0:T(4,128)S(1)}, f32[4,512]{1,0:T(4,128)S(1)}, /*index=5*/bf16[1024,256]{1,0:T(8,128)(2,1)}) custom-call(bf16[512,512]{1,0:T(8,128)(2,1)S(1)} %bitcast.2, bf16[512,512]{1,0:T(8,128)(2,1)S(1)} %collective-permute-done.6.refs_1_, ...), custom_call_target="tpu_custom_call" | custom-call | flops 1073741824 | bytes 1048576 | tf_op jit(solution)/shard_map/teacher/pallas_call | solution.py:35
  39.5 0.3 collective-permute-start.7
  39.8 1.7 %collective-permute-start.10 = (f32[4,512]{1,0:T(4,128)S(1)}, f32[4,512]{1,0:T(4,128)S(1)}, u32[]{:S(2)}, u32[]{:S(2)}) collective-permute-start(f32[4,512]{1,0:T(4,128)S(1)} %get-tuple-element.58), channel_id=1, source_target_pairs={{0,16},{16,32},{32,48},{48,0},{1,17},{17,33},{33,49},{49,1},{2,18}... | collective-permute-start | bytes 24584 | tf_op jit(solution)/shard_map/ppermute | solution.py:231
  41.5 0.6 collective-permute-start.11
  42.1 0.4 student_units.1.refs_2_.refs_5_
  42.5 0.6 collective-permute-done.7.refs_4_
  43.2 1.5 %collective-permute-done.10.refs_2_ = f32[4,512]{1,0:T(4,128)S(1)} collective-permute-done((f32[4,512]{1,0:T(4,128)S(1)}, f32[4,512]{1,0:T(4,128)S(1)}, u32[]{:S(2)}, u32[]{:S(2)}) %collective-permute-start.10) | collective-permute-done | bytes 8224 | tf_op jit(solution)/shard_map/ppermute | solution.py:231
  44.7 2.0 %collective-permute-done.11.refs_3_ = f32[4,512]{1,0:T(4,128)S(1)} collective-permute-done((f32[4,512]{1,0:T(4,128)S(1)}, f32[4,512]{1,0:T(4,128)S(1)}, u32[]{:S(2)}, u32[]{:S(2)}) %collective-permute-start.11) | collective-permute-done | bytes 8224 | tf_op jit(solution)/shard_map/ppermute | solution.py:231
  46.7 0.7 rows.3
  47.4 1.2 collective-permute-done.12
  48.6 15.6 %all_to_all.25.refs_1_ = f32[32,8,128]{2,1,0:T(8,128)S(1)} all-to-all(f32[32,8,128]{2,1,0:T(8,128)S(1)} %broadcast_in_dim.6), channel_id=1, replica_groups=mesh['y'=4,'x'=4,'z'=8,'core'=2] {'y','z'}, dimensions={0} | all-to-all | bytes 262144 | tf_op jit(solution)/shard_map/all_to_all | solution.py:236
  64.2 0.7 columns.2
  65.0 0.1 collective-permute-start.13
  65.1 2.7 %collective-permute-start.14 = (f32[4,512]{1,0:T(4,128)S(1)}, f32[4,512]{1,0:T(4,128)S(1)}, u32[]{:S(2)}, u32[]{:S(2)}) collective-permute-start(f32[4,512]{1,0:T(4,128)S(1)} %get-tuple-element.65), channel_id=1, source_target_pairs={{0,32},{16,48},{32,0},{48,16},{1,33},{17,49},{33,1},{49,17},{2,34}... | collective-permute-start | bytes 24584 | tf_op jit(solution)/shard_map/ppermute | solution.py:231
  67.7 0.6 collective-permute-start.15
  68.3 1.6 %collective-permute-done.13.refs_2_ = f32[4,512]{1,0:T(4,128)S(1)} collective-permute-done((f32[4,512]{1,0:T(4,128)S(1)}, f32[4,512]{1,0:T(4,128)S(1)}, u32[]{:S(2)}, u32[]{:S(2)}) %collective-permute-start.13) | collective-permute-done | bytes 8224 | tf_op jit(solution)/shard_map/ppermute | solution.py:231
  69.9 0.4 collective-permute-done.14.refs_3_
  70.3 1.1 collective-permute-done.15.refs_4_
  71.4 0.7 rows.4
  72.1 1.2 collective-permute-done.16
  73.3 14.2 %all_to_all.26.refs_1_ = f32[32,8,128]{2,1,0:T(8,128)S(1)} all-to-all(f32[32,8,128]{2,1,0:T(8,128)S(1)} %broadcast_in_dim.7), channel_id=1, replica_groups=mesh['y'=4,'x'=4,'z'=8,'core'=2] {'y','z'}, dimensions={0} | all-to-all | bytes 262144 | tf_op jit(solution)/shard_map/all_to_all | solution.py:236
  87.5 0.7 columns.3
  88.2 1.5 %collective-permute-start.17 = (f32[4,512]{1,0:T(4,128)S(1)}, f32[4,512]{1,0:T(4,128)S(1)}, u32[]{:S(2)}, u32[]{:S(2)}) collective-permute-start(f32[4,512]{1,0:T(4,128)S(1)} %get-tuple-element.70), channel_id=1, source_target_pairs={{0,16},{16,32},{32,48},{48,0},{1,17},{17,33},{33,49},{49,1},{2,18}... | collective-permute-start | bytes 24584 | tf_op jit(solution)/shard_map/ppermute | solution.py:231
  89.7 2.1 %collective-permute-start.18 = (f32[4,512]{1,0:T(4,128)S(1)}, f32[4,512]{1,0:T(4,128)S(1)}, u32[]{:S(2)}, u32[]{:S(2)}) collective-permute-start(f32[4,512]{1,0:T(4,128)S(1)} %get-tuple-element.71), channel_id=1, source_target_pairs={{0,32},{16,48},{32,0},{48,16},{1,33},{17,49},{33,1},{49,17},{2,34}... | collective-permute-start | bytes 24584 | tf_op jit(solution)/shard_map/ppermute | solution.py:231
  91.8 0.7 collective-permute-start.19
  92.5 2.1 %student.1 = (f32[1024,2048]{1,0:T(8,128)S(1)}, f32[8,128]{1,0:T(8,128)S(1)}, bf16[1024,256]{1,0:T(8,128)(2,1)S(1)}) custom-call(bf16[512,512]{1,0:T(8,128)(2,1)S(1)} %bitcast.3, bf16[512,512]{1,0:T(8,128)(2,1)S(1)} %collective-permute-done.6.refs_1_, bf16[2048,256]{1,0:T(8,128)(2,1)S(1)} %student_units.1.refs_2_.refs_5_), custom_call_target="tpu_custom_call" | custom-call | flops 1073741824 | bytes 1048576 | tf_op jit(solution)/shard_map/student/pallas_call | solution.py:35
  94.6 0.3 collective-permute-done.18.refs_3_
  94.9 0.6 collective-permute-done.19.refs_4_
  95.5 0.6 rows.5
  96.1 0.3 collective-permute-start.20
  96.4 1.2 collective-permute-done.20
  97.6 16.8 %all_to_all.27.refs_3_ = f32[32,16,128]{2,1,0:T(8,128)S(1)} all-to-all(f32[32,16,128]{2,1,0:T(8,128)S(1)} %broadcast_in_dim.8), channel_id=1, replica_groups=mesh['y'=4,'x'=4,'z'=8,'core'=2] {'y','z'}, dimensions={0} | all-to-all | bytes 524288 | tf_op jit(solution)/shard_map/all_to_all | solution.py:236
  114.4 4.2 %grads.1 = (f32[1024,256]{1,0:T(8,128)S(1)}, f32[512,256]{1,0:T(8,128)S(1)}, f32[512,256]{1,0:T(8,128)S(1)}, f32[256,256]{1,0:T(8,128)S(1)}, f32[256,256]{1,0:T(8,128)S(1)}, /*index=5*/f32[512,256]{1,0:T(8,128)S(1)}) custom-call(f32[1024,2048]{1,0:T(8,128)S(1)} %get-tuple-element.49.refs_0_, f32[1024,2048]{1,0:T(8,128)S(1)} %get-tuple-element.56.refs_1_, ...), custom_call_target="tpu_custom_call" | custom-call | flops 2147483648 | bytes 1048576 | tf_op jit(solution)/shard_map/grads/pallas_call | solution.py:35
  118.7 0.1 collective-permute-start.21
  118.8 0.6 collective-permute-start.22
  119.4 2.7 %collective-permute-start.23 = (f32[256,256]{1,0:T(8,128)S(1)}, f32[256,256]{1,0:T(8,128)S(1)}, u32[]{:S(2)}, u32[]{:S(2)}) collective-permute-start(f32[256,256]{1,0:T(8,128)S(1)} %get-tuple-element.83), channel_id=1, source_target_pairs={{0,48},{16,0},{32,16},{48,32},{1,49},{17,1},{33,17},{49,33},{2,50}... | collective-permute-start | bytes 786440 | tf_op jit(solution)/shard_map/ppermute | solution.py:231
  122.1 0.8 pair.1
  122.9 4.6 %all-to-all-start.4 = ((f32[32,16,256]{2,1,0:T(8,128)}), f32[32,16,256]{2,1,0:T(8,128)S(1)}, u32[]{:S(2)}, u32[]{:S(2)}) async-start(f32[32,16,256]{2,1,0:T(8,128)} %pair.1), calls=%async_computation.4 | async-start | bytes 1048576 | tf_op jit(solution)/shard_map/all_to_all | solution.py:335
  127.5 1.2 collective-permute-done.22.refs_2_
  128.7 0.1 relay.1
  128.8 0.1 collective-permute-start.24
  128.9 3.2 %collective-permute-start.25 = (f32[512,256]{1,0:T(8,128)S(1)}, f32[512,256]{1,0:T(8,128)S(1)}, u32[]{:S(2)}, u32[]{:S(2)}) collective-permute-start(f32[512,256]{1,0:T(8,128)S(1)} %get-tuple-element.85), channel_id=1, source_target_pairs={{0,48},{16,0},{32,16},{48,32},{1,49},{17,1},{33,17},{49,33},{2,50}... | collective-permute-start | bytes 1572872 | tf_op jit(solution)/shard_map/ppermute | solution.py:231
  132.1 11.4 %collective-permute-done.24.refs_2_ = f32[512,256]{1,0:T(8,128)S(1)} collective-permute-done((f32[512,256]{1,0:T(8,128)S(1)}, f32[512,256]{1,0:T(8,128)S(1)}, u32[]{:S(2)}, u32[]{:S(2)}) %collective-permute-start.24) | collective-permute-done | bytes 524320 | tf_op jit(solution)/shard_map/ppermute | solution.py:231
  143.6 1.0 proto_grad.1
  144.6 0.6 all-to-all-done.4.refs_1_
  145.2 0.8 row_grad.1
  (25 shorter events, 0.2 us)
Async XLA Ops:
  0.6 16.3 %collective-permute-start = (bf16[512,256]{1,0:T(8,128)(2,1)}, bf16[512,256]{1,0:T(8,128)(2,1)S(1)}, u32[]{:S(2)}, u32[]{:S(2)}) collective-permute-start(bf16[512,256]{1,0:T(8,128)(2,1)} %refs_0_.5), channel_id=1, source_target_pairs={{0,16},{16,32},{32,48},{48,0},{1,17},{17,33},{33,49},{49,1},{2,18}... | collective-permute-start | bytes 786440 | tf_op jit(solution)/shard_map/ppermute | solution.py:231
  2.2 16.9 %collective-permute-start.1 = (bf16[512,256]{1,0:T(8,128)(2,1)}, bf16[512,256]{1,0:T(8,128)(2,1)S(1)}, u32[]{:S(2)}, u32[]{:S(2)}) collective-permute-start(bf16[512,256]{1,0:T(8,128)(2,1)} %refs_0_.5), channel_id=1, source_target_pairs={{0,48},{16,0},{32,16},{48,32},{1,49},{17,1},{33,17},{49,33},{2,50}... | collective-permute-start | bytes 786440 | tf_op jit(solution)/shard_map/ppermute | solution.py:231
  5.5 28.4 %all-to-all-start = ((bf16[32,16,512]{2,1,0:T(8,128)(2,1)}), bf16[32,16,512]{2,1,0:T(8,128)(2,1)S(1)}, u32[]{:S(2)}, u32[]{:S(2)}) async-start(bf16[32,16,512]{2,1,0:T(8,128)(2,1)} %pack.1), calls=%async_computation | async-start | bytes 1048576 | tf_op jit(solution)/shard_map/all_to_all | solution.py:282
  16.9 12.5 %copy-start.1 = (bf16[512,256]{1,0:T(8,128)(2,1)S(1)}, bf16[512,256]{1,0:T(8,128)(2,1)}, u32[]{:S(2)}) copy-start(bf16[512,256]{1,0:T(8,128)(2,1)} %refs_0_.5) | copy-start | bytes 786436
  16.9 25.2 %copy-start = (bf16[512,256]{1,0:T(8,128)(2,1)S(1)}, bf16[512,256]{1,0:T(8,128)(2,1)}, u32[]{:S(2)}) copy-start(bf16[512,256]{1,0:T(8,128)(2,1)} %refs_0_.8) | copy-start | bytes 786436
  16.9 12.9 %collective-permute-start.5 = (bf16[512,256]{1,0:T(8,128)(2,1)}, bf16[512,256]{1,0:T(8,128)(2,1)S(1)}, u32[]{:S(2)}, u32[]{:S(2)}) collective-permute-start(bf16[512,256]{1,0:T(8,128)(2,1)} %refs_0_.8), channel_id=1, source_target_pairs={{0,48},{16,0},{32,16},{48,32},{1,49},{17,1},{33,17},{49,33},{2,50}... | collective-permute-start | bytes 786440 | tf_op jit(solution)/shard_map/ppermute | solution.py:231
  18.6 11.3 %collective-permute-start.4 = (bf16[512,256]{1,0:T(8,128)(2,1)}, bf16[512,256]{1,0:T(8,128)(2,1)S(1)}, u32[]{:S(2)}, u32[]{:S(2)}) collective-permute-start(bf16[512,256]{1,0:T(8,128)(2,1)} %refs_0_.8), channel_id=1, source_target_pairs={{0,16},{16,32},{32,48},{48,0},{1,17},{17,33},{33,49},{49,1},{2,18}... | collective-permute-start | bytes 786440 | tf_op jit(solution)/shard_map/ppermute | solution.py:231
  19.1 10.4 %collective-permute-start.2 = (bf16[256,256]{1,0:T(8,128)(2,1)S(1)}, bf16[256,256]{1,0:T(8,128)(2,1)S(1)}, u32[]{:S(2)}, u32[]{:S(2)}) collective-permute-start(bf16[256,256]{1,0:T(8,128)(2,1)S(1)} %get-tuple-element.44), channel_id=1, source_target_pairs={{0,16},{16,32},{32,48},{48,0},{1,17},{17,33},{33,49},{49,1},{2,18}... | collective-permute-start | bytes 393224 | tf_op jit(solution)/shard_map/ppermute | solution.py:231
  19.4 10.0 %collective-permute-start.3 = (bf16[256,256]{1,0:T(8,128)(2,1)S(1)}, bf16[256,256]{1,0:T(8,128)(2,1)S(1)}, u32[]{:S(2)}, u32[]{:S(2)}) collective-permute-start(bf16[256,256]{1,0:T(8,128)(2,1)S(1)} %get-tuple-element.45), channel_id=1, source_target_pairs={{0,48},{16,0},{32,16},{48,32},{1,49},{17,1},{33,17},{49,33},{2,50}... | collective-permute-start | bytes 393224 | tf_op jit(solution)/shard_map/ppermute | solution.py:231
  34.0 3.3 %collective-permute-start.6 = (bf16[512,512]{1,0:T(8,128)(2,1)S(1)}, bf16[512,512]{1,0:T(8,128)(2,1)S(1)}, u32[]{:S(2)}, u32[]{:S(2)}) collective-permute-start(bf16[512,512]{1,0:T(8,128)(2,1)S(1)} %bitcast.1), channel_id=1, source_target_pairs={{0,1},{1,0},{2,3},{3,2},{4,5},{5,4},{6,7},{7,6},{8,9},{9,8},{10,11... | collective-permute-start | bytes 1572872 | tf_op jit(solution)/shard_map/ppermute | solution.py:231
  34.0 8.1 %collective-permute-start.8 = (bf16[256,256]{1,0:T(8,128)(2,1)S(1)}, bf16[256,256]{1,0:T(8,128)(2,1)S(1)}, u32[]{:S(2)}, u32[]{:S(2)}) collective-permute-start(bf16[256,256]{1,0:T(8,128)(2,1)S(1)} %get-tuple-element.52), channel_id=1, source_target_pairs={{0,16},{16,32},{32,48},{48,0},{1,17},{17,33},{33,49},{49,1},{2,18}... | collective-permute-start | bytes 393224 | tf_op jit(solution)/shard_map/ppermute | solution.py:231
  34.4 7.8 %collective-permute-start.9 = (bf16[256,256]{1,0:T(8,128)(2,1)S(1)}, bf16[256,256]{1,0:T(8,128)(2,1)S(1)}, u32[]{:S(2)}, u32[]{:S(2)}) collective-permute-start(bf16[256,256]{1,0:T(8,128)(2,1)S(1)} %get-tuple-element.53), channel_id=1, source_target_pairs={{0,48},{16,0},{32,16},{48,32},{1,49},{17,1},{33,17},{49,33},{2,50}... | collective-permute-start | bytes 393224 | tf_op jit(solution)/shard_map/ppermute | solution.py:231
  39.5 3.7 %collective-permute-start.7 = (f32[4,512]{1,0:T(4,128)S(1)}, f32[4,512]{1,0:T(4,128)S(1)}, u32[]{:S(2)}, u32[]{:S(2)}) collective-permute-start(f32[4,512]{1,0:T(4,128)S(1)} %get-tuple-element.50), channel_id=1, source_target_pairs={{0,48},{16,0},{32,16},{48,32},{1,49},{17,1},{33,17},{49,33},{2,50}... | collective-permute-start | bytes 24584 | tf_op jit(solution)/shard_map/ppermute | solution.py:231
  39.8 4.9 %collective-permute-start.10 = (f32[4,512]{1,0:T(4,128)S(1)}, f32[4,512]{1,0:T(4,128)S(1)}, u32[]{:S(2)}, u32[]{:S(2)}) collective-permute-start(f32[4,512]{1,0:T(4,128)S(1)} %get-tuple-element.58), channel_id=1, source_target_pairs={{0,16},{16,32},{32,48},{48,0},{1,17},{17,33},{33,49},{49,1},{2,18}... | collective-permute-start | bytes 24584 | tf_op jit(solution)/shard_map/ppermute | solution.py:231
  41.5 5.2 %collective-permute-start.11 = (f32[4,512]{1,0:T(4,128)S(1)}, f32[4,512]{1,0:T(4,128)S(1)}, u32[]{:S(2)}, u32[]{:S(2)}) collective-permute-start(f32[4,512]{1,0:T(4,128)S(1)} %get-tuple-element.59), channel_id=1, source_target_pairs={{0,32},{16,48},{32,0},{48,16},{1,33},{17,49},{33,1},{49,17},{2,34}... | collective-permute-start | bytes 24584 | tf_op jit(solution)/shard_map/ppermute | solution.py:231
  47.4 1.2 collective-permute-start.12
  65.0 4.9 %collective-permute-start.13 = (f32[4,512]{1,0:T(4,128)S(1)}, f32[4,512]{1,0:T(4,128)S(1)}, u32[]{:S(2)}, u32[]{:S(2)}) collective-permute-start(f32[4,512]{1,0:T(4,128)S(1)} %get-tuple-element.64), channel_id=1, source_target_pairs={{0,16},{16,32},{32,48},{48,0},{1,17},{17,33},{33,49},{49,1},{2,18}... | collective-permute-start | bytes 24584 | tf_op jit(solution)/shard_map/ppermute | solution.py:231
  65.1 5.2 %collective-permute-start.14 = (f32[4,512]{1,0:T(4,128)S(1)}, f32[4,512]{1,0:T(4,128)S(1)}, u32[]{:S(2)}, u32[]{:S(2)}) collective-permute-start(f32[4,512]{1,0:T(4,128)S(1)} %get-tuple-element.65), channel_id=1, source_target_pairs={{0,32},{16,48},{32,0},{48,16},{1,33},{17,49},{33,1},{49,17},{2,34}... | collective-permute-start | bytes 24584 | tf_op jit(solution)/shard_map/ppermute | solution.py:231
  67.7 3.7 %collective-permute-start.15 = (f32[4,512]{1,0:T(4,128)S(1)}, f32[4,512]{1,0:T(4,128)S(1)}, u32[]{:S(2)}, u32[]{:S(2)}) collective-permute-start(f32[4,512]{1,0:T(4,128)S(1)} %get-tuple-element.66), channel_id=1, source_target_pairs={{0,48},{16,0},{32,16},{48,32},{1,49},{17,1},{33,17},{49,33},{2,50}... | collective-permute-start | bytes 24584 | tf_op jit(solution)/shard_map/ppermute | solution.py:231
  72.1 1.2 collective-permute-start.16
  88.2 6.3 %collective-permute-start.17 = (f32[4,512]{1,0:T(4,128)S(1)}, f32[4,512]{1,0:T(4,128)S(1)}, u32[]{:S(2)}, u32[]{:S(2)}) collective-permute-start(f32[4,512]{1,0:T(4,128)S(1)} %get-tuple-element.70), channel_id=1, source_target_pairs={{0,16},{16,32},{32,48},{48,0},{1,17},{17,33},{33,49},{49,1},{2,18}... | collective-permute-start | bytes 24584 | tf_op jit(solution)/shard_map/ppermute | solution.py:231
  89.7 5.2 %collective-permute-start.18 = (f32[4,512]{1,0:T(4,128)S(1)}, f32[4,512]{1,0:T(4,128)S(1)}, u32[]{:S(2)}, u32[]{:S(2)}) collective-permute-start(f32[4,512]{1,0:T(4,128)S(1)} %get-tuple-element.71), channel_id=1, source_target_pairs={{0,32},{16,48},{32,0},{48,16},{1,33},{17,49},{33,1},{49,17},{2,34}... | collective-permute-start | bytes 24584 | tf_op jit(solution)/shard_map/ppermute | solution.py:231
  91.8 3.7 %collective-permute-start.19 = (f32[4,512]{1,0:T(4,128)S(1)}, f32[4,512]{1,0:T(4,128)S(1)}, u32[]{:S(2)}, u32[]{:S(2)}) collective-permute-start(f32[4,512]{1,0:T(4,128)S(1)} %get-tuple-element.72), channel_id=1, source_target_pairs={{0,48},{16,0},{32,16},{48,32},{1,49},{17,1},{33,17},{49,33},{2,50}... | collective-permute-start | bytes 24584 | tf_op jit(solution)/shard_map/ppermute | solution.py:231
  96.1 1.5 %collective-permute-start.20 = (f32[16,128]{1,0:T(8,128)S(1)}, f32[16,128]{1,0:T(8,128)S(1)}, u32[]{:S(2)}, u32[]{:S(2)}) collective-permute-start(f32[16,128]{1,0:T(8,128)S(1)} %get-tuple-element.76), channel_id=1, source_target_pairs={{0,1},{1,0},{2,3},{3,2},{4,5},{5,4},{6,7},{7,6},{8,9},{9,8},{10,11... | collective-permute-start | bytes 24584 | tf_op jit(solution)/shard_map/ppermute | solution.py:231
  118.7 3.4 %collective-permute-start.21 = (f32[512,256]{1,0:T(8,128)S(1)}, f32[512,256]{1,0:T(8,128)S(1)}, u32[]{:S(2)}, u32[]{:S(2)}) collective-permute-start(f32[512,256]{1,0:T(8,128)S(1)} %slice.3), channel_id=1, source_target_pairs={{0,1},{1,0},{2,3},{3,2},{4,5},{5,4},{6,7},{7,6},{8,9},{9,8},{10,11... | collective-permute-start | bytes 1572872 | tf_op jit(solution)/shard_map/ppermute | solution.py:231
  118.8 9.9 %collective-permute-start.22 = (f32[256,256]{1,0:T(8,128)S(1)}, f32[256,256]{1,0:T(8,128)S(1)}, u32[]{:S(2)}, u32[]{:S(2)}) collective-permute-start(f32[256,256]{1,0:T(8,128)S(1)} %get-tuple-element.82), channel_id=1, source_target_pairs={{0,16},{16,32},{32,48},{48,0},{1,17},{17,33},{33,49},{49,1},{2,18}... | collective-permute-start | bytes 786440 | tf_op jit(solution)/shard_map/ppermute | solution.py:231
  119.4 9.3 %collective-permute-start.23 = (f32[256,256]{1,0:T(8,128)S(1)}, f32[256,256]{1,0:T(8,128)S(1)}, u32[]{:S(2)}, u32[]{:S(2)}) collective-permute-start(f32[256,256]{1,0:T(8,128)S(1)} %get-tuple-element.83), channel_id=1, source_target_pairs={{0,48},{16,0},{32,16},{48,32},{1,49},{17,1},{33,17},{49,33},{2,50}... | collective-permute-start | bytes 786440 | tf_op jit(solution)/shard_map/ppermute | solution.py:231
  122.9 22.2 %all-to-all-start.4 = ((f32[32,16,256]{2,1,0:T(8,128)}), f32[32,16,256]{2,1,0:T(8,128)S(1)}, u32[]{:S(2)}, u32[]{:S(2)}) async-start(f32[32,16,256]{2,1,0:T(8,128)} %pair.1), calls=%async_computation.4 | async-start | bytes 1048576 | tf_op jit(solution)/shard_map/all_to_all | solution.py:335
  128.7 16.5 %copy-start.2 = (bf16[16,256]{1,0:T(8,128)(2,1)S(1)}, bf16[16,256]{1,0:T(8,128)(2,1)}, u32[]{:S(2)}) copy-start(bf16[16,256]{1,0:T(8,128)(2,1)} %refs_0_.7) | copy-start | bytes 24580
  128.8 14.8 %collective-permute-start.24 = (f32[512,256]{1,0:T(8,128)S(1)}, f32[512,256]{1,0:T(8,128)S(1)}, u32[]{:S(2)}, u32[]{:S(2)}) collective-permute-start(f32[512,256]{1,0:T(8,128)S(1)} %get-tuple-element.84), channel_id=1, source_target_pairs={{0,16},{16,32},{32,48},{48,0},{1,17},{17,33},{33,49},{49,1},{2,18}... | collective-permute-start | bytes 1572872 | tf_op jit(solution)/shard_map/ppermute | solution.py:231
  128.9 14.6 %collective-permute-start.25 = (f32[512,256]{1,0:T(8,128)S(1)}, f32[512,256]{1,0:T(8,128)S(1)}, u32[]{:S(2)}, u32[]{:S(2)}) collective-permute-start(f32[512,256]{1,0:T(8,128)S(1)} %get-tuple-element.85), channel_id=1, source_target_pairs={{0,48},{16,0},{32,16},{48,32},{1,49},{17,1},{33,17},{49,33},{2,50}... | collective-permute-start | bytes 1572872 | tf_op jit(solution)/shard_map/ppermute | solution.py:231

commit v5 on v4

--- a/solution.py
+++ b/solution.py
@@ -163,44 +163,53 @@
             r = slice(i * LANES, (i + 1) * LANES)
             total = total + exp_ref[r, at : at + LANES] * scale[k : k + 1, o : o + LANES]
         out_ref[i : i + 1, :] = row_of_sums(total)
+    half = count // 2
+    swap_ref[:half, :] = out_ref[half:, :]
+    swap_ref[half:, :] = out_ref[:half, :]
     for ref in extra:
-        out_ref[count : 2 * count, :] = ref[...]
-    for at in range(0, out_ref.shape[0], count):
-        swap_ref[at : at + count // 2, :] = out_ref[at + count // 2 : at + count, :]
-        swap_ref[at + count // 2 : at + count, :] = out_ref[at : at + count // 2, :]
-
-
-def grads_kernel(
-    factor, exp_t, exp_s, scale_ref, mass_ref, feat_ref, weight_ref, feat_out, w0, w1, w2a, w2b, w3, grad_ref
-):
-    inverse = factor / jnp.sum(mass_ref[...], axis=0)
-    rows, cols = exp_t.shape
+        out_ref[half:, :] = ref[:half, :]
+        swap_ref[half:, :] = ref[half:, :]
+
+
+def scale_kernel(factor, mass_ref, out_ref):
+    out_ref[...] = factor / jnp.sum(mass_ref[...], axis=0)
+
+
+def logits_kernel(first, exp_t, exp_s, scale_ref, inverse_ref, weight_ref, grad_ref, feat_out):
+    rows, cols = grad_ref.shape
     count, block = rows // LANES, cols // STEPS
-    row = [column(inverse[i : i + 1, :]) for i in range(count)]
-    total = [column(inverse[count + i : count + i + 1, :]) for i in range(count)]
-    for k, outs in enumerate(((w0,), (w1,), (w2a, w2b), (w3,))):
-        for i in range(count):
-            r = slice(i * LANES, (i + 1) * LANES)
-            for o in range(0, block, LANES):
-                c = slice(k * block + o, k * block + o + LANES)
-                target = exp_t[r, c] * scale_ref[k : k + 1, o : o + LANES] * row[i]
-                grad_ref[r, c] = (exp_s[r, c] * total[i] - target).astype(bf16)
-        at = k * block
-        for out in outs:
-            size = out.shape[0]
-            out[...] = lax.dot_general(
+    for i in range(count):
+        r = slice(i * LANES, (i + 1) * LANES)
+        e = slice(first + i * LANES, first + (i + 1) * LANES)
+        row = column(inverse_ref[i : i + 1, :])
+        total = column(inverse_ref[count + i : count + i + 1, :])
+        for at in range(0, cols, LANES):
+            k, o = at // block, at % block
+            c = slice(at, at + LANES)
+            target = exp_t[e, c] * scale_ref[k : k + 1, o : o + LANES] * row
+            grad_ref[r, c] = (exp_s[e, c] * total - target).astype(bf16)
+    feat_out[...] = jnp.dot(grad_ref[...], weight_ref[...], preferred_element_type=f32)
+
+
+def weights_kernel(grad_own, grad_sib, feat_ref, *outs):
+    half = grad_own.shape[0]
+    at = 0
+    for out in outs:
+        size = out.shape[0]
+        total = 0.0
+        for grad_ref, first in ((grad_own, 0), (grad_sib, half)):
+            total = total + lax.dot_general(
                 grad_ref[:, at : at + size],
-                feat_ref[...],
+                feat_ref[first : first + half, :],
                 (((0,), (0,)), ((), ())),
                 preferred_element_type=f32,
             )
-            at += size
-    feat_out[...] = jnp.dot(grad_ref[...], weight_ref[...], preferred_element_type=f32)
+        out[...] = total
+        at += size
 
 
 def pair_kernel(mine, other, out):
-    half = other.shape[0]
-    out[...] = (mine[:half, :] + other[...]).reshape(out.shape)
+    out[...] = (mine[...] + other[...]).reshape(out.shape)
 
 
 def relay_kernel(forward, back, upper, lower, forward_out, back_out):
@@ -301,7 +310,7 @@
     for sweep in range(SWEEPS):
         last = sweep + 1 == SWEEPS
         extra = (student_sums,) if last else ()
-        out = jax.ShapeDtypeStruct((rows // LANES * (1 + len(extra)), LANES), f32)
+        out = jax.ShapeDtypeStruct((rows // LANES, LANES), f32)
         mine, swapped, scale = call(
             row_kernel,
             [out, out, masses[0]],
@@ -313,24 +322,43 @@
         if not last:
             mass = share(call(column_kernel, masses, (exp_t, row_masses), work // 8, "columns"))
 
-    feat_grad, *weight_parts = call(
-        functools.partial(grads_kernel, factor),
+    half = rows // 2
+    inverse = call(
+        functools.partial(scale_kernel, factor),
+        jax.ShapeDtypeStruct((rows // LANES, LANES), f32),
+        (row_masses,),
+        0,
+        "scales",
+    )
+    def logits(first, scales, after):
+        return call(
+            functools.partial(logits_kernel, first),
+            [pltpu.VMEM((half, cols), bf16), jax.ShapeDtypeStruct((half, width), f32)],
+            (exp_t, exp_s, scale, scales, student_weight),
+            work // 2,
+            "logits",
+            after=after,
+        )
+
+    own_grads, own_feat = logits(0, inverse, ())
+    sib_grads, sib_feat = logits(half, shift(inverse, "core", 1), (own_feat,))
+    weight_parts = call(
+        weights_kernel,
         [
             jax.ShapeDtypeStruct((size, width), f32)
-            for size in (rows, own_protos, own_protos, own_protos // 2, own_protos // 2, own_protos)
+            for size in (own_protos, own_protos, own_protos // 2, own_protos // 2, own_protos)
         ],
-        (exp_t, exp_s, scale, row_masses, student_feat, student_weight),
-        2 * work,
-        "grads",
-        [pltpu.VMEM((rows, cols), bf16)],
-    )
-    half = rows // 2
+        (own_grads, sib_grads, student_feat),
+        work,
+        "weights",
+    )
     feat_pair = call(
         pair_kernel,
         jax.ShapeDtypeStruct((half // own_rows, own_rows, width), f32),
-        (feat_grad, shift(feat_grad[half:], "core", 1)),
+        (own_feat, shift(sib_feat, "core", 1)),
         100 * work,
         "pair",
+        after=weight_parts[:1],
     )
     feat_share = lax.all_to_all(feat_pair, ROWS, 0, 0, tiled=True)
     own_part, back_part, upper_part, lower_part, forward_part = weight_parts

time: 147 us -> 144 us (0.980)
  blocking collectives: 46.6 us -> 44 us
    all_to_all x3, blocking collectives: 46.6 us -> 44 us  [spread(): lax.all_to_all(jnp.broadcast_to(values[None], (count,) + values.shape), R...]
    ppermute x26 -> x27, waiting for transfers between devices: 31.3 us -> 30.6 us  [shift(): lax.ppermute(values, axis, [(i, (i + step) % size) for i in range(size)])]
    ppermute x26 -> x27, starting transfers between devices: 29.3 us -> 29.9 us  [shift(): lax.ppermute(values, axis, [(i, (i + step) % size) for i in range(size)])]
    pallas_call x17 -> x20, Pallas kernels: 17.2 us -> 17 us  [call(): pl.pallas_call(lambda *refs: kernel(*refs[count:]), out_shape=outs, in_sp...]
  transfers between devices with their start and end apart: 28 -> 29, of which waited for: 16 -> 16; matrix products, arithmetic and copies ran while one was open for 0% -> 0% of each run, Pallas kernels for 6% -> 8%
where the time goes in v5:
time: 144 us; the launch traced here: 143 us
  starting transfers between devices  45.6 us (32%)
  blocking collectives  44 us (31%)
  waiting for transfers between devices  36 us (25%)
  Pallas kernels  17 us (12%)
    all_to_all x3, blocking collectives, spread(): lax.all_to_all(jnp.broadcast_to(values[None], (count,) + values.shape), R...  44 us
    ppermute x27, waiting for transfers between devices, shift(): lax.ppermute(values, axis, [(i, (i + step) % size) for i in range(size)])  30.6 us
    ppermute x27, starting transfers between devices, shift(): lax.ppermute(values, axis, [(i, (i + step) % size) for i in range(size)])  29.9 us
    pallas_call x20, Pallas kernels, call(): pl.pallas_call(lambda *refs: kernel(*refs[count:]), out_shape=outs, in_sp...  17 us
    all_to_all x1, starting transfers between devices, body(): own = lax.all_to_all(packed, ROWS, 0, 0, tiled=True).reshape(-1, 2 * width)  11.4 us
    all_to_all x1, starting transfers between devices, body(): feat_share = lax.all_to_all(feat_pair, ROWS, 0, 0, tiled=True)  4.37 us
    all_to_all x1, waiting for transfers between devices, body(): own = lax.all_to_all(packed, ROWS, 0, 0, tiled=True).reshape(-1, 2 * width)  4.11 us
  transfers between devices with their start and end apart: 29, of which 16 were waited for; matrix products, arithmetic and copies ran while one was open for 0% of the time, Pallas kernels for 8%

profile of v5, /device:TPU:32, one launch (start us, length us, event | category | flops | bytes accessed | tf_op | source)
XLA Modules:
  0.0 143.5 jit_solution(6993157320175133409)
XLA Ops:
  0.6 1.6 %collective-permute-start = (bf16[512,256]{1,0:T(8,128)(2,1)}, bf16[512,256]{1,0:T(8,128)(2,1)S(1)}, u32[]{:S(2)}, u32[]{:S(2)}) collective-permute-start(bf16[512,256]{1,0:T(8,128)(2,1)} %refs_0_.5), channel_id=1, source_target_pairs={{0,16},{16,32},{32,48},{48,0},{1,17},{17,33},{33,49},{49,1},{2,18}... | collective-permute-start | bytes 786440 | tf_op jit(solution)/shard_map/ppermute | solution.py:240
  2.2 1.7 %collective-permute-start.1 = (bf16[512,256]{1,0:T(8,128)(2,1)}, bf16[512,256]{1,0:T(8,128)(2,1)S(1)}, u32[]{:S(2)}, u32[]{:S(2)}) collective-permute-start(bf16[512,256]{1,0:T(8,128)(2,1)} %refs_0_.5), channel_id=1, source_target_pairs={{0,48},{16,0},{32,16},{48,32},{1,49},{17,1},{33,17},{49,33},{2,50}... | collective-permute-start | bytes 786440 | tf_op jit(solution)/shard_map/ppermute | solution.py:240
  3.9 1.6 %pack.1 = bf16[32,16,512]{2,1,0:T(8,128)(2,1)} custom-call(bf16[16,256]{1,0:T(8,128)(2,1)} %refs_0_.4, bf16[16,256]{1,0:T(8,128)(2,1)} %refs_0_.7), custom_call_target="tpu_custom_call" | custom-call | bytes 1048576 | tf_op jit(solution)/shard_map/pack/pallas_call | solution.py:35
  5.5 11.4 %all-to-all-start = ((bf16[32,16,512]{2,1,0:T(8,128)(2,1)}), bf16[32,16,512]{2,1,0:T(8,128)(2,1)S(1)}, u32[]{:S(2)}, u32[]{:S(2)}) async-start(bf16[32,16,512]{2,1,0:T(8,128)(2,1)} %pack.1), calls=%async_computation | async-start | bytes 1048576 | tf_op jit(solution)/shard_map/all_to_all | solution.py:291
  16.9 0.0 copy-start.1
  16.9 0.0 copy-start
  16.9 1.6 %collective-permute-start.5 = (bf16[512,256]{1,0:T(8,128)(2,1)}, bf16[512,256]{1,0:T(8,128)(2,1)S(1)}, u32[]{:S(2)}, u32[]{:S(2)}) collective-permute-start(bf16[512,256]{1,0:T(8,128)(2,1)} %refs_0_.8), channel_id=1, source_target_pairs={{0,48},{16,0},{32,16},{48,32},{1,49},{17,1},{33,17},{49,33},{2,50}... | collective-permute-start | bytes 786440 | tf_op jit(solution)/shard_map/ppermute | solution.py:240
  18.6 0.5 collective-permute-start.4
  19.1 0.3 collective-permute-start.2
  19.4 3.0 %collective-permute-start.3 = (bf16[256,256]{1,0:T(8,128)(2,1)S(1)}, bf16[256,256]{1,0:T(8,128)(2,1)S(1)}, u32[]{:S(2)}, u32[]{:S(2)}) collective-permute-start(bf16[256,256]{1,0:T(8,128)(2,1)S(1)} %get-tuple-element.48), channel_id=1, source_target_pairs={{0,48},{16,0},{32,16},{48,32},{1,49},{17,1},{33,17},{49,33},{2,50}... | collective-permute-start | bytes 393224 | tf_op jit(solution)/shard_map/ppermute | solution.py:240
  22.4 7.0 %collective-permute-done.2.refs_2_ = bf16[256,256]{1,0:T(8,128)(2,1)S(1)} collective-permute-done((bf16[256,256]{1,0:T(8,128)(2,1)S(1)}, bf16[256,256]{1,0:T(8,128)(2,1)S(1)}, u32[]{:S(2)}, u32[]{:S(2)}) %collective-permute-start.2) | collective-permute-done | bytes 131104 | tf_op jit(solution)/shard_map/ppermute | solution.py:240
  29.5 0.4 teacher_units.1.refs_2_
  29.9 4.1 %all-to-all-done = bf16[32,16,512]{2,1,0:T(8,128)(2,1)S(1)} async-done(((bf16[32,16,512]{2,1,0:T(8,128)(2,1)}), bf16[32,16,512]{2,1,0:T(8,128)(2,1)S(1)}, u32[]{:S(2)}, u32[]{:S(2)}) %all-to-all-start) | async-done | bytes 524320 | tf_op jit(solution)/shard_map/all_to_all | solution.py:291
  34.0 0.4 collective-permute-start.8
  34.4 3.0 %collective-permute-start.9 = (bf16[256,256]{1,0:T(8,128)(2,1)S(1)}, bf16[256,256]{1,0:T(8,128)(2,1)S(1)}, u32[]{:S(2)}, u32[]{:S(2)}) collective-permute-start(bf16[256,256]{1,0:T(8,128)(2,1)S(1)} %get-tuple-element.56), channel_id=1, source_target_pairs={{0,48},{16,0},{32,16},{48,32},{1,49},{17,1},{33,17},{49,33},{2,50}... | collective-permute-start | bytes 393224 | tf_op jit(solution)/shard_map/ppermute | solution.py:240
  37.3 2.2 %teacher.1 = (f32[1024,2048]{1,0:T(8,128)S(1)}, f32[4,512]{1,0:T(4,128)S(1)}, f32[4,512]{1,0:T(4,128)S(1)}, f32[4,512]{1,0:T(4,128)S(1)}, f32[4,512]{1,0:T(4,128)S(1)}, /*index=5*/bf16[1024,256]{1,0:T(8,128)(2,1)}) custom-call(bf16[512,512]{1,0:T(8,128)(2,1)S(1)} %bitcast.2, bf16[512,512]{1,0:T(8,128)(2,1)S(1)} %collective-permute-done.6.refs_1_, ...), custom_call_target="tpu_custom_call" | custom-call | flops 1073741824 | bytes 1048576 | tf_op jit(solution)/shard_map/teacher/pallas_call | solution.py:35
  39.5 0.3 collective-permute-start.7
  39.8 1.7 %collective-permute-start.10 = (f32[4,512]{1,0:T(4,128)S(1)}, f32[4,512]{1,0:T(4,128)S(1)}, u32[]{:S(2)}, u32[]{:S(2)}) collective-permute-start(f32[4,512]{1,0:T(4,128)S(1)} %get-tuple-element.61), channel_id=1, source_target_pairs={{0,16},{16,32},{32,48},{48,0},{1,17},{17,33},{33,49},{49,1},{2,18}... | collective-permute-start | bytes 24584 | tf_op jit(solution)/shard_map/ppermute | solution.py:240
  41.5 0.6 collective-permute-start.11
  42.1 0.4 student_units.1.refs_2_.refs_4_.refs_5_
  42.5 0.6 collective-permute-done.7.refs_4_
  43.2 1.5 %collective-permute-done.10.refs_2_ = f32[4,512]{1,0:T(4,128)S(1)} collective-permute-done((f32[4,512]{1,0:T(4,128)S(1)}, f32[4,512]{1,0:T(4,128)S(1)}, u32[]{:S(2)}, u32[]{:S(2)}) %collective-permute-start.10) | collective-permute-done | bytes 8224 | tf_op jit(solution)/shard_map/ppermute | solution.py:240
  44.7 2.0 %collective-permute-done.11.refs_3_ = f32[4,512]{1,0:T(4,128)S(1)} collective-permute-done((f32[4,512]{1,0:T(4,128)S(1)}, f32[4,512]{1,0:T(4,128)S(1)}, u32[]{:S(2)}, u32[]{:S(2)}) %collective-permute-start.11) | collective-permute-done | bytes 8224 | tf_op jit(solution)/shard_map/ppermute | solution.py:240
  46.7 0.7 rows.3
  47.4 1.2 collective-permute-done.12
  48.6 15.6 %all_to_all.25.refs_1_ = f32[32,8,128]{2,1,0:T(8,128)S(1)} all-to-all(f32[32,8,128]{2,1,0:T(8,128)S(1)} %broadcast_in_dim.6), channel_id=1, replica_groups=mesh['y'=4,'x'=4,'z'=8,'core'=2] {'y','z'}, dimensions={0} | all-to-all | bytes 262144 | tf_op jit(solution)/shard_map/all_to_all | solution.py:245
  64.2 0.7 columns.2
  65.0 0.1 collective-permute-start.13
  65.1 2.7 %collective-permute-start.14 = (f32[4,512]{1,0:T(4,128)S(1)}, f32[4,512]{1,0:T(4,128)S(1)}, u32[]{:S(2)}, u32[]{:S(2)}) collective-permute-start(f32[4,512]{1,0:T(4,128)S(1)} %get-tuple-element.68), channel_id=1, source_target_pairs={{0,32},{16,48},{32,0},{48,16},{1,33},{17,49},{33,1},{49,17},{2,34}... | collective-permute-start | bytes 24584 | tf_op jit(solution)/shard_map/ppermute | solution.py:240
  67.7 0.6 collective-permute-start.15
  68.3 1.6 %collective-permute-done.13.refs_2_ = f32[4,512]{1,0:T(4,128)S(1)} collective-permute-done((f32[4,512]{1,0:T(4,128)S(1)}, f32[4,512]{1,0:T(4,128)S(1)}, u32[]{:S(2)}, u32[]{:S(2)}) %collective-permute-start.13) | collective-permute-done | bytes 8224 | tf_op jit(solution)/shard_map/ppermute | solution.py:240
  69.9 0.4 collective-permute-done.14.refs_3_
  70.3 1.1 collective-permute-done.15.refs_4_
  71.4 0.7 rows.4
  72.1 1.2 collective-permute-done.16
  73.3 14.2 %all_to_all.26.refs_1_ = f32[32,8,128]{2,1,0:T(8,128)S(1)} all-to-all(f32[32,8,128]{2,1,0:T(8,128)S(1)} %broadcast_in_dim.7), channel_id=1, replica_groups=mesh['y'=4,'x'=4,'z'=8,'core'=2] {'y','z'}, dimensions={0} | all-to-all | bytes 262144 | tf_op jit(solution)/shard_map/all_to_all | solution.py:245
  87.5 0.7 columns.3
  88.2 1.5 %collective-permute-start.17 = (f32[4,512]{1,0:T(4,128)S(1)}, f32[4,512]{1,0:T(4,128)S(1)}, u32[]{:S(2)}, u32[]{:S(2)}) collective-permute-start(f32[4,512]{1,0:T(4,128)S(1)} %get-tuple-element.73), channel_id=1, source_target_pairs={{0,16},{16,32},{32,48},{48,0},{1,17},{17,33},{33,49},{49,1},{2,18}... | collective-permute-start | bytes 24584 | tf_op jit(solution)/shard_map/ppermute | solution.py:240
  89.7 2.1 %collective-permute-start.18 = (f32[4,512]{1,0:T(4,128)S(1)}, f32[4,512]{1,0:T(4,128)S(1)}, u32[]{:S(2)}, u32[]{:S(2)}) collective-permute-start(f32[4,512]{1,0:T(4,128)S(1)} %get-tuple-element.74), channel_id=1, source_target_pairs={{0,32},{16,48},{32,0},{48,16},{1,33},{17,49},{33,1},{49,17},{2,34}... | collective-permute-start | bytes 24584 | tf_op jit(solution)/shard_map/ppermute | solution.py:240
  91.8 0.7 collective-permute-start.19
  92.5 2.1 %student.1 = (f32[1024,2048]{1,0:T(8,128)S(1)}, f32[8,128]{1,0:T(8,128)S(1)}, bf16[1024,256]{1,0:T(8,128)(2,1)S(1)}) custom-call(bf16[512,512]{1,0:T(8,128)(2,1)S(1)} %bitcast.3, bf16[512,512]{1,0:T(8,128)(2,1)S(1)} %collective-permute-done.6.refs_1_, bf16[2048,256]{1,0:T(8,128)(2,1)S(1)} %student_units.1.refs_2_.refs_4_.refs_5_), custom_call_target="tpu_custom_call" | custom-call | flops 1073741824 | bytes 1048576 | tf_op jit(solution)/shard_map/student/pallas_call | solution.py:35
  94.5 0.3 collective-permute-done.18.refs_3_
  94.9 0.6 collective-permute-done.19.refs_4_
  95.5 0.6 rows.5
  96.1 0.3 collective-permute-start.20
  96.4 1.2 collective-permute-done.20
  97.6 14.2 %all_to_all.27.refs_0_ = f32[32,8,128]{2,1,0:T(8,128)S(1)} all-to-all(f32[32,8,128]{2,1,0:T(8,128)S(1)} %broadcast_in_dim.8), channel_id=1, replica_groups=mesh['y'=4,'x'=4,'z'=8,'core'=2] {'y','z'}, dimensions={0} | all-to-all | bytes 262144 | tf_op jit(solution)/shard_map/all_to_all | solution.py:245
  111.8 0.1 collective-permute-start.21
  111.9 1.3 logits.2
  113.2 1.3 logits.3
  114.5 0.6 collective-permute-start.22
  115.1 1.4 weights.1
  116.5 0.6 collective-permute-start.23
  117.1 2.7 %collective-permute-start.24 = (f32[256,256]{1,0:T(8,128)S(1)}, f32[256,256]{1,0:T(8,128)S(1)}, u32[]{:S(2)}, u32[]{:S(2)}) collective-permute-start(f32[256,256]{1,0:T(8,128)S(1)} %get-tuple-element.89), channel_id=1, source_target_pairs={{0,48},{16,0},{32,16},{48,32},{1,49},{17,1},{33,17},{49,33},{2,50}... | collective-permute-start | bytes 786440 | tf_op jit(solution)/shard_map/ppermute | solution.py:240
  119.8 0.9 pair.1
  120.7 4.4 %all-to-all-start.4 = ((f32[32,16,256]{2,1,0:T(8,128)}), f32[32,16,256]{2,1,0:T(8,128)S(1)}, u32[]{:S(2)}, u32[]{:S(2)}) async-start(f32[32,16,256]{2,1,0:T(8,128)} %pair.1), calls=%async_computation.4 | async-start | bytes 1048576 | tf_op jit(solution)/shard_map/all_to_all | solution.py:363
  125.1 1.0 collective-permute-done.23.refs_2_
  126.0 0.1 relay.1
  126.1 0.1 collective-permute-start.25
  126.2 3.2 %collective-permute-start.26 = (f32[512,256]{1,0:T(8,128)S(1)}, f32[512,256]{1,0:T(8,128)S(1)}, u32[]{:S(2)}, u32[]{:S(2)}) collective-permute-start(f32[512,256]{1,0:T(8,128)S(1)} %get-tuple-element.91), channel_id=1, source_target_pairs={{0,48},{16,0},{32,16},{48,32},{1,49},{17,1},{33,17},{49,33},{2,50}... | collective-permute-start | bytes 1572872 | tf_op jit(solution)/shard_map/ppermute | solution.py:240
  129.4 11.0 %collective-permute-done.25.refs_2_ = f32[512,256]{1,0:T(8,128)S(1)} collective-permute-done((f32[512,256]{1,0:T(8,128)S(1)}, f32[512,256]{1,0:T(8,128)S(1)}, u32[]{:S(2)}, u32[]{:S(2)}) %collective-permute-start.25) | collective-permute-done | bytes 524320 | tf_op jit(solution)/shard_map/ppermute | solution.py:240
  140.4 1.0 proto_grad.1
  141.4 1.2 all-to-all-done.4.refs_1_
  142.7 0.8 row_grad.1
  (29 shorter events, 0.2 us)
Async XLA Ops:
  0.6 16.3 %collective-permute-start = (bf16[512,256]{1,0:T(8,128)(2,1)}, bf16[512,256]{1,0:T(8,128)(2,1)S(1)}, u32[]{:S(2)}, u32[]{:S(2)}) collective-permute-start(bf16[512,256]{1,0:T(8,128)(2,1)} %refs_0_.5), channel_id=1, source_target_pairs={{0,16},{16,32},{32,48},{48,0},{1,17},{17,33},{33,49},{49,1},{2,18}... | collective-permute-start | bytes 786440 | tf_op jit(solution)/shard_map/ppermute | solution.py:240
  2.2 16.9 %collective-permute-start.1 = (bf16[512,256]{1,0:T(8,128)(2,1)}, bf16[512,256]{1,0:T(8,128)(2,1)S(1)}, u32[]{:S(2)}, u32[]{:S(2)}) collective-permute-start(bf16[512,256]{1,0:T(8,128)(2,1)} %refs_0_.5), channel_id=1, source_target_pairs={{0,48},{16,0},{32,16},{48,32},{1,49},{17,1},{33,17},{49,33},{2,50}... | collective-permute-start | bytes 786440 | tf_op jit(solution)/shard_map/ppermute | solution.py:240
  5.5 28.4 %all-to-all-start = ((bf16[32,16,512]{2,1,0:T(8,128)(2,1)}), bf16[32,16,512]{2,1,0:T(8,128)(2,1)S(1)}, u32[]{:S(2)}, u32[]{:S(2)}) async-start(bf16[32,16,512]{2,1,0:T(8,128)(2,1)} %pack.1), calls=%async_computation | async-start | bytes 1048576 | tf_op jit(solution)/shard_map/all_to_all | solution.py:291
  16.9 12.5 %copy-start.1 = (bf16[512,256]{1,0:T(8,128)(2,1)S(1)}, bf16[512,256]{1,0:T(8,128)(2,1)}, u32[]{:S(2)}) copy-start(bf16[512,256]{1,0:T(8,128)(2,1)} %refs_0_.5) | copy-start | bytes 786436
  16.9 25.2 %copy-start = (bf16[512,256]{1,0:T(8,128)(2,1)S(1)}, bf16[512,256]{1,0:T(8,128)(2,1)}, u32[]{:S(2)}) copy-start(bf16[512,256]{1,0:T(8,128)(2,1)} %refs_0_.8) | copy-start | bytes 786436
  16.9 12.9 %collective-permute-start.5 = (bf16[512,256]{1,0:T(8,128)(2,1)}, bf16[512,256]{1,0:T(8,128)(2,1)S(1)}, u32[]{:S(2)}, u32[]{:S(2)}) collective-permute-start(bf16[512,256]{1,0:T(8,128)(2,1)} %refs_0_.8), channel_id=1, source_target_pairs={{0,48},{16,0},{32,16},{48,32},{1,49},{17,1},{33,17},{49,33},{2,50}... | collective-permute-start | bytes 786440 | tf_op jit(solution)/shard_map/ppermute | solution.py:240
  18.6 11.3 %collective-permute-start.4 = (bf16[512,256]{1,0:T(8,128)(2,1)}, bf16[512,256]{1,0:T(8,128)(2,1)S(1)}, u32[]{:S(2)}, u32[]{:S(2)}) collective-permute-start(bf16[512,256]{1,0:T(8,128)(2,1)} %refs_0_.8), channel_id=1, source_target_pairs={{0,16},{16,32},{32,48},{48,0},{1,17},{17,33},{33,49},{49,1},{2,18}... | collective-permute-start | bytes 786440 | tf_op jit(solution)/shard_map/ppermute | solution.py:240
  19.1 10.4 %collective-permute-start.2 = (bf16[256,256]{1,0:T(8,128)(2,1)S(1)}, bf16[256,256]{1,0:T(8,128)(2,1)S(1)}, u32[]{:S(2)}, u32[]{:S(2)}) collective-permute-start(bf16[256,256]{1,0:T(8,128)(2,1)S(1)} %get-tuple-element.47), channel_id=1, source_target_pairs={{0,16},{16,32},{32,48},{48,0},{1,17},{17,33},{33,49},{49,1},{2,18}... | collective-permute-start | bytes 393224 | tf_op jit(solution)/shard_map/ppermute | solution.py:240
  19.4 10.0 %collective-permute-start.3 = (bf16[256,256]{1,0:T(8,128)(2,1)S(1)}, bf16[256,256]{1,0:T(8,128)(2,1)S(1)}, u32[]{:S(2)}, u32[]{:S(2)}) collective-permute-start(bf16[256,256]{1,0:T(8,128)(2,1)S(1)} %get-tuple-element.48), channel_id=1, source_target_pairs={{0,48},{16,0},{32,16},{48,32},{1,49},{17,1},{33,17},{49,33},{2,50}... | collective-permute-start | bytes 393224 | tf_op jit(solution)/shard_map/ppermute | solution.py:240
  34.0 3.3 %collective-permute-start.6 = (bf16[512,512]{1,0:T(8,128)(2,1)S(1)}, bf16[512,512]{1,0:T(8,128)(2,1)S(1)}, u32[]{:S(2)}, u32[]{:S(2)}) collective-permute-start(bf16[512,512]{1,0:T(8,128)(2,1)S(1)} %bitcast.1), channel_id=1, source_target_pairs={{0,1},{1,0},{2,3},{3,2},{4,5},{5,4},{6,7},{7,6},{8,9},{9,8},{10,11... | collective-permute-start | bytes 1572872 | tf_op jit(solution)/shard_map/ppermute | solution.py:240
  34.0 8.1 %collective-permute-start.8 = (bf16[256,256]{1,0:T(8,128)(2,1)S(1)}, bf16[256,256]{1,0:T(8,128)(2,1)S(1)}, u32[]{:S(2)}, u32[]{:S(2)}) collective-permute-start(bf16[256,256]{1,0:T(8,128)(2,1)S(1)} %get-tuple-element.55), channel_id=1, source_target_pairs={{0,16},{16,32},{32,48},{48,0},{1,17},{17,33},{33,49},{49,1},{2,18}... | collective-permute-start | bytes 393224 | tf_op jit(solution)/shard_map/ppermute | solution.py:240
  34.4 7.8 %collective-permute-start.9 = (bf16[256,256]{1,0:T(8,128)(2,1)S(1)}, bf16[256,256]{1,0:T(8,128)(2,1)S(1)}, u32[]{:S(2)}, u32[]{:S(2)}) collective-permute-start(bf16[256,256]{1,0:T(8,128)(2,1)S(1)} %get-tuple-element.56), channel_id=1, source_target_pairs={{0,48},{16,0},{32,16},{48,32},{1,49},{17,1},{33,17},{49,33},{2,50}... | collective-permute-start | bytes 393224 | tf_op jit(solution)/shard_map/ppermute | solution.py:240
  39.5 3.7 %collective-permute-start.7 = (f32[4,512]{1,0:T(4,128)S(1)}, f32[4,512]{1,0:T(4,128)S(1)}, u32[]{:S(2)}, u32[]{:S(2)}) collective-permute-start(f32[4,512]{1,0:T(4,128)S(1)} %get-tuple-element.53), channel_id=1, source_target_pairs={{0,48},{16,0},{32,16},{48,32},{1,49},{17,1},{33,17},{49,33},{2,50}... | collective-permute-start | bytes 24584 | tf_op jit(solution)/shard_map/ppermute | solution.py:240
  39.8 4.9 %collective-permute-start.10 = (f32[4,512]{1,0:T(4,128)S(1)}, f32[4,512]{1,0:T(4,128)S(1)}, u32[]{:S(2)}, u32[]{:S(2)}) collective-permute-start(f32[4,512]{1,0:T(4,128)S(1)} %get-tuple-element.61), channel_id=1, source_target_pairs={{0,16},{16,32},{32,48},{48,0},{1,17},{17,33},{33,49},{49,1},{2,18}... | collective-permute-start | bytes 24584 | tf_op jit(solution)/shard_map/ppermute | solution.py:240
  41.5 5.2 %collective-permute-start.11 = (f32[4,512]{1,0:T(4,128)S(1)}, f32[4,512]{1,0:T(4,128)S(1)}, u32[]{:S(2)}, u32[]{:S(2)}) collective-permute-start(f32[4,512]{1,0:T(4,128)S(1)} %get-tuple-element.62), channel_id=1, source_target_pairs={{0,32},{16,48},{32,0},{48,16},{1,33},{17,49},{33,1},{49,17},{2,34}... | collective-permute-start | bytes 24584 | tf_op jit(solution)/shard_map/ppermute | solution.py:240
  47.4 1.2 collective-permute-start.12
  65.0 4.9 %collective-permute-start.13 = (f32[4,512]{1,0:T(4,128)S(1)}, f32[4,512]{1,0:T(4,128)S(1)}, u32[]{:S(2)}, u32[]{:S(2)}) collective-permute-start(f32[4,512]{1,0:T(4,128)S(1)} %get-tuple-element.67), channel_id=1, source_target_pairs={{0,16},{16,32},{32,48},{48,0},{1,17},{17,33},{33,49},{49,1},{2,18}... | collective-permute-start | bytes 24584 | tf_op jit(solution)/shard_map/ppermute | solution.py:240
  65.1 5.2 %collective-permute-start.14 = (f32[4,512]{1,0:T(4,128)S(1)}, f32[4,512]{1,0:T(4,128)S(1)}, u32[]{:S(2)}, u32[]{:S(2)}) collective-permute-start(f32[4,512]{1,0:T(4,128)S(1)} %get-tuple-element.68), channel_id=1, source_target_pairs={{0,32},{16,48},{32,0},{48,16},{1,33},{17,49},{33,1},{49,17},{2,34}... | collective-permute-start | bytes 24584 | tf_op jit(solution)/shard_map/ppermute | solution.py:240
  67.7 3.7 %collective-permute-start.15 = (f32[4,512]{1,0:T(4,128)S(1)}, f32[4,512]{1,0:T(4,128)S(1)}, u32[]{:S(2)}, u32[]{:S(2)}) collective-permute-start(f32[4,512]{1,0:T(4,128)S(1)} %get-tuple-element.69), channel_id=1, source_target_pairs={{0,48},{16,0},{32,16},{48,32},{1,49},{17,1},{33,17},{49,33},{2,50}... | collective-permute-start | bytes 24584 | tf_op jit(solution)/shard_map/ppermute | solution.py:240
  72.1 1.2 collective-permute-start.16
  88.2 6.3 %collective-permute-start.17 = (f32[4,512]{1,0:T(4,128)S(1)}, f32[4,512]{1,0:T(4,128)S(1)}, u32[]{:S(2)}, u32[]{:S(2)}) collective-permute-start(f32[4,512]{1,0:T(4,128)S(1)} %get-tuple-element.73), channel_id=1, source_target_pairs={{0,16},{16,32},{32,48},{48,0},{1,17},{17,33},{33,49},{49,1},{2,18}... | collective-permute-start | bytes 24584 | tf_op jit(solution)/shard_map/ppermute | solution.py:240
  89.7 5.2 %collective-permute-start.18 = (f32[4,512]{1,0:T(4,128)S(1)}, f32[4,512]{1,0:T(4,128)S(1)}, u32[]{:S(2)}, u32[]{:S(2)}) collective-permute-start(f32[4,512]{1,0:T(4,128)S(1)} %get-tuple-element.74), channel_id=1, source_target_pairs={{0,32},{16,48},{32,0},{48,16},{1,33},{17,49},{33,1},{49,17},{2,34}... | collective-permute-start | bytes 24584 | tf_op jit(solution)/shard_map/ppermute | solution.py:240
  91.8 3.7 %collective-permute-start.19 = (f32[4,512]{1,0:T(4,128)S(1)}, f32[4,512]{1,0:T(4,128)S(1)}, u32[]{:S(2)}, u32[]{:S(2)}) collective-permute-start(f32[4,512]{1,0:T(4,128)S(1)} %get-tuple-element.75), channel_id=1, source_target_pairs={{0,48},{16,0},{32,16},{48,32},{1,49},{17,1},{33,17},{49,33},{2,50}... | collective-permute-start | bytes 24584 | tf_op jit(solution)/shard_map/ppermute | solution.py:240
  96.1 1.5 %collective-permute-start.20 = (f32[8,128]{1,0:T(8,128)S(1)}, f32[8,128]{1,0:T(8,128)S(1)}, u32[]{:S(2)}, u32[]{:S(2)}) collective-permute-start(f32[8,128]{1,0:T(8,128)S(1)} %get-tuple-element.79), channel_id=1, source_target_pairs={{0,1},{1,0},{2,3},{3,2},{4,5},{5,4},{6,7},{7,6},{8,9},{9,8},{10,11... | collective-permute-start | bytes 12296 | tf_op jit(solution)/shard_map/ppermute | solution.py:240
  111.8 1.4 collective-permute-start.21
  114.5 5.3 %collective-permute-start.22 = (f32[512,256]{1,0:T(8,128)S(1)}, f32[512,256]{1,0:T(8,128)S(1)}, u32[]{:S(2)}, u32[]{:S(2)}) collective-permute-start(f32[512,256]{1,0:T(8,128)S(1)} %get-tuple-element.85), channel_id=1, source_target_pairs={{0,1},{1,0},{2,3},{3,2},{4,5},{5,4},{6,7},{7,6},{8,9},{9,8},{10,11... | collective-permute-start | bytes 1572872 | tf_op jit(solution)/shard_map/ppermute | solution.py:240
  116.5 9.5 %collective-permute-start.23 = (f32[256,256]{1,0:T(8,128)S(1)}, f32[256,256]{1,0:T(8,128)S(1)}, u32[]{:S(2)}, u32[]{:S(2)}) collective-permute-start(f32[256,256]{1,0:T(8,128)S(1)} %get-tuple-element.88), channel_id=1, source_target_pairs={{0,16},{16,32},{32,48},{48,0},{1,17},{17,33},{33,49},{49,1},{2,18}... | collective-permute-start | bytes 786440 | tf_op jit(solution)/shard_map/ppermute | solution.py:240
  117.1 8.9 %collective-permute-start.24 = (f32[256,256]{1,0:T(8,128)S(1)}, f32[256,256]{1,0:T(8,128)S(1)}, u32[]{:S(2)}, u32[]{:S(2)}) collective-permute-start(f32[256,256]{1,0:T(8,128)S(1)} %get-tuple-element.89), channel_id=1, source_target_pairs={{0,48},{16,0},{32,16},{48,32},{1,49},{17,1},{33,17},{49,33},{2,50}... | collective-permute-start | bytes 786440 | tf_op jit(solution)/shard_map/ppermute | solution.py:240
  120.7 22.0 %all-to-all-start.4 = ((f32[32,16,256]{2,1,0:T(8,128)}), f32[32,16,256]{2,1,0:T(8,128)S(1)}, u32[]{:S(2)}, u32[]{:S(2)}) async-start(f32[32,16,256]{2,1,0:T(8,128)} %pair.1), calls=%async_computation.4 | async-start | bytes 1048576 | tf_op jit(solution)/shard_map/all_to_all | solution.py:363
  126.0 16.7 %copy-start.2 = (bf16[16,256]{1,0:T(8,128)(2,1)S(1)}, bf16[16,256]{1,0:T(8,128)(2,1)}, u32[]{:S(2)}) copy-start(bf16[16,256]{1,0:T(8,128)(2,1)} %refs_0_.7) | copy-start | bytes 24580
  126.1 14.3 %collective-permute-start.25 = (f32[512,256]{1,0:T(8,128)S(1)}, f32[512,256]{1,0:T(8,128)S(1)}, u32[]{:S(2)}, u32[]{:S(2)}) collective-permute-start(f32[512,256]{1,0:T(8,128)S(1)} %get-tuple-element.90), channel_id=1, source_target_pairs={{0,16},{16,32},{32,48},{48,0},{1,17},{17,33},{33,49},{49,1},{2,18}... | collective-permute-start | bytes 1572872 | tf_op jit(solution)/shard_map/ppermute | solution.py:240
  126.2 14.2 %collective-permute-start.26 = (f32[512,256]{1,0:T(8,128)S(1)}, f32[512,256]{1,0:T(8,128)S(1)}, u32[]{:S(2)}, u32[]{:S(2)}) collective-permute-start(f32[512,256]{1,0:T(8,128)S(1)} %get-tuple-element.91), channel_id=1, source_target_pairs={{0,48},{16,0},{32,16},{48,32},{1,49},{17,1},{33,17},{49,33},{2,50}... | collective-permute-start | bytes 1572872 | tf_op jit(solution)/shard_map/ppermute | solution.py:240

commit v6 on v5

--- a/solution.py
+++ b/solution.py
@@ -101,17 +101,33 @@
     return lax.dot_general(rows, weights, (((1,), (1,)), ((), ())), preferred_element_type=f32)
 
 
-def teacher_kernel(own, sib, weight_ref, exp_ref, m0, m1, m2, m3, feat_ref):
-    load_features(0, own, sib, feat_ref)
+def teacher_masses(raw, weight_ref, exp_ref, feat_ref, before):
+    feat_ref[...] = unit(raw[:, : feat_ref.shape[1]])
     rows, block = feat_ref.shape[0], weight_ref.shape[0] // STEPS
     for k in range(STEPS):
         cols = slice(k * block, (k + 1) * block)
-        total = jnp.zeros((8, block), f32)
+        total = before(k)
         for at in range(0, rows, TILE):
             r = slice(at, at + TILE)
             part = jnp.exp(scores(feat_ref[r, :], weight_ref[cols, :]) * (1.0 / TEACHER_TEMP))
             exp_ref[r, cols] = part
             total = total + jnp.sum(part.reshape(TILE // 8, 8, block), axis=0)
+        yield k, cols, total
+
+
+def teacher_own_kernel(own, weight_ref, exp_ref, mass_ref, feat_ref):
+    zero = jnp.zeros((8, weight_ref.shape[0] // STEPS), f32)
+    for k, cols, total in teacher_masses(own, weight_ref, exp_ref, feat_ref, lambda unused: zero):
+        mass_ref[:, cols] = total
+
+
+def teacher_sib_kernel(sib, weight_ref, mass_ref, exp_ref, m0, m1, m2, m3, feat_ref):
+    block = weight_ref.shape[0] // STEPS
+
+    def before(k):
+        return mass_ref[:, k * block : (k + 1) * block]
+
+    for k, cols, total in teacher_masses(sib, weight_ref, exp_ref, feat_ref, before):
         store_rolled((m0, m1, m2, m3), k, jnp.sum(total, axis=0, keepdims=True))
 
 
@@ -131,39 +147,40 @@
             sum_ref[i : i + 1, :] = row_of_sums(total[t * LANES : (t + 1) * LANES])
 
 
-def column_kernel(exp_ref, mass_ref, m0, m1, m2, m3):
+def column_kernel(exp_own, exp_sib, mass_ref, m0, m1, m2, m3):
     scale = 1.0 / jnp.sum(mass_ref[...], axis=0)
-    rows, cols = exp_ref.shape
+    rows, cols = exp_own.shape
     block = cols // STEPS
     wide = 2 * block
     for h in range(cols // wide):
         total = jnp.zeros((8, wide), f32)
-        for i in range(rows // LANES):
+        for i in range(2 * rows // LANES):
+            exp_ref, first = (exp_own, exp_sib)[i * LANES // rows], i * LANES % rows
             col = column(scale[i : i + 1, :])
             for j in range(0, LANES, 8):
-                at = i * LANES + j
                 factor = jnp.concatenate([col[j : j + 8, :]] * (wide // LANES), axis=1)
+                at = first + j
                 total = total + exp_ref[at : at + 8, h * wide : (h + 1) * wide] * factor
         whole = jnp.sum(total, axis=0, keepdims=True)
         for b in range(2):
             store_rolled((m0, m1, m2, m3), 2 * h + b, whole[:, b * block : (b + 1) * block])
 
 
-def row_kernel(exp_ref, m0, m1, m2, m3, *refs):
+def row_kernel(exp_own, exp_sib, m0, m1, m2, m3, *refs):
     extra, (out_ref, swap_ref, scale_ref) = refs[:-3], refs[-3:]
     scale = 1.0 / (m0[...] + m1[...] + m2[...] + m3[...])
     scale_ref[...] = scale
-    rows, cols = exp_ref.shape
+    rows, cols = exp_own.shape
     block = cols // STEPS
-    count = rows // LANES
-    for i in range(count):
+    half = rows // LANES
+    for i in range(2 * half):
+        exp_ref, first = (exp_own, exp_sib)[i // half], i % half * LANES
         total = jnp.zeros((LANES, LANES), f32)
         for at in range(0, cols, LANES):
             k, o = at // block, at % block
-            r = slice(i * LANES, (i + 1) * LANES)
+            r = slice(first, first + LANES)
             total = total + exp_ref[r, at : at + LANES] * scale[k : k + 1, o : o + LANES]
         out_ref[i : i + 1, :] = row_of_sums(total)
-    half = count // 2
     swap_ref[:half, :] = out_ref[half:, :]
     swap_ref[half:, :] = out_ref[:half, :]
     for ref in extra:
@@ -186,38 +203,51 @@
         for at in range(0, cols, LANES):
             k, o = at // block, at % block
             c = slice(at, at + LANES)
-            target = exp_t[e, c] * scale_ref[k : k + 1, o : o + LANES] * row
+            target = exp_t[r, c] * scale_ref[k : k + 1, o : o + LANES] * row
             grad_ref[r, c] = (exp_s[e, c] * total - target).astype(bf16)
     feat_out[...] = jnp.dot(grad_ref[...], weight_ref[...], preferred_element_type=f32)
 
 
-def weights_kernel(grad_own, grad_sib, feat_ref, *outs):
-    half = grad_own.shape[0]
-    at = 0
-    for out in outs:
-        size = out.shape[0]
+def weights_kernel(
+    grad_own, grad_sib, feat_ref, mine, forward, back, forward_last, back_last
+):
+    half = mine.shape[0] // 2
+    few = forward.shape[0] - half
+    whole = slice(0, half)
+    places = (
+        ((mine, 0, whole),),
+        ((mine, half, whole),),
+        ((back, half, slice(0, few)), (back_last, half, slice(few, half))),
+        ((back_last, 0, whole),),
+        ((forward, 0, whole),),
+        ((back, 0, whole),),
+        ((forward_last, 0, whole),),
+        ((forward, half, slice(0, few)), (forward_last, half, slice(few, half))),
+    )
+    rows = grad_own.shape[0]
+    for k, stores in enumerate(places):
         total = 0.0
-        for grad_ref, first in ((grad_own, 0), (grad_sib, half)):
+        for grad_ref, first in ((grad_own, 0), (grad_sib, rows)):
             total = total + lax.dot_general(
-                grad_ref[:, at : at + size],
-                feat_ref[first : first + half, :],
+                grad_ref[:, k * half : (k + 1) * half],
+                feat_ref[first : first + rows, :],
                 (((0,), (0,)), ((), ())),
                 preferred_element_type=f32,
             )
-        out[...] = total
-        at += size
+        for out, at, taken in stores:
+            part = total[taken]
+            out[at : at + part.shape[0], :] = part
 
 
 def pair_kernel(mine, other, out):
     out[...] = (mine[...] + other[...]).reshape(out.shape)
 
 
-def relay_kernel(forward, back, upper, lower, forward_out, back_out):
-    half = upper.shape[0]
-    forward_out[:half, :] = forward[:half, :] + upper[...]
-    forward_out[half:, :] = forward[half:, :]
-    back_out[:half, :] = back[:half, :]
-    back_out[half:, :] = back[half:, :] + lower[...]
+def relay_kernel(forward, back, before, after, forward_out, back_out):
+    half = (forward.shape[0] + before.shape[0]) // 3
+    for mine, got, out in ((forward, before, forward_out), (back, after, back_out)):
+        out[:half, :] = mine[:half, :] + got[:half, :]
+        out[half:, :] = mine[half:, :]
 
 
 def project(raw, grads):
@@ -231,8 +261,19 @@
     out[...] = project(raw[...], jnp.sum(parts[...], axis=0))
 
 
-def proto_grad_kernel(raw, mine, before, after, out):
-    out[...] = project(raw[...], mine[...] + before[...] + after[...])
+def proto_grad_kernel(raw, mine, before, after, before_last, after_last, out):
+    half = out.shape[0] // 2
+    few = before.shape[0] - half
+    places = (
+        (0, few, before_last, 0, after, half),
+        (few, half - few, before_last, few, after_last, half),
+        (half, few, after_last, 0, before, half),
+        (half + few, half - few, after_last, few, before_last, half),
+    )
+    for at, size, one, i, two, j in places:
+        r = slice(at, at + size)
+        sums = mine[r, :] + one[i : i + size, :] + two[j : j + size, :]
+        out[r, :] = project(raw[r, :], sums)
 
 
 def shift(values, axis, step):
@@ -257,11 +298,7 @@
 
 
 def share(blocks):
-    return [blocks[0]] + [shift(blocks[k], "x", k) for k in range(1, STEPS)]
-
-
-def share_rows(mine, swapped):
-    return spread(mine + shift(swapped, "core", 1))
+    return [blocks[0]] + [shift(blocks[k], "x", k) for k in (2, 3, 1)]
 
 
 def body(student_rows, teacher_rows, student_protos, teacher_protos):
@@ -299,14 +336,25 @@
     student_weight = call(unit_kernel, weights, student_blocks, 0, "student_units")
     sib = shift(own, "core", 1)
 
-    exp_t, *mass = call(
-        teacher_kernel, [exps] + masses + [feats], (own, sib, teacher_weight), work, "teacher"
-    )
-    mass = share(mass[:STEPS])
-    mass[3], student_weight = lax.optimization_barrier((mass[3], student_weight))
-    exp_s, student_sums, student_feat = call(
-        student_kernel, [exps, sums, feats], (own, sib, student_weight), work, "student"
-    )
+    half = rows // 2
+    half_exps, half_feats = pltpu.VMEM((half, cols), f32), [pltpu.VMEM((half, width), bf16)]
+    exp_own, mass = call(
+        teacher_own_kernel,
+        [half_exps, jax.ShapeDtypeStruct((8, cols), f32)],
+        (own, teacher_weight),
+        work // 2,
+        "teacher_own",
+        half_feats,
+    )
+    exp_sib, *mass = call(
+        teacher_sib_kernel,
+        [half_exps] + masses,
+        (sib, teacher_weight, mass),
+        work // 2,
+        "teacher_sib",
+        half_feats,
+    )
+    mass = share(mass)
     for sweep in range(SWEEPS):
         last = sweep + 1 == SWEEPS
         extra = (student_sums,) if last else ()
@@ -314,15 +362,20 @@
         mine, swapped, scale = call(
             row_kernel,
             [out, out, masses[0]],
-            (exp_t, *mass, *extra),
+            (exp_own, exp_sib, *mass, *extra),
             work // 8,
             "rows",
         )
-        row_masses = share_rows(mine, swapped)
+        row_masses = mine + shift(swapped, "core", 1)
+        if sweep == 0:
+            row_masses, student_weight = lax.optimization_barrier((row_masses, student_weight))
+            exp_s, student_sums, student_feat = call(
+                student_kernel, [exps, sums, feats], (own, sib, student_weight), work, "student"
+            )
+        row_masses = spread(row_masses)
         if not last:
-            mass = share(call(column_kernel, masses, (exp_t, row_masses), work // 8, "columns"))
-
-    half = rows // 2
+            mass = share(call(column_kernel, masses, (exp_own, exp_sib, row_masses), work // 8, "columns"))
+
     inverse = call(
         functools.partial(scale_kernel, factor),
         jax.ShapeDtypeStruct((rows // LANES, LANES), f32),
@@ -330,7 +383,7 @@
         0,
         "scales",
     )
-    def logits(first, scales, after):
+    def logits(first, exp_t, scales, after):
         return call(
             functools.partial(logits_kernel, first),
             [pltpu.VMEM((half, cols), bf16), jax.ShapeDtypeStruct((half, width), f32)],
@@ -340,13 +393,14 @@
             after=after,
         )
 
-    own_grads, own_feat = logits(0, inverse, ())
-    sib_grads, sib_feat = logits(half, shift(inverse, "core", 1), (own_feat,))
+    own_grads, own_feat = logits(0, exp_own, inverse, ())
+    sib_grads, sib_feat = logits(half, exp_sib, shift(inverse, "core", 1), (own_feat,))
+    pre, post = own_protos * 5 // 8, own_protos * (12 - 5) // 8
     weight_parts = call(
         weights_kernel,
         [
             jax.ShapeDtypeStruct((size, width), f32)
-            for size in (own_protos, own_protos, own_protos // 2, own_protos // 2, own_protos)
+            for size in (own_protos, pre, pre, post, post)
         ],
         (own_grads, sib_grads, student_feat),
         work,
@@ -361,18 +415,20 @@
         after=weight_parts[:1],
     )
     feat_share = lax.all_to_all(feat_pair, ROWS, 0, 0, tiled=True)
-    own_part, back_part, upper_part, lower_part, forward_part = weight_parts
-    forward_part, back_part = call(
+    own_part, forward_part, back_part, forward_last, back_last = weight_parts
+    before, after = shift(forward_part, "x", 1), shift(back_part, "x", -1)
+    forward_last, back_last = call(
         relay_kernel,
-        [jax.ShapeDtypeStruct((own_protos, width), f32)] * 2,
-        (forward_part, back_part, shift(upper_part, "x", 1), shift(lower_part, "x", -1)),
+        [jax.ShapeDtypeStruct(forward_last.shape, f32)] * 2,
+        (forward_last, back_last, before, after),
         100 * work,
         "relay",
     )
+    last = (shift(forward_last, "x", 1), shift(back_last, "x", -1))
     proto_grad = call(
         proto_grad_kernel,
         jax.ShapeDtypeStruct((own_protos, width), f32),
-        (student_protos, own_part, shift(forward_part, "x", 1), shift(back_part, "x", -1)),
+        (student_protos, own_part, before, after, *last),
         0,
         "proto_grad",
     )

time: 144 us -> 143 us (level)
    ppermute x27, waiting for transfers between devices: 30.6 us -> 32.1 us  [shift(): lax.ppermute(values, axis, [(i, (i + step) % size) for i in range(size)])]
    pallas_call x20 -> x21, Pallas kernels: 17 us -> 16.4 us  [call(): pl.pallas_call(lambda *refs: kernel(*refs[count:]), out_shape=outs, in_sp...]
  transfers between devices with their start and end apart: 29 -> 29, of which waited for: 16 -> 13; matrix products, arithmetic and copies ran while one was open for 0% -> 0% of each run, Pallas kernels for 8% -> 8%
where the time goes in v6:
time: 143 us
  starting transfers between devices  44.3 us (31%)
  blocking collectives  43.8 us (31%)
  waiting for transfers between devices  37.4 us (26%)
  Pallas kernels  16.4 us (11%)
    all_to_all x3, blocking collectives, spread(): lax.all_to_all(jnp.broadcast_to(values[None], (count,) + values.shape), R...  43.8 us
    ppermute x27, waiting for transfers between devices, shift(): lax.ppermute(values, axis, [(i, (i + step) % size) for i in range(size)])  32.1 us
    ppermute x27, starting transfers between devices, shift(): lax.ppermute(values, axis, [(i, (i + step) % size) for i in range(size)])  28.5 us
    pallas_call x21, Pallas kernels, call(): pl.pallas_call(lambda *refs: kernel(*refs[count:]), out_shape=outs, in_sp...  16.4 us
    all_to_all x1, starting transfers between devices, body(): own = lax.all_to_all(packed, ROWS, 0, 0, tiled=True).reshape(-1, 2 * width)  11.4 us
    all_to_all x1, starting transfers between devices, body(): feat_share = lax.all_to_all(feat_pair, ROWS, 0, 0, tiled=True)  4.37 us
    all_to_all x1, waiting for transfers between devices, body(): own = lax.all_to_all(packed, ROWS, 0, 0, tiled=True).reshape(-1, 2 * width)  4.12 us
  transfers between devices with their start and end apart: 29, of which 13 were waited for; matrix products, arithmetic and copies ran while one was open for 0% of the time, Pallas kernels for 8%

profile of v6, /device:TPU:32, one launch (start us, length us, event | category | flops | bytes accessed | tf_op | source)
XLA Modules:
  0.0 142.9 jit_solution(6329748672234529471)
XLA Ops:
  0.6 1.6 %collective-permute-start = (bf16[512,256]{1,0:T(8,128)(2,1)}, bf16[512,256]{1,0:T(8,128)(2,1)S(1)}, u32[]{:S(2)}, u32[]{:S(2)}) collective-permute-start(bf16[512,256]{1,0:T(8,128)(2,1)} %refs_0_.5), channel_id=1, source_target_pairs={{0,16},{16,32},{32,48},{48,0},{1,17},{17,33},{33,49},{49,1},{2,18}... | collective-permute-start | bytes 786440 | tf_op jit(solution)/shard_map/ppermute | solution.py:281
  2.2 1.7 %collective-permute-start.1 = (bf16[512,256]{1,0:T(8,128)(2,1)}, bf16[512,256]{1,0:T(8,128)(2,1)S(1)}, u32[]{:S(2)}, u32[]{:S(2)}) collective-permute-start(bf16[512,256]{1,0:T(8,128)(2,1)} %refs_0_.5), channel_id=1, source_target_pairs={{0,48},{16,0},{32,16},{48,32},{1,49},{17,1},{33,17},{49,33},{2,50}... | collective-permute-start | bytes 786440 | tf_op jit(solution)/shard_map/ppermute | solution.py:281
  3.9 1.6 %pack.1 = bf16[32,16,512]{2,1,0:T(8,128)(2,1)} custom-call(bf16[16,256]{1,0:T(8,128)(2,1)} %refs_0_.4, bf16[16,256]{1,0:T(8,128)(2,1)} %refs_0_.7), custom_call_target="tpu_custom_call" | custom-call | bytes 1048576 | tf_op jit(solution)/shard_map/pack/pallas_call | solution.py:35
  5.5 11.4 %all-to-all-start = ((bf16[32,16,512]{2,1,0:T(8,128)(2,1)}), bf16[32,16,512]{2,1,0:T(8,128)(2,1)S(1)}, u32[]{:S(2)}, u32[]{:S(2)}) async-start(bf16[32,16,512]{2,1,0:T(8,128)(2,1)} %pack.1), calls=%async_computation | async-start | bytes 1048576 | tf_op jit(solution)/shard_map/all_to_all | solution.py:328
  16.9 0.0 copy-start.2
  16.9 1.6 %collective-permute-start.5 = (bf16[512,256]{1,0:T(8,128)(2,1)}, bf16[512,256]{1,0:T(8,128)(2,1)S(1)}, u32[]{:S(2)}, u32[]{:S(2)}) collective-permute-start(bf16[512,256]{1,0:T(8,128)(2,1)} %refs_0_.8), channel_id=1, source_target_pairs={{0,48},{16,0},{32,16},{48,32},{1,49},{17,1},{33,17},{49,33},{2,50}... | collective-permute-start | bytes 786440 | tf_op jit(solution)/shard_map/ppermute | solution.py:281
  18.6 0.5 collective-permute-start.4
  19.1 0.3 collective-permute-start.2
  19.4 3.0 %collective-permute-start.3 = (bf16[256,256]{1,0:T(8,128)(2,1)S(1)}, bf16[256,256]{1,0:T(8,128)(2,1)S(1)}, u32[]{:S(2)}, u32[]{:S(2)}) collective-permute-start(bf16[256,256]{1,0:T(8,128)(2,1)S(1)} %get-tuple-element.50), channel_id=1, source_target_pairs={{0,48},{16,0},{32,16},{48,32},{1,49},{17,1},{33,17},{49,33},{2,50}... | collective-permute-start | bytes 393224 | tf_op jit(solution)/shard_map/ppermute | solution.py:281
  22.4 7.0 %collective-permute-done.2.refs_2_ = bf16[256,256]{1,0:T(8,128)(2,1)S(1)} collective-permute-done((bf16[256,256]{1,0:T(8,128)(2,1)S(1)}, bf16[256,256]{1,0:T(8,128)(2,1)S(1)}, u32[]{:S(2)}, u32[]{:S(2)}) %collective-permute-start.2) | collective-permute-done | bytes 131104 | tf_op jit(solution)/shard_map/ppermute | solution.py:281
  29.4 0.4 teacher_units.1.refs_1_
  29.8 4.1 %all-to-all-done = bf16[32,16,512]{2,1,0:T(8,128)(2,1)S(1)} async-done(((bf16[32,16,512]{2,1,0:T(8,128)(2,1)}), bf16[32,16,512]{2,1,0:T(8,128)(2,1)S(1)}, u32[]{:S(2)}, u32[]{:S(2)}) %all-to-all-start) | async-done | bytes 524320 | tf_op jit(solution)/shard_map/all_to_all | solution.py:328
  34.0 0.4 collective-permute-start.11
  34.4 3.0 %collective-permute-start.12 = (bf16[256,256]{1,0:T(8,128)(2,1)S(1)}, bf16[256,256]{1,0:T(8,128)(2,1)S(1)}, u32[]{:S(2)}, u32[]{:S(2)}) collective-permute-start(bf16[256,256]{1,0:T(8,128)(2,1)S(1)} %get-tuple-element.65), channel_id=1, source_target_pairs={{0,48},{16,0},{32,16},{48,32},{1,49},{17,1},{33,17},{49,33},{2,50}... | collective-permute-start | bytes 393224 | tf_op jit(solution)/shard_map/ppermute | solution.py:281
  37.3 0.8 teacher_own.1
  38.1 0.8 teacher_sib.1
  39.0 0.7 collective-permute-start.7
  39.7 1.1 collective-permute-start.8
  40.8 0.9 collective-permute-start.9
  41.7 2.6 %collective-permute-done.7.refs_3_ = f32[4,512]{1,0:T(4,128)S(1)} collective-permute-done((f32[4,512]{1,0:T(4,128)S(1)}, f32[4,512]{1,0:T(4,128)S(1)}, u32[]{:S(2)}, u32[]{:S(2)}) %collective-permute-start.7) | collective-permute-done | bytes 8224 | tf_op jit(solution)/shard_map/ppermute | solution.py:281
  44.3 1.4 collective-permute-done.9.refs_5_
  45.7 0.7 rows.3
  46.4 0.2 collective-permute-start.10
  46.6 0.0 copy-done
  46.6 0.4 student_units.1.refs_2_.refs_4_.refs_5_
  47.0 0.7 collective-permute-done.10
  47.8 15.4 %all_to_all.25.refs_2_ = f32[32,8,128]{2,1,0:T(8,128)S(1)} all-to-all(f32[32,8,128]{2,1,0:T(8,128)S(1)} %broadcast_in_dim.6), channel_id=1, replica_groups=mesh['y'=4,'x'=4,'z'=8,'core'=2] {'y','z'}, dimensions={0} | all-to-all | bytes 262144 | tf_op jit(solution)/shard_map/all_to_all | solution.py:286
  63.2 0.7 columns.2
  63.9 0.8 collective-permute-start.13
  64.8 1.3 collective-permute-start.14
  66.0 0.8 collective-permute-start.15
  66.8 2.4 %collective-permute-done.13.refs_3_ = f32[4,512]{1,0:T(4,128)S(1)} collective-permute-done((f32[4,512]{1,0:T(4,128)S(1)}, f32[4,512]{1,0:T(4,128)S(1)}, u32[]{:S(2)}, u32[]{:S(2)}) %collective-permute-start.13) | collective-permute-done | bytes 8224 | tf_op jit(solution)/shard_map/ppermute | solution.py:281
  69.2 1.7 %collective-permute-done.15.refs_5_ = f32[4,512]{1,0:T(4,128)S(1)} collective-permute-done((f32[4,512]{1,0:T(4,128)S(1)}, f32[4,512]{1,0:T(4,128)S(1)}, u32[]{:S(2)}, u32[]{:S(2)}) %collective-permute-start.15) | collective-permute-done | bytes 8224 | tf_op jit(solution)/shard_map/ppermute | solution.py:281
  70.9 0.7 rows.4
  71.6 1.2 collective-permute-done.16
  72.8 14.2 %all_to_all.26.refs_2_ = f32[32,8,128]{2,1,0:T(8,128)S(1)} all-to-all(f32[32,8,128]{2,1,0:T(8,128)S(1)} %broadcast_in_dim.7), channel_id=1, replica_groups=mesh['y'=4,'x'=4,'z'=8,'core'=2] {'y','z'}, dimensions={0} | all-to-all | bytes 262144 | tf_op jit(solution)/shard_map/all_to_all | solution.py:286
  87.0 0.7 columns.3
  87.7 1.1 collective-permute-start.17
  88.8 1.2 collective-permute-start.18
  90.0 0.8 collective-permute-start.19
  90.9 2.1 %student.1 = (f32[1024,2048]{1,0:T(8,128)S(1)}, f32[8,128]{1,0:T(8,128)S(1)}, bf16[1024,256]{1,0:T(8,128)(2,1)S(1)}) custom-call(bf16[512,512]{1,0:T(8,128)(2,1)S(1)} %bitcast.3, bf16[512,512]{1,0:T(8,128)(2,1)S(1)} %collective-permute-done.6.refs_0_.refs_1_, bf16[2048,256]{1,0:T(8,128)(2,1)S(1)} %student_units.1.refs_2_.refs_4_.refs_5_), custom_call_target="tpu_custom_call" | custom-call | flops 1073741824 | bytes 1048576 | tf_op jit(solution)/shard_map/student/pallas_call | solution.py:35
  92.9 0.0 collective-permute-done.17.refs_3_
  93.0 1.9 %collective-permute-done.19.refs_5_ = f32[4,512]{1,0:T(4,128)S(1)} collective-permute-done((f32[4,512]{1,0:T(4,128)S(1)}, f32[4,512]{1,0:T(4,128)S(1)}, u32[]{:S(2)}, u32[]{:S(2)}) %collective-permute-start.19) | collective-permute-done | bytes 8224 | tf_op jit(solution)/shard_map/ppermute | solution.py:281
  94.9 0.6 rows.5
  95.5 0.1 collective-permute-start.20
  95.6 1.2 collective-permute-done.20
  96.8 14.2 %all_to_all.27.refs_0_ = f32[32,8,128]{2,1,0:T(8,128)S(1)} all-to-all(f32[32,8,128]{2,1,0:T(8,128)S(1)} %broadcast_in_dim.8), channel_id=1, replica_groups=mesh['y'=4,'x'=4,'z'=8,'core'=2] {'y','z'}, dimensions={0} | all-to-all | bytes 262144 | tf_op jit(solution)/shard_map/all_to_all | solution.py:286
  111.0 0.3 collective-permute-start.21
  111.3 1.3 logits.2
  112.7 1.3 logits.3
  114.0 0.6 collective-permute-start.22
  114.6 1.3 weights.1
  115.9 0.1 collective-permute-start.23
  116.0 3.2 %collective-permute-start.24 = (f32[320,256]{1,0:T(8,128)S(1)}, f32[320,256]{1,0:T(8,128)S(1)}, u32[]{:S(2)}, u32[]{:S(2)}) collective-permute-start(f32[320,256]{1,0:T(8,128)S(1)} %get-tuple-element.91), channel_id=1, source_target_pairs={{0,48},{16,0},{32,16},{48,32},{1,49},{17,1},{33,17},{49,33},{2,50}... | collective-permute-start | bytes 983048 | tf_op jit(solution)/shard_map/ppermute | solution.py:281
  119.2 0.9 pair.1
  120.1 4.4 %all-to-all-start.4 = ((f32[32,16,256]{2,1,0:T(8,128)}), f32[32,16,256]{2,1,0:T(8,128)S(1)}, u32[]{:S(2)}, u32[]{:S(2)}) async-start(f32[32,16,256]{2,1,0:T(8,128)} %pair.1), calls=%async_computation.4 | async-start | bytes 1048576 | tf_op jit(solution)/shard_map/all_to_all | solution.py:417
  124.5 2.4 %collective-permute-done.23.refs_2_ = f32[320,256]{1,0:T(8,128)S(1)} collective-permute-done((f32[320,256]{1,0:T(8,128)S(1)}, f32[320,256]{1,0:T(8,128)S(1)}, u32[]{:S(2)}, u32[]{:S(2)}) %collective-permute-start.23) | collective-permute-done | bytes 327712 | tf_op jit(solution)/shard_map/ppermute | solution.py:281
  126.8 0.1 relay.1
  126.9 0.1 collective-permute-start.25
  127.0 3.2 %collective-permute-start.26 = (f32[448,256]{1,0:T(8,128)S(1)}, f32[448,256]{1,0:T(8,128)S(1)}, u32[]{:S(2)}, u32[]{:S(2)}) collective-permute-start(f32[448,256]{1,0:T(8,128)S(1)} %get-tuple-element.95), channel_id=1, source_target_pairs={{0,48},{16,0},{32,16},{48,32},{1,49},{17,1},{33,17},{49,33},{2,50}... | collective-permute-start | bytes 1376264 | tf_op jit(solution)/shard_map/ppermute | solution.py:281
  130.2 9.6 %collective-permute-done.25.refs_4_ = f32[448,256]{1,0:T(8,128)S(1)} collective-permute-done((f32[448,256]{1,0:T(8,128)S(1)}, f32[448,256]{1,0:T(8,128)S(1)}, u32[]{:S(2)}, u32[]{:S(2)}) %collective-permute-start.25) | collective-permute-done | bytes 458784 | tf_op jit(solution)/shard_map/ppermute | solution.py:281
  139.8 1.0 proto_grad.1
  140.9 1.2 all-to-all-done.4.refs_1_
  142.1 0.8 row_grad.1
  (32 shorter events, 0.2 us)
Async XLA Ops:
  0.6 16.3 %collective-permute-start = (bf16[512,256]{1,0:T(8,128)(2,1)}, bf16[512,256]{1,0:T(8,128)(2,1)S(1)}, u32[]{:S(2)}, u32[]{:S(2)}) collective-permute-start(bf16[512,256]{1,0:T(8,128)(2,1)} %refs_0_.5), channel_id=1, source_target_pairs={{0,16},{16,32},{32,48},{48,0},{1,17},{17,33},{33,49},{49,1},{2,18}... | collective-permute-start | bytes 786440 | tf_op jit(solution)/shard_map/ppermute | solution.py:281
  2.2 16.9 %collective-permute-start.1 = (bf16[512,256]{1,0:T(8,128)(2,1)}, bf16[512,256]{1,0:T(8,128)(2,1)S(1)}, u32[]{:S(2)}, u32[]{:S(2)}) collective-permute-start(bf16[512,256]{1,0:T(8,128)(2,1)} %refs_0_.5), channel_id=1, source_target_pairs={{0,48},{16,0},{32,16},{48,32},{1,49},{17,1},{33,17},{49,33},{2,50}... | collective-permute-start | bytes 786440 | tf_op jit(solution)/shard_map/ppermute | solution.py:281
  5.5 28.4 %all-to-all-start = ((bf16[32,16,512]{2,1,0:T(8,128)(2,1)}), bf16[32,16,512]{2,1,0:T(8,128)(2,1)S(1)}, u32[]{:S(2)}, u32[]{:S(2)}) async-start(bf16[32,16,512]{2,1,0:T(8,128)(2,1)} %pack.1), calls=%async_computation | async-start | bytes 1048576 | tf_op jit(solution)/shard_map/all_to_all | solution.py:328
  16.9 12.5 %copy-start.2 = (bf16[512,256]{1,0:T(8,128)(2,1)S(1)}, bf16[512,256]{1,0:T(8,128)(2,1)}, u32[]{:S(2)}) copy-start(bf16[512,256]{1,0:T(8,128)(2,1)} %refs_0_.5) | copy-start | bytes 786436
  16.9 12.9 %collective-permute-start.5 = (bf16[512,256]{1,0:T(8,128)(2,1)}, bf16[512,256]{1,0:T(8,128)(2,1)S(1)}, u32[]{:S(2)}, u32[]{:S(2)}) collective-permute-start(bf16[512,256]{1,0:T(8,128)(2,1)} %refs_0_.8), channel_id=1, source_target_pairs={{0,48},{16,0},{32,16},{48,32},{1,49},{17,1},{33,17},{49,33},{2,50}... | collective-permute-start | bytes 786440 | tf_op jit(solution)/shard_map/ppermute | solution.py:281
  18.6 11.3 %collective-permute-start.4 = (bf16[512,256]{1,0:T(8,128)(2,1)}, bf16[512,256]{1,0:T(8,128)(2,1)S(1)}, u32[]{:S(2)}, u32[]{:S(2)}) collective-permute-start(bf16[512,256]{1,0:T(8,128)(2,1)} %refs_0_.8), channel_id=1, source_target_pairs={{0,16},{16,32},{32,48},{48,0},{1,17},{17,33},{33,49},{49,1},{2,18}... | collective-permute-start | bytes 786440 | tf_op jit(solution)/shard_map/ppermute | solution.py:281
  19.1 10.4 %collective-permute-start.2 = (bf16[256,256]{1,0:T(8,128)(2,1)S(1)}, bf16[256,256]{1,0:T(8,128)(2,1)S(1)}, u32[]{:S(2)}, u32[]{:S(2)}) collective-permute-start(bf16[256,256]{1,0:T(8,128)(2,1)S(1)} %get-tuple-element.49), channel_id=1, source_target_pairs={{0,16},{16,32},{32,48},{48,0},{1,17},{17,33},{33,49},{49,1},{2,18}... | collective-permute-start | bytes 393224 | tf_op jit(solution)/shard_map/ppermute | solution.py:281
  19.4 10.0 %collective-permute-start.3 = (bf16[256,256]{1,0:T(8,128)(2,1)S(1)}, bf16[256,256]{1,0:T(8,128)(2,1)S(1)}, u32[]{:S(2)}, u32[]{:S(2)}) collective-permute-start(bf16[256,256]{1,0:T(8,128)(2,1)S(1)} %get-tuple-element.50), channel_id=1, source_target_pairs={{0,48},{16,0},{32,16},{48,32},{1,49},{17,1},{33,17},{49,33},{2,50}... | collective-permute-start | bytes 393224 | tf_op jit(solution)/shard_map/ppermute | solution.py:281
  34.0 4.2 %collective-permute-start.6 = (bf16[512,512]{1,0:T(8,128)(2,1)S(1)}, bf16[512,512]{1,0:T(8,128)(2,1)S(1)}, u32[]{:S(2)}, u32[]{:S(2)}) collective-permute-start(bf16[512,512]{1,0:T(8,128)(2,1)S(1)} %bitcast.1), channel_id=1, source_target_pairs={{0,1},{1,0},{2,3},{3,2},{4,5},{5,4},{6,7},{7,6},{8,9},{9,8},{10,11... | collective-permute-start | bytes 1572872 | tf_op jit(solution)/shard_map/ppermute | solution.py:281
  34.0 12.6 %collective-permute-start.11 = (bf16[256,256]{1,0:T(8,128)(2,1)S(1)}, bf16[256,256]{1,0:T(8,128)(2,1)S(1)}, u32[]{:S(2)}, u32[]{:S(2)}) collective-permute-start(bf16[256,256]{1,0:T(8,128)(2,1)S(1)} %get-tuple-element.64), channel_id=1, source_target_pairs={{0,16},{16,32},{32,48},{48,0},{1,17},{17,33},{33,49},{49,1},{2,18}... | collective-permute-start | bytes 393224 | tf_op jit(solution)/shard_map/ppermute | solution.py:281
  34.4 12.3 %collective-permute-start.12 = (bf16[256,256]{1,0:T(8,128)(2,1)S(1)}, bf16[256,256]{1,0:T(8,128)(2,1)S(1)}, u32[]{:S(2)}, u32[]{:S(2)}) collective-permute-start(bf16[256,256]{1,0:T(8,128)(2,1)S(1)} %get-tuple-element.65), channel_id=1, source_target_pairs={{0,48},{16,0},{32,16},{48,32},{1,49},{17,1},{33,17},{49,33},{2,50}... | collective-permute-start | bytes 393224 | tf_op jit(solution)/shard_map/ppermute | solution.py:281
  39.0 5.3 %collective-permute-start.7 = (f32[4,512]{1,0:T(4,128)S(1)}, f32[4,512]{1,0:T(4,128)S(1)}, u32[]{:S(2)}, u32[]{:S(2)}) collective-permute-start(f32[4,512]{1,0:T(4,128)S(1)} %get-tuple-element.58), channel_id=1, source_target_pairs={{0,32},{16,48},{32,0},{48,16},{1,33},{17,49},{33,1},{49,17},{2,34}... | collective-permute-start | bytes 24584 | tf_op jit(solution)/shard_map/ppermute | solution.py:281
  39.7 4.6 %collective-permute-start.8 = (f32[4,512]{1,0:T(4,128)S(1)}, f32[4,512]{1,0:T(4,128)S(1)}, u32[]{:S(2)}, u32[]{:S(2)}) collective-permute-start(f32[4,512]{1,0:T(4,128)S(1)} %get-tuple-element.59), channel_id=1, source_target_pairs={{0,48},{16,0},{32,16},{48,32},{1,49},{17,1},{33,17},{49,33},{2,50}... | collective-permute-start | bytes 24584 | tf_op jit(solution)/shard_map/ppermute | solution.py:281
  40.8 4.9 %collective-permute-start.9 = (f32[4,512]{1,0:T(4,128)S(1)}, f32[4,512]{1,0:T(4,128)S(1)}, u32[]{:S(2)}, u32[]{:S(2)}) collective-permute-start(f32[4,512]{1,0:T(4,128)S(1)} %get-tuple-element.60), channel_id=1, source_target_pairs={{0,16},{16,32},{32,48},{48,0},{1,17},{17,33},{33,49},{49,1},{2,18}... | collective-permute-start | bytes 24584 | tf_op jit(solution)/shard_map/ppermute | solution.py:281
  45.7 1.0 copy-start
  46.4 1.3 collective-permute-start.10
  63.9 5.2 %collective-permute-start.13 = (f32[4,512]{1,0:T(4,128)S(1)}, f32[4,512]{1,0:T(4,128)S(1)}, u32[]{:S(2)}, u32[]{:S(2)}) collective-permute-start(f32[4,512]{1,0:T(4,128)S(1)} %get-tuple-element.71), channel_id=1, source_target_pairs={{0,32},{16,48},{32,0},{48,16},{1,33},{17,49},{33,1},{49,17},{2,34}... | collective-permute-start | bytes 24584 | tf_op jit(solution)/shard_map/ppermute | solution.py:281
  64.8 4.4 %collective-permute-start.14 = (f32[4,512]{1,0:T(4,128)S(1)}, f32[4,512]{1,0:T(4,128)S(1)}, u32[]{:S(2)}, u32[]{:S(2)}) collective-permute-start(f32[4,512]{1,0:T(4,128)S(1)} %get-tuple-element.72), channel_id=1, source_target_pairs={{0,48},{16,0},{32,16},{48,32},{1,49},{17,1},{33,17},{49,33},{2,50}... | collective-permute-start | bytes 24584 | tf_op jit(solution)/shard_map/ppermute | solution.py:281
  66.0 4.9 %collective-permute-start.15 = (f32[4,512]{1,0:T(4,128)S(1)}, f32[4,512]{1,0:T(4,128)S(1)}, u32[]{:S(2)}, u32[]{:S(2)}) collective-permute-start(f32[4,512]{1,0:T(4,128)S(1)} %get-tuple-element.73), channel_id=1, source_target_pairs={{0,16},{16,32},{32,48},{48,0},{1,17},{17,33},{33,49},{49,1},{2,18}... | collective-permute-start | bytes 24584 | tf_op jit(solution)/shard_map/ppermute | solution.py:281
  71.6 1.2 collective-permute-start.16
  87.7 5.2 %collective-permute-start.17 = (f32[4,512]{1,0:T(4,128)S(1)}, f32[4,512]{1,0:T(4,128)S(1)}, u32[]{:S(2)}, u32[]{:S(2)}) collective-permute-start(f32[4,512]{1,0:T(4,128)S(1)} %get-tuple-element.77), channel_id=1, source_target_pairs={{0,32},{16,48},{32,0},{48,16},{1,33},{17,49},{33,1},{49,17},{2,34}... | collective-permute-start | bytes 24584 | tf_op jit(solution)/shard_map/ppermute | solution.py:281
  88.8 4.1 %collective-permute-start.18 = (f32[4,512]{1,0:T(4,128)S(1)}, f32[4,512]{1,0:T(4,128)S(1)}, u32[]{:S(2)}, u32[]{:S(2)}) collective-permute-start(f32[4,512]{1,0:T(4,128)S(1)} %get-tuple-element.78), channel_id=1, source_target_pairs={{0,48},{16,0},{32,16},{48,32},{1,49},{17,1},{33,17},{49,33},{2,50}... | collective-permute-start | bytes 24584 | tf_op jit(solution)/shard_map/ppermute | solution.py:281
  90.0 4.9 %collective-permute-start.19 = (f32[4,512]{1,0:T(4,128)S(1)}, f32[4,512]{1,0:T(4,128)S(1)}, u32[]{:S(2)}, u32[]{:S(2)}) collective-permute-start(f32[4,512]{1,0:T(4,128)S(1)} %get-tuple-element.79), channel_id=1, source_target_pairs={{0,16},{16,32},{32,48},{48,0},{1,17},{17,33},{33,49},{49,1},{2,18}... | collective-permute-start | bytes 24584 | tf_op jit(solution)/shard_map/ppermute | solution.py:281
  95.5 1.3 collective-permute-start.20
  111.0 1.6 %collective-permute-start.21 = (f32[8,128]{1,0:T(8,128)S(1)}, f32[8,128]{1,0:T(8,128)S(1)}, u32[]{:S(2)}, u32[]{:S(2)}) collective-permute-start(f32[8,128]{1,0:T(8,128)S(1)} %scales.1.refs_3_), channel_id=1, source_target_pairs={{0,1},{1,0},{2,3},{3,2},{4,5},{5,4},{6,7},{7,6},{8,9},{9,8},{10,11... | collective-permute-start | bytes 12296 | tf_op jit(solution)/shard_map/ppermute | solution.py:281
  114.0 5.2 %collective-permute-start.22 = (f32[512,256]{1,0:T(8,128)S(1)}, f32[512,256]{1,0:T(8,128)S(1)}, u32[]{:S(2)}, u32[]{:S(2)}) collective-permute-start(f32[512,256]{1,0:T(8,128)S(1)} %get-tuple-element.89), channel_id=1, source_target_pairs={{0,1},{1,0},{2,3},{3,2},{4,5},{5,4},{6,7},{7,6},{8,9},{9,8},{10,11... | collective-permute-start | bytes 1572872 | tf_op jit(solution)/shard_map/ppermute | solution.py:281
  115.9 10.9 %collective-permute-start.23 = (f32[320,256]{1,0:T(8,128)S(1)}, f32[320,256]{1,0:T(8,128)S(1)}, u32[]{:S(2)}, u32[]{:S(2)}) collective-permute-start(f32[320,256]{1,0:T(8,128)S(1)} %get-tuple-element.90), channel_id=1, source_target_pairs={{0,16},{16,32},{32,48},{48,0},{1,17},{17,33},{33,49},{49,1},{2,18}... | collective-permute-start | bytes 983048 | tf_op jit(solution)/shard_map/ppermute | solution.py:281
  116.0 10.8 %collective-permute-start.24 = (f32[320,256]{1,0:T(8,128)S(1)}, f32[320,256]{1,0:T(8,128)S(1)}, u32[]{:S(2)}, u32[]{:S(2)}) collective-permute-start(f32[320,256]{1,0:T(8,128)S(1)} %get-tuple-element.91), channel_id=1, source_target_pairs={{0,48},{16,0},{32,16},{48,32},{1,49},{17,1},{33,17},{49,33},{2,50}... | collective-permute-start | bytes 983048 | tf_op jit(solution)/shard_map/ppermute | solution.py:281
  120.1 22.0 %all-to-all-start.4 = ((f32[32,16,256]{2,1,0:T(8,128)}), f32[32,16,256]{2,1,0:T(8,128)S(1)}, u32[]{:S(2)}, u32[]{:S(2)}) async-start(f32[32,16,256]{2,1,0:T(8,128)} %pair.1), calls=%async_computation.4 | async-start | bytes 1048576 | tf_op jit(solution)/shard_map/all_to_all | solution.py:417
  126.8 13.0 %copy-start.1 = (bf16[512,256]{1,0:T(8,128)(2,1)S(1)}, bf16[512,256]{1,0:T(8,128)(2,1)}, u32[]{:S(2)}) copy-start(bf16[512,256]{1,0:T(8,128)(2,1)} %refs_0_.8) | copy-start | bytes 786436
  126.8 15.3 %copy-start.3 = (bf16[16,256]{1,0:T(8,128)(2,1)S(1)}, bf16[16,256]{1,0:T(8,128)(2,1)}, u32[]{:S(2)}) copy-start(bf16[16,256]{1,0:T(8,128)(2,1)} %refs_0_.7) | copy-start | bytes 24580
  126.9 12.9 %collective-permute-start.25 = (f32[448,256]{1,0:T(8,128)S(1)}, f32[448,256]{1,0:T(8,128)S(1)}, u32[]{:S(2)}, u32[]{:S(2)}) collective-permute-start(f32[448,256]{1,0:T(8,128)S(1)} %get-tuple-element.94), channel_id=1, source_target_pairs={{0,16},{16,32},{32,48},{48,0},{1,17},{17,33},{33,49},{49,1},{2,18}... | collective-permute-start | bytes 1376264 | tf_op jit(solution)/shard_map/ppermute | solution.py:281
  127.0 12.8 %collective-permute-start.26 = (f32[448,256]{1,0:T(8,128)S(1)}, f32[448,256]{1,0:T(8,128)S(1)}, u32[]{:S(2)}, u32[]{:S(2)}) collective-permute-start(f32[448,256]{1,0:T(8,128)S(1)} %get-tuple-element.95), channel_id=1, source_target_pairs={{0,48},{16,0},{32,16},{48,32},{1,49},{17,1},{33,17},{49,33},{2,50}... | collective-permute-start | bytes 1376264 | tf_op jit(solution)/shard_map/ppermute | solution.py:281

commit v7 on v6

--- a/solution.py
+++ b/solution.py
@@ -375,6 +375,8 @@
         row_masses = spread(row_masses)
         if not last:
             mass = share(call(column_kernel, masses, (exp_own, exp_sib, row_masses), work // 8, "columns"))
+        if sweep == 0:
+            mass[3], student_sums = lax.optimization_barrier((mass[3], student_sums))
 
     inverse = call(
         functools.partial(scale_kernel, factor),

time: 143 us -> 143 us (level)
  no operation moved by 1% of the time
where the time goes in v7:
time: 143 us
  starting transfers between devices  44.3 us (31%)
  blocking collectives  43.8 us (31%)
  waiting for transfers between devices  37.4 us (26%)
  Pallas kernels  16.4 us (11%)
    all_to_all x3, blocking collectives, spread(): lax.all_to_all(jnp.broadcast_to(values[None], (count,) + values.shape), R...  43.8 us
    ppermute x27, waiting for transfers between devices, shift(): lax.ppermute(values, axis, [(i, (i + step) % size) for i in range(size)])  32.1 us
    ppermute x27, starting transfers between devices, shift(): lax.ppermute(values, axis, [(i, (i + step) % size) for i in range(size)])  28.5 us
    pallas_call x21, Pallas kernels, call(): pl.pallas_call(lambda *refs: kernel(*refs[count:]), out_shape=outs, in_sp...  16.4 us
    all_to_all x1, starting transfers between devices, body(): own = lax.all_to_all(packed, ROWS, 0, 0, tiled=True).reshape(-1, 2 * width)  11.4 us
    all_to_all x1, starting transfers between devices, body(): feat_share = lax.all_to_all(feat_pair, ROWS, 0, 0, tiled=True)  4.37 us
    all_to_all x1, waiting for transfers between devices, body(): own = lax.all_to_all(packed, ROWS, 0, 0, tiled=True).reshape(-1, 2 * width)  4.12 us
  transfers between devices with their start and end apart: 29, of which 13 were waited for; matrix products, arithmetic and copies ran while one was open for 0% of the time, Pallas kernels for 8%

profile of v7, /device:TPU:32, one launch (start us, length us, event | category | flops | bytes accessed | tf_op | source)
XLA Modules:
  0.0 142.9 jit_solution(8659831546021698565)
XLA Ops:
  0.6 1.6 %collective-permute-start = (bf16[512,256]{1,0:T(8,128)(2,1)}, bf16[512,256]{1,0:T(8,128)(2,1)S(1)}, u32[]{:S(2)}, u32[]{:S(2)}) collective-permute-start(bf16[512,256]{1,0:T(8,128)(2,1)} %refs_0_.5), channel_id=1, source_target_pairs={{0,16},{16,32},{32,48},{48,0},{1,17},{17,33},{33,49},{49,1},{2,18}... | collective-permute-start | bytes 786440 | tf_op jit(solution)/shard_map/ppermute | solution.py:281
  2.2 1.7 %collective-permute-start.1 = (bf16[512,256]{1,0:T(8,128)(2,1)}, bf16[512,256]{1,0:T(8,128)(2,1)S(1)}, u32[]{:S(2)}, u32[]{:S(2)}) collective-permute-start(bf16[512,256]{1,0:T(8,128)(2,1)} %refs_0_.5), channel_id=1, source_target_pairs={{0,48},{16,0},{32,16},{48,32},{1,49},{17,1},{33,17},{49,33},{2,50}... | collective-permute-start | bytes 786440 | tf_op jit(solution)/shard_map/ppermute | solution.py:281
  3.9 1.6 %pack.1 = bf16[32,16,512]{2,1,0:T(8,128)(2,1)} custom-call(bf16[16,256]{1,0:T(8,128)(2,1)} %refs_0_.4, bf16[16,256]{1,0:T(8,128)(2,1)} %refs_0_.7), custom_call_target="tpu_custom_call" | custom-call | bytes 1048576 | tf_op jit(solution)/shard_map/pack/pallas_call | solution.py:35
  5.5 11.4 %all-to-all-start = ((bf16[32,16,512]{2,1,0:T(8,128)(2,1)}), bf16[32,16,512]{2,1,0:T(8,128)(2,1)S(1)}, u32[]{:S(2)}, u32[]{:S(2)}) async-start(bf16[32,16,512]{2,1,0:T(8,128)(2,1)} %pack.1), calls=%async_computation | async-start | bytes 1048576 | tf_op jit(solution)/shard_map/all_to_all | solution.py:328
  16.9 0.0 copy-start.2
  16.9 1.6 %collective-permute-start.5 = (bf16[512,256]{1,0:T(8,128)(2,1)}, bf16[512,256]{1,0:T(8,128)(2,1)S(1)}, u32[]{:S(2)}, u32[]{:S(2)}) collective-permute-start(bf16[512,256]{1,0:T(8,128)(2,1)} %refs_0_.8), channel_id=1, source_target_pairs={{0,48},{16,0},{32,16},{48,32},{1,49},{17,1},{33,17},{49,33},{2,50}... | collective-permute-start | bytes 786440 | tf_op jit(solution)/shard_map/ppermute | solution.py:281
  18.6 0.5 collective-permute-start.4
  19.1 0.0 collective-permute-done.1.refs_1_.refs_4_
  19.1 0.3 collective-permute-start.2
  19.4 3.0 %collective-permute-start.3 = (bf16[256,256]{1,0:T(8,128)(2,1)S(1)}, bf16[256,256]{1,0:T(8,128)(2,1)S(1)}, u32[]{:S(2)}, u32[]{:S(2)}) collective-permute-start(bf16[256,256]{1,0:T(8,128)(2,1)S(1)} %get-tuple-element.52), channel_id=1, source_target_pairs={{0,48},{16,0},{32,16},{48,32},{1,49},{17,1},{33,17},{49,33},{2,50}... | collective-permute-start | bytes 393224 | tf_op jit(solution)/shard_map/ppermute | solution.py:281
  22.4 7.0 %collective-permute-done.2.refs_2_ = bf16[256,256]{1,0:T(8,128)(2,1)S(1)} collective-permute-done((bf16[256,256]{1,0:T(8,128)(2,1)S(1)}, bf16[256,256]{1,0:T(8,128)(2,1)S(1)}, u32[]{:S(2)}, u32[]{:S(2)}) %collective-permute-start.2) | collective-permute-done | bytes 131104 | tf_op jit(solution)/shard_map/ppermute | solution.py:281
  29.4 0.4 teacher_units.1.refs_1_
  29.8 4.1 %all-to-all-done = bf16[32,16,512]{2,1,0:T(8,128)(2,1)S(1)} async-done(((bf16[32,16,512]{2,1,0:T(8,128)(2,1)}), bf16[32,16,512]{2,1,0:T(8,128)(2,1)S(1)}, u32[]{:S(2)}, u32[]{:S(2)}) %all-to-all-start) | async-done | bytes 524320 | tf_op jit(solution)/shard_map/all_to_all | solution.py:328
  34.0 0.4 collective-permute-start.11
  34.4 3.0 %collective-permute-start.12 = (bf16[256,256]{1,0:T(8,128)(2,1)S(1)}, bf16[256,256]{1,0:T(8,128)(2,1)S(1)}, u32[]{:S(2)}, u32[]{:S(2)}) collective-permute-start(bf16[256,256]{1,0:T(8,128)(2,1)S(1)} %get-tuple-element.67), channel_id=1, source_target_pairs={{0,48},{16,0},{32,16},{48,32},{1,49},{17,1},{33,17},{49,33},{2,50}... | collective-permute-start | bytes 393224 | tf_op jit(solution)/shard_map/ppermute | solution.py:281
  37.3 0.8 teacher_own.1
  38.1 0.8 teacher_sib.1
  39.0 0.7 collective-permute-start.7
  39.7 1.1 collective-permute-start.8
  40.8 0.9 collective-permute-start.9
  41.7 2.6 %collective-permute-done.7.refs_3_ = f32[4,512]{1,0:T(4,128)S(1)} collective-permute-done((f32[4,512]{1,0:T(4,128)S(1)}, f32[4,512]{1,0:T(4,128)S(1)}, u32[]{:S(2)}, u32[]{:S(2)}) %collective-permute-start.7) | collective-permute-done | bytes 8224 | tf_op jit(solution)/shard_map/ppermute | solution.py:281
  44.3 1.4 collective-permute-done.9.refs_5_
  45.7 0.7 rows.3
  46.4 0.2 collective-permute-start.10
  46.6 0.0 copy-done
  46.6 0.4 student_units.1.refs_2_.refs_4_.refs_5_
  47.0 0.7 collective-permute-done.10
  47.8 15.4 %all_to_all.25.refs_2_ = f32[32,8,128]{2,1,0:T(8,128)S(1)} all-to-all(f32[32,8,128]{2,1,0:T(8,128)S(1)} %broadcast_in_dim.6), channel_id=1, replica_groups=mesh['y'=4,'x'=4,'z'=8,'core'=2] {'y','z'}, dimensions={0} | all-to-all | bytes 262144 | tf_op jit(solution)/shard_map/all_to_all | solution.py:286
  63.2 0.7 columns.2
  63.9 0.8 collective-permute-start.13
  64.8 1.3 collective-permute-start.14
  66.0 0.8 collective-permute-start.15
  66.8 2.1 %student.1 = (f32[1024,2048]{1,0:T(8,128)S(1)}, f32[8,128]{1,0:T(8,128)S(1)}, bf16[1024,256]{1,0:T(8,128)(2,1)S(1)}) custom-call(bf16[512,512]{1,0:T(8,128)(2,1)S(1)} %bitcast.3, bf16[512,512]{1,0:T(8,128)(2,1)S(1)} %collective-permute-done.6.refs_0_.refs_1_, bf16[2048,256]{1,0:T(8,128)(2,1)S(1)} %student_units.1.refs_2_.refs_4_.refs_5_), custom_call_target="tpu_custom_call" | custom-call | flops 1073741824 | bytes 1048576 | tf_op jit(solution)/shard_map/student/pallas_call | solution.py:35
  68.9 2.0 %collective-permute-done.15.refs_5_ = f32[4,512]{1,0:T(4,128)S(1)} collective-permute-done((f32[4,512]{1,0:T(4,128)S(1)}, f32[4,512]{1,0:T(4,128)S(1)}, u32[]{:S(2)}, u32[]{:S(2)}) %collective-permute-start.15) | collective-permute-done | bytes 8224 | tf_op jit(solution)/shard_map/ppermute | solution.py:281
  70.9 0.7 rows.4
  71.6 1.2 collective-permute-done.16
  72.8 14.2 %all_to_all.26.refs_2_ = f32[32,8,128]{2,1,0:T(8,128)S(1)} all-to-all(f32[32,8,128]{2,1,0:T(8,128)S(1)} %broadcast_in_dim.7), channel_id=1, replica_groups=mesh['y'=4,'x'=4,'z'=8,'core'=2] {'y','z'}, dimensions={0} | all-to-all | bytes 262144 | tf_op jit(solution)/shard_map/all_to_all | solution.py:286
  87.0 0.7 columns.3
  87.7 1.1 collective-permute-start.17
  88.8 1.2 collective-permute-start.18
  90.1 0.8 collective-permute-start.19
  90.9 2.1 %collective-permute-done.17.refs_3_ = f32[4,512]{1,0:T(4,128)S(1)} collective-permute-done((f32[4,512]{1,0:T(4,128)S(1)}, f32[4,512]{1,0:T(4,128)S(1)}, u32[]{:S(2)}, u32[]{:S(2)}) %collective-permute-start.17) | collective-permute-done | bytes 8224 | tf_op jit(solution)/shard_map/ppermute | solution.py:281
  93.0 1.9 %collective-permute-done.19.refs_5_ = f32[4,512]{1,0:T(4,128)S(1)} collective-permute-done((f32[4,512]{1,0:T(4,128)S(1)}, f32[4,512]{1,0:T(4,128)S(1)}, u32[]{:S(2)}, u32[]{:S(2)}) %collective-permute-start.19) | collective-permute-done | bytes 8224 | tf_op jit(solution)/shard_map/ppermute | solution.py:281
  94.9 0.6 rows.5
  95.6 0.1 collective-permute-start.20
  95.7 1.2 collective-permute-done.20
  96.8 14.2 %all_to_all.27.refs_0_ = f32[32,8,128]{2,1,0:T(8,128)S(1)} all-to-all(f32[32,8,128]{2,1,0:T(8,128)S(1)} %broadcast_in_dim.8), channel_id=1, replica_groups=mesh['y'=4,'x'=4,'z'=8,'core'=2] {'y','z'}, dimensions={0} | all-to-all | bytes 262144 | tf_op jit(solution)/shard_map/all_to_all | solution.py:286
  111.0 0.3 collective-permute-start.21
  111.4 1.3 logits.2
  112.7 1.3 logits.3
  114.0 0.6 collective-permute-start.22
  114.6 1.3 weights.1
  115.9 0.1 collective-permute-start.23
  116.0 3.2 %collective-permute-start.24 = (f32[320,256]{1,0:T(8,128)S(1)}, f32[320,256]{1,0:T(8,128)S(1)}, u32[]{:S(2)}, u32[]{:S(2)}) collective-permute-start(f32[320,256]{1,0:T(8,128)S(1)} %get-tuple-element.95), channel_id=1, source_target_pairs={{0,48},{16,0},{32,16},{48,32},{1,49},{17,1},{33,17},{49,33},{2,50}... | collective-permute-start | bytes 983048 | tf_op jit(solution)/shard_map/ppermute | solution.py:281
  119.2 0.9 pair.1
  120.1 4.4 %all-to-all-start.4 = ((f32[32,16,256]{2,1,0:T(8,128)}), f32[32,16,256]{2,1,0:T(8,128)S(1)}, u32[]{:S(2)}, u32[]{:S(2)}) async-start(f32[32,16,256]{2,1,0:T(8,128)} %pair.1), calls=%async_computation.4 | async-start | bytes 1048576 | tf_op jit(solution)/shard_map/all_to_all | solution.py:419
  124.5 2.4 %collective-permute-done.23.refs_2_ = f32[320,256]{1,0:T(8,128)S(1)} collective-permute-done((f32[320,256]{1,0:T(8,128)S(1)}, f32[320,256]{1,0:T(8,128)S(1)}, u32[]{:S(2)}, u32[]{:S(2)}) %collective-permute-start.23) | collective-permute-done | bytes 327712 | tf_op jit(solution)/shard_map/ppermute | solution.py:281
  126.8 0.1 relay.1
  126.9 0.1 collective-permute-start.25
  127.0 3.2 %collective-permute-start.26 = (f32[448,256]{1,0:T(8,128)S(1)}, f32[448,256]{1,0:T(8,128)S(1)}, u32[]{:S(2)}, u32[]{:S(2)}) collective-permute-start(f32[448,256]{1,0:T(8,128)S(1)} %get-tuple-element.99), channel_id=1, source_target_pairs={{0,48},{16,0},{32,16},{48,32},{1,49},{17,1},{33,17},{49,33},{2,50}... | collective-permute-start | bytes 1376264 | tf_op jit(solution)/shard_map/ppermute | solution.py:281
  130.2 9.6 %collective-permute-done.25.refs_4_ = f32[448,256]{1,0:T(8,128)S(1)} collective-permute-done((f32[448,256]{1,0:T(8,128)S(1)}, f32[448,256]{1,0:T(8,128)S(1)}, u32[]{:S(2)}, u32[]{:S(2)}) %collective-permute-start.25) | collective-permute-done | bytes 458784 | tf_op jit(solution)/shard_map/ppermute | solution.py:281
  139.8 1.0 proto_grad.1
  140.9 1.2 all-to-all-done.4.refs_1_
  142.1 0.8 row_grad.1
  (32 shorter events, 0.2 us)
Async XLA Ops:
  0.6 16.3 %collective-permute-start = (bf16[512,256]{1,0:T(8,128)(2,1)}, bf16[512,256]{1,0:T(8,128)(2,1)S(1)}, u32[]{:S(2)}, u32[]{:S(2)}) collective-permute-start(bf16[512,256]{1,0:T(8,128)(2,1)} %refs_0_.5), channel_id=1, source_target_pairs={{0,16},{16,32},{32,48},{48,0},{1,17},{17,33},{33,49},{49,1},{2,18}... | collective-permute-start | bytes 786440 | tf_op jit(solution)/shard_map/ppermute | solution.py:281
  2.2 16.9 %collective-permute-start.1 = (bf16[512,256]{1,0:T(8,128)(2,1)}, bf16[512,256]{1,0:T(8,128)(2,1)S(1)}, u32[]{:S(2)}, u32[]{:S(2)}) collective-permute-start(bf16[512,256]{1,0:T(8,128)(2,1)} %refs_0_.5), channel_id=1, source_target_pairs={{0,48},{16,0},{32,16},{48,32},{1,49},{17,1},{33,17},{49,33},{2,50}... | collective-permute-start | bytes 786440 | tf_op jit(solution)/shard_map/ppermute | solution.py:281
  5.5 28.4 %all-to-all-start = ((bf16[32,16,512]{2,1,0:T(8,128)(2,1)}), bf16[32,16,512]{2,1,0:T(8,128)(2,1)S(1)}, u32[]{:S(2)}, u32[]{:S(2)}) async-start(bf16[32,16,512]{2,1,0:T(8,128)(2,1)} %pack.1), calls=%async_computation | async-start | bytes 1048576 | tf_op jit(solution)/shard_map/all_to_all | solution.py:328
  16.9 12.5 %copy-start.2 = (bf16[512,256]{1,0:T(8,128)(2,1)S(1)}, bf16[512,256]{1,0:T(8,128)(2,1)}, u32[]{:S(2)}) copy-start(bf16[512,256]{1,0:T(8,128)(2,1)} %refs_0_.5) | copy-start | bytes 786436
  16.9 12.9 %collective-permute-start.5 = (bf16[512,256]{1,0:T(8,128)(2,1)}, bf16[512,256]{1,0:T(8,128)(2,1)S(1)}, u32[]{:S(2)}, u32[]{:S(2)}) collective-permute-start(bf16[512,256]{1,0:T(8,128)(2,1)} %refs_0_.8), channel_id=1, source_target_pairs={{0,48},{16,0},{32,16},{48,32},{1,49},{17,1},{33,17},{49,33},{2,50}... | collective-permute-start | bytes 786440 | tf_op jit(solution)/shard_map/ppermute | solution.py:281
  18.6 11.3 %collective-permute-start.4 = (bf16[512,256]{1,0:T(8,128)(2,1)}, bf16[512,256]{1,0:T(8,128)(2,1)S(1)}, u32[]{:S(2)}, u32[]{:S(2)}) collective-permute-start(bf16[512,256]{1,0:T(8,128)(2,1)} %refs_0_.8), channel_id=1, source_target_pairs={{0,16},{16,32},{32,48},{48,0},{1,17},{17,33},{33,49},{49,1},{2,18}... | collective-permute-start | bytes 786440 | tf_op jit(solution)/shard_map/ppermute | solution.py:281
  19.1 10.4 %collective-permute-start.2 = (bf16[256,256]{1,0:T(8,128)(2,1)S(1)}, bf16[256,256]{1,0:T(8,128)(2,1)S(1)}, u32[]{:S(2)}, u32[]{:S(2)}) collective-permute-start(bf16[256,256]{1,0:T(8,128)(2,1)S(1)} %get-tuple-element.51), channel_id=1, source_target_pairs={{0,16},{16,32},{32,48},{48,0},{1,17},{17,33},{33,49},{49,1},{2,18}... | collective-permute-start | bytes 393224 | tf_op jit(solution)/shard_map/ppermute | solution.py:281
  19.4 10.0 %collective-permute-start.3 = (bf16[256,256]{1,0:T(8,128)(2,1)S(1)}, bf16[256,256]{1,0:T(8,128)(2,1)S(1)}, u32[]{:S(2)}, u32[]{:S(2)}) collective-permute-start(bf16[256,256]{1,0:T(8,128)(2,1)S(1)} %get-tuple-element.52), channel_id=1, source_target_pairs={{0,48},{16,0},{32,16},{48,32},{1,49},{17,1},{33,17},{49,33},{2,50}... | collective-permute-start | bytes 393224 | tf_op jit(solution)/shard_map/ppermute | solution.py:281
  34.0 4.2 %collective-permute-start.6 = (bf16[512,512]{1,0:T(8,128)(2,1)S(1)}, bf16[512,512]{1,0:T(8,128)(2,1)S(1)}, u32[]{:S(2)}, u32[]{:S(2)}) collective-permute-start(bf16[512,512]{1,0:T(8,128)(2,1)S(1)} %bitcast.1), channel_id=1, source_target_pairs={{0,1},{1,0},{2,3},{3,2},{4,5},{5,4},{6,7},{7,6},{8,9},{9,8},{10,11... | collective-permute-start | bytes 1572872 | tf_op jit(solution)/shard_map/ppermute | solution.py:281
  34.0 12.6 %collective-permute-start.11 = (bf16[256,256]{1,0:T(8,128)(2,1)S(1)}, bf16[256,256]{1,0:T(8,128)(2,1)S(1)}, u32[]{:S(2)}, u32[]{:S(2)}) collective-permute-start(bf16[256,256]{1,0:T(8,128)(2,1)S(1)} %get-tuple-element.66), channel_id=1, source_target_pairs={{0,16},{16,32},{32,48},{48,0},{1,17},{17,33},{33,49},{49,1},{2,18}... | collective-permute-start | bytes 393224 | tf_op jit(solution)/shard_map/ppermute | solution.py:281
  34.4 12.3 %collective-permute-start.12 = (bf16[256,256]{1,0:T(8,128)(2,1)S(1)}, bf16[256,256]{1,0:T(8,128)(2,1)S(1)}, u32[]{:S(2)}, u32[]{:S(2)}) collective-permute-start(bf16[256,256]{1,0:T(8,128)(2,1)S(1)} %get-tuple-element.67), channel_id=1, source_target_pairs={{0,48},{16,0},{32,16},{48,32},{1,49},{17,1},{33,17},{49,33},{2,50}... | collective-permute-start | bytes 393224 | tf_op jit(solution)/shard_map/ppermute | solution.py:281
  39.0 5.3 %collective-permute-start.7 = (f32[4,512]{1,0:T(4,128)S(1)}, f32[4,512]{1,0:T(4,128)S(1)}, u32[]{:S(2)}, u32[]{:S(2)}) collective-permute-start(f32[4,512]{1,0:T(4,128)S(1)} %get-tuple-element.60), channel_id=1, source_target_pairs={{0,32},{16,48},{32,0},{48,16},{1,33},{17,49},{33,1},{49,17},{2,34}... | collective-permute-start | bytes 24584 | tf_op jit(solution)/shard_map/ppermute | solution.py:281
  39.7 4.6 %collective-permute-start.8 = (f32[4,512]{1,0:T(4,128)S(1)}, f32[4,512]{1,0:T(4,128)S(1)}, u32[]{:S(2)}, u32[]{:S(2)}) collective-permute-start(f32[4,512]{1,0:T(4,128)S(1)} %get-tuple-element.61), channel_id=1, source_target_pairs={{0,48},{16,0},{32,16},{48,32},{1,49},{17,1},{33,17},{49,33},{2,50}... | collective-permute-start | bytes 24584 | tf_op jit(solution)/shard_map/ppermute | solution.py:281
  40.8 4.9 %collective-permute-start.9 = (f32[4,512]{1,0:T(4,128)S(1)}, f32[4,512]{1,0:T(4,128)S(1)}, u32[]{:S(2)}, u32[]{:S(2)}) collective-permute-start(f32[4,512]{1,0:T(4,128)S(1)} %get-tuple-element.62), channel_id=1, source_target_pairs={{0,16},{16,32},{32,48},{48,0},{1,17},{17,33},{33,49},{49,1},{2,18}... | collective-permute-start | bytes 24584 | tf_op jit(solution)/shard_map/ppermute | solution.py:281
  45.7 1.0 copy-start
  46.4 1.3 collective-permute-start.10
  63.9 7.0 %collective-permute-start.13 = (f32[4,512]{1,0:T(4,128)S(1)}, f32[4,512]{1,0:T(4,128)S(1)}, u32[]{:S(2)}, u32[]{:S(2)}) collective-permute-start(f32[4,512]{1,0:T(4,128)S(1)} %get-tuple-element.73), channel_id=1, source_target_pairs={{0,32},{16,48},{32,0},{48,16},{1,33},{17,49},{33,1},{49,17},{2,34}... | collective-permute-start | bytes 24584 | tf_op jit(solution)/shard_map/ppermute | solution.py:281
  64.8 6.1 %collective-permute-start.14 = (f32[4,512]{1,0:T(4,128)S(1)}, f32[4,512]{1,0:T(4,128)S(1)}, u32[]{:S(2)}, u32[]{:S(2)}) collective-permute-start(f32[4,512]{1,0:T(4,128)S(1)} %get-tuple-element.74), channel_id=1, source_target_pairs={{0,48},{16,0},{32,16},{48,32},{1,49},{17,1},{33,17},{49,33},{2,50}... | collective-permute-start | bytes 24584 | tf_op jit(solution)/shard_map/ppermute | solution.py:281
  66.0 4.9 %collective-permute-start.15 = (f32[4,512]{1,0:T(4,128)S(1)}, f32[4,512]{1,0:T(4,128)S(1)}, u32[]{:S(2)}, u32[]{:S(2)}) collective-permute-start(f32[4,512]{1,0:T(4,128)S(1)} %get-tuple-element.75), channel_id=1, source_target_pairs={{0,16},{16,32},{32,48},{48,0},{1,17},{17,33},{33,49},{49,1},{2,18}... | collective-permute-start | bytes 24584 | tf_op jit(solution)/shard_map/ppermute | solution.py:281
  71.6 1.2 collective-permute-start.16
  87.7 5.2 %collective-permute-start.17 = (f32[4,512]{1,0:T(4,128)S(1)}, f32[4,512]{1,0:T(4,128)S(1)}, u32[]{:S(2)}, u32[]{:S(2)}) collective-permute-start(f32[4,512]{1,0:T(4,128)S(1)} %get-tuple-element.81), channel_id=1, source_target_pairs={{0,32},{16,48},{32,0},{48,16},{1,33},{17,49},{33,1},{49,17},{2,34}... | collective-permute-start | bytes 24584 | tf_op jit(solution)/shard_map/ppermute | solution.py:281
  88.8 4.1 %collective-permute-start.18 = (f32[4,512]{1,0:T(4,128)S(1)}, f32[4,512]{1,0:T(4,128)S(1)}, u32[]{:S(2)}, u32[]{:S(2)}) collective-permute-start(f32[4,512]{1,0:T(4,128)S(1)} %get-tuple-element.82), channel_id=1, source_target_pairs={{0,48},{16,0},{32,16},{48,32},{1,49},{17,1},{33,17},{49,33},{2,50}... | collective-permute-start | bytes 24584 | tf_op jit(solution)/shard_map/ppermute | solution.py:281
  90.1 4.9 %collective-permute-start.19 = (f32[4,512]{1,0:T(4,128)S(1)}, f32[4,512]{1,0:T(4,128)S(1)}, u32[]{:S(2)}, u32[]{:S(2)}) collective-permute-start(f32[4,512]{1,0:T(4,128)S(1)} %get-tuple-element.83), channel_id=1, source_target_pairs={{0,16},{16,32},{32,48},{48,0},{1,17},{17,33},{33,49},{49,1},{2,18}... | collective-permute-start | bytes 24584 | tf_op jit(solution)/shard_map/ppermute | solution.py:281
  95.6 1.3 collective-permute-start.20
  111.0 1.6 %collective-permute-start.21 = (f32[8,128]{1,0:T(8,128)S(1)}, f32[8,128]{1,0:T(8,128)S(1)}, u32[]{:S(2)}, u32[]{:S(2)}) collective-permute-start(f32[8,128]{1,0:T(8,128)S(1)} %scales.1.refs_3_), channel_id=1, source_target_pairs={{0,1},{1,0},{2,3},{3,2},{4,5},{5,4},{6,7},{7,6},{8,9},{9,8},{10,11... | collective-permute-start | bytes 12296 | tf_op jit(solution)/shard_map/ppermute | solution.py:281
  114.0 5.2 %collective-permute-start.22 = (f32[512,256]{1,0:T(8,128)S(1)}, f32[512,256]{1,0:T(8,128)S(1)}, u32[]{:S(2)}, u32[]{:S(2)}) collective-permute-start(f32[512,256]{1,0:T(8,128)S(1)} %get-tuple-element.93), channel_id=1, source_target_pairs={{0,1},{1,0},{2,3},{3,2},{4,5},{5,4},{6,7},{7,6},{8,9},{9,8},{10,11... | collective-permute-start | bytes 1572872 | tf_op jit(solution)/shard_map/ppermute | solution.py:281
  115.9 10.9 %collective-permute-start.23 = (f32[320,256]{1,0:T(8,128)S(1)}, f32[320,256]{1,0:T(8,128)S(1)}, u32[]{:S(2)}, u32[]{:S(2)}) collective-permute-start(f32[320,256]{1,0:T(8,128)S(1)} %get-tuple-element.94), channel_id=1, source_target_pairs={{0,16},{16,32},{32,48},{48,0},{1,17},{17,33},{33,49},{49,1},{2,18}... | collective-permute-start | bytes 983048 | tf_op jit(solution)/shard_map/ppermute | solution.py:281
  116.0 10.8 %collective-permute-start.24 = (f32[320,256]{1,0:T(8,128)S(1)}, f32[320,256]{1,0:T(8,128)S(1)}, u32[]{:S(2)}, u32[]{:S(2)}) collective-permute-start(f32[320,256]{1,0:T(8,128)S(1)} %get-tuple-element.95), channel_id=1, source_target_pairs={{0,48},{16,0},{32,16},{48,32},{1,49},{17,1},{33,17},{49,33},{2,50}... | collective-permute-start | bytes 983048 | tf_op jit(solution)/shard_map/ppermute | solution.py:281
  120.1 22.0 %all-to-all-start.4 = ((f32[32,16,256]{2,1,0:T(8,128)}), f32[32,16,256]{2,1,0:T(8,128)S(1)}, u32[]{:S(2)}, u32[]{:S(2)}) async-start(f32[32,16,256]{2,1,0:T(8,128)} %pair.1), calls=%async_computation.4 | async-start | bytes 1048576 | tf_op jit(solution)/shard_map/all_to_all | solution.py:419
  126.8 13.0 %copy-start.1 = (bf16[512,256]{1,0:T(8,128)(2,1)S(1)}, bf16[512,256]{1,0:T(8,128)(2,1)}, u32[]{:S(2)}) copy-start(bf16[512,256]{1,0:T(8,128)(2,1)} %refs_0_.8) | copy-start | bytes 786436
  126.8 15.3 %copy-start.3 = (bf16[16,256]{1,0:T(8,128)(2,1)S(1)}, bf16[16,256]{1,0:T(8,128)(2,1)}, u32[]{:S(2)}) copy-start(bf16[16,256]{1,0:T(8,128)(2,1)} %refs_0_.7) | copy-start | bytes 24580
  126.9 12.9 %collective-permute-start.25 = (f32[448,256]{1,0:T(8,128)S(1)}, f32[448,256]{1,0:T(8,128)S(1)}, u32[]{:S(2)}, u32[]{:S(2)}) collective-permute-start(f32[448,256]{1,0:T(8,128)S(1)} %get-tuple-element.98), channel_id=1, source_target_pairs={{0,16},{16,32},{32,48},{48,0},{1,17},{17,33},{33,49},{49,1},{2,18}... | collective-permute-start | bytes 1376264 | tf_op jit(solution)/shard_map/ppermute | solution.py:281
  127.0 12.8 %collective-permute-start.26 = (f32[448,256]{1,0:T(8,128)S(1)}, f32[448,256]{1,0:T(8,128)S(1)}, u32[]{:S(2)}, u32[]{:S(2)}) collective-permute-start(f32[448,256]{1,0:T(8,128)S(1)} %get-tuple-element.99), channel_id=1, source_target_pairs={{0,48},{16,0},{32,16},{48,32},{1,49},{17,1},{33,17},{49,33},{2,50}... | collective-permute-start | bytes 1376264 | tf_op jit(solution)/shard_map/ppermute | solution.py:281

commit v8 on v7

--- a/solution.py
+++ b/solution.py
@@ -397,7 +397,7 @@
 
     own_grads, own_feat = logits(0, exp_own, inverse, ())
     sib_grads, sib_feat = logits(half, exp_sib, shift(inverse, "core", 1), (own_feat,))
-    pre, post = own_protos * 5 // 8, own_protos * (12 - 5) // 8
+    pre, post = own_protos * 11 // 16, own_protos * 13 // 16
     weight_parts = call(
         weights_kernel,
         [

time: 143 us -> 143 us (level)
  no operation moved by 1% of the time
where the time goes in v8:
time: 143 us
  starting transfers between devices  44.3 us (31%)
  blocking collectives  43.8 us (31%)
  waiting for transfers between devices  37.4 us (26%)
  Pallas kernels  16.4 us (11%)
    all_to_all x3, blocking collectives, spread(): lax.all_to_all(jnp.broadcast_to(values[None], (count,) + values.shape), R...  43.8 us
    ppermute x27, waiting for transfers between devices, shift(): lax.ppermute(values, axis, [(i, (i + step) % size) for i in range(size)])  32.1 us
    ppermute x27, starting transfers between devices, shift(): lax.ppermute(values, axis, [(i, (i + step) % size) for i in range(size)])  28.5 us
    pallas_call x21, Pallas kernels, call(): pl.pallas_call(lambda *refs: kernel(*refs[count:]), out_shape=outs, in_sp...  16.4 us
    all_to_all x1, starting transfers between devices, body(): own = lax.all_to_all(packed, ROWS, 0, 0, tiled=True).reshape(-1, 2 * width)  11.4 us
    all_to_all x1, starting transfers between devices, body(): feat_share = lax.all_to_all(feat_pair, ROWS, 0, 0, tiled=True)  4.37 us
    all_to_all x1, waiting for transfers between devices, body(): own = lax.all_to_all(packed, ROWS, 0, 0, tiled=True).reshape(-1, 2 * width)  4.12 us
  transfers between devices with their start and end apart: 29, of which 13 were waited for; matrix products, arithmetic and copies ran while one was open for 0% of the time, Pallas kernels for 8%

profile of v8, /device:TPU:32, one launch (start us, length us, event | category | flops | bytes accessed | tf_op | source)
XLA Modules:
  0.0 142.9 jit_solution(9059835009414997040)
XLA Ops:
  0.6 1.6 %collective-permute-start = (bf16[512,256]{1,0:T(8,128)(2,1)}, bf16[512,256]{1,0:T(8,128)(2,1)S(1)}, u32[]{:S(2)}, u32[]{:S(2)}) collective-permute-start(bf16[512,256]{1,0:T(8,128)(2,1)} %refs_0_.5), channel_id=1, source_target_pairs={{0,16},{16,32},{32,48},{48,0},{1,17},{17,33},{33,49},{49,1},{2,18}... | collective-permute-start | bytes 786440 | tf_op jit(solution)/shard_map/ppermute | solution.py:281
  2.2 1.7 %collective-permute-start.1 = (bf16[512,256]{1,0:T(8,128)(2,1)}, bf16[512,256]{1,0:T(8,128)(2,1)S(1)}, u32[]{:S(2)}, u32[]{:S(2)}) collective-permute-start(bf16[512,256]{1,0:T(8,128)(2,1)} %refs_0_.5), channel_id=1, source_target_pairs={{0,48},{16,0},{32,16},{48,32},{1,49},{17,1},{33,17},{49,33},{2,50}... | collective-permute-start | bytes 786440 | tf_op jit(solution)/shard_map/ppermute | solution.py:281
  3.9 1.6 %pack.1 = bf16[32,16,512]{2,1,0:T(8,128)(2,1)} custom-call(bf16[16,256]{1,0:T(8,128)(2,1)} %refs_0_.4, bf16[16,256]{1,0:T(8,128)(2,1)} %refs_0_.7), custom_call_target="tpu_custom_call" | custom-call | bytes 1048576 | tf_op jit(solution)/shard_map/pack/pallas_call | solution.py:35
  5.5 11.4 %all-to-all-start = ((bf16[32,16,512]{2,1,0:T(8,128)(2,1)}), bf16[32,16,512]{2,1,0:T(8,128)(2,1)S(1)}, u32[]{:S(2)}, u32[]{:S(2)}) async-start(bf16[32,16,512]{2,1,0:T(8,128)(2,1)} %pack.1), calls=%async_computation | async-start | bytes 1048576 | tf_op jit(solution)/shard_map/all_to_all | solution.py:328
  16.9 0.0 copy-start.2
  16.9 1.6 %collective-permute-start.5 = (bf16[512,256]{1,0:T(8,128)(2,1)}, bf16[512,256]{1,0:T(8,128)(2,1)S(1)}, u32[]{:S(2)}, u32[]{:S(2)}) collective-permute-start(bf16[512,256]{1,0:T(8,128)(2,1)} %refs_0_.8), channel_id=1, source_target_pairs={{0,48},{16,0},{32,16},{48,32},{1,49},{17,1},{33,17},{49,33},{2,50}... | collective-permute-start | bytes 786440 | tf_op jit(solution)/shard_map/ppermute | solution.py:281
  18.6 0.5 collective-permute-start.4
  19.1 0.0 collective-permute-done.1.refs_1_.refs_4_
  19.1 0.3 collective-permute-start.2
  19.4 3.0 %collective-permute-start.3 = (bf16[256,256]{1,0:T(8,128)(2,1)S(1)}, bf16[256,256]{1,0:T(8,128)(2,1)S(1)}, u32[]{:S(2)}, u32[]{:S(2)}) collective-permute-start(bf16[256,256]{1,0:T(8,128)(2,1)S(1)} %get-tuple-element.52), channel_id=1, source_target_pairs={{0,48},{16,0},{32,16},{48,32},{1,49},{17,1},{33,17},{49,33},{2,50}... | collective-permute-start | bytes 393224 | tf_op jit(solution)/shard_map/ppermute | solution.py:281
  22.4 7.0 %collective-permute-done.2.refs_2_ = bf16[256,256]{1,0:T(8,128)(2,1)S(1)} collective-permute-done((bf16[256,256]{1,0:T(8,128)(2,1)S(1)}, bf16[256,256]{1,0:T(8,128)(2,1)S(1)}, u32[]{:S(2)}, u32[]{:S(2)}) %collective-permute-start.2) | collective-permute-done | bytes 131104 | tf_op jit(solution)/shard_map/ppermute | solution.py:281
  29.4 0.4 teacher_units.1.refs_1_
  29.8 4.1 %all-to-all-done = bf16[32,16,512]{2,1,0:T(8,128)(2,1)S(1)} async-done(((bf16[32,16,512]{2,1,0:T(8,128)(2,1)}), bf16[32,16,512]{2,1,0:T(8,128)(2,1)S(1)}, u32[]{:S(2)}, u32[]{:S(2)}) %all-to-all-start) | async-done | bytes 524320 | tf_op jit(solution)/shard_map/all_to_all | solution.py:328
  34.0 0.4 collective-permute-start.11
  34.4 3.0 %collective-permute-start.12 = (bf16[256,256]{1,0:T(8,128)(2,1)S(1)}, bf16[256,256]{1,0:T(8,128)(2,1)S(1)}, u32[]{:S(2)}, u32[]{:S(2)}) collective-permute-start(bf16[256,256]{1,0:T(8,128)(2,1)S(1)} %get-tuple-element.67), channel_id=1, source_target_pairs={{0,48},{16,0},{32,16},{48,32},{1,49},{17,1},{33,17},{49,33},{2,50}... | collective-permute-start | bytes 393224 | tf_op jit(solution)/shard_map/ppermute | solution.py:281
  37.3 0.8 teacher_own.1
  38.1 0.8 teacher_sib.1
  39.0 0.7 collective-permute-start.7
  39.7 1.1 collective-permute-start.8
  40.8 0.9 collective-permute-start.9
  41.7 2.6 %collective-permute-done.7.refs_3_ = f32[4,512]{1,0:T(4,128)S(1)} collective-permute-done((f32[4,512]{1,0:T(4,128)S(1)}, f32[4,512]{1,0:T(4,128)S(1)}, u32[]{:S(2)}, u32[]{:S(2)}) %collective-permute-start.7) | collective-permute-done | bytes 8224 | tf_op jit(solution)/shard_map/ppermute | solution.py:281
  44.3 1.4 collective-permute-done.9.refs_5_
  45.7 0.7 rows.3
  46.4 0.2 collective-permute-start.10
  46.6 0.0 copy-done
  46.6 0.4 student_units.1.refs_2_.refs_4_.refs_5_
  47.0 0.7 collective-permute-done.10
  47.8 15.4 %all_to_all.25.refs_2_ = f32[32,8,128]{2,1,0:T(8,128)S(1)} all-to-all(f32[32,8,128]{2,1,0:T(8,128)S(1)} %broadcast_in_dim.6), channel_id=1, replica_groups=mesh['y'=4,'x'=4,'z'=8,'core'=2] {'y','z'}, dimensions={0} | all-to-all | bytes 262144 | tf_op jit(solution)/shard_map/all_to_all | solution.py:286
  63.2 0.7 columns.2
  63.9 0.8 collective-permute-start.13
  64.8 1.3 collective-permute-start.14
  66.0 0.8 collective-permute-start.15
  66.8 2.1 %student.1 = (f32[1024,2048]{1,0:T(8,128)S(1)}, f32[8,128]{1,0:T(8,128)S(1)}, bf16[1024,256]{1,0:T(8,128)(2,1)S(1)}) custom-call(bf16[512,512]{1,0:T(8,128)(2,1)S(1)} %bitcast.3, bf16[512,512]{1,0:T(8,128)(2,1)S(1)} %collective-permute-done.6.refs_0_.refs_1_, bf16[2048,256]{1,0:T(8,128)(2,1)S(1)} %student_units.1.refs_2_.refs_4_.refs_5_), custom_call_target="tpu_custom_call" | custom-call | flops 1073741824 | bytes 1048576 | tf_op jit(solution)/shard_map/student/pallas_call | solution.py:35
  68.9 2.0 %collective-permute-done.15.refs_5_ = f32[4,512]{1,0:T(4,128)S(1)} collective-permute-done((f32[4,512]{1,0:T(4,128)S(1)}, f32[4,512]{1,0:T(4,128)S(1)}, u32[]{:S(2)}, u32[]{:S(2)}) %collective-permute-start.15) | collective-permute-done | bytes 8224 | tf_op jit(solution)/shard_map/ppermute | solution.py:281
  70.9 0.7 rows.4
  71.6 1.2 collective-permute-done.16
  72.8 14.2 %all_to_all.26.refs_2_ = f32[32,8,128]{2,1,0:T(8,128)S(1)} all-to-all(f32[32,8,128]{2,1,0:T(8,128)S(1)} %broadcast_in_dim.7), channel_id=1, replica_groups=mesh['y'=4,'x'=4,'z'=8,'core'=2] {'y','z'}, dimensions={0} | all-to-all | bytes 262144 | tf_op jit(solution)/shard_map/all_to_all | solution.py:286
  87.0 0.7 columns.3
  87.7 1.1 collective-permute-start.17
  88.8 1.2 collective-permute-start.18
  90.1 0.8 collective-permute-start.19
  90.9 2.1 %collective-permute-done.17.refs_3_ = f32[4,512]{1,0:T(4,128)S(1)} collective-permute-done((f32[4,512]{1,0:T(4,128)S(1)}, f32[4,512]{1,0:T(4,128)S(1)}, u32[]{:S(2)}, u32[]{:S(2)}) %collective-permute-start.17) | collective-permute-done | bytes 8224 | tf_op jit(solution)/shard_map/ppermute | solution.py:281
  93.0 1.9 %collective-permute-done.19.refs_5_ = f32[4,512]{1,0:T(4,128)S(1)} collective-permute-done((f32[4,512]{1,0:T(4,128)S(1)}, f32[4,512]{1,0:T(4,128)S(1)}, u32[]{:S(2)}, u32[]{:S(2)}) %collective-permute-start.19) | collective-permute-done | bytes 8224 | tf_op jit(solution)/shard_map/ppermute | solution.py:281
  94.9 0.6 rows.5
  95.6 0.1 collective-permute-start.20
  95.7 1.2 collective-permute-done.20
  96.8 14.2 %all_to_all.27.refs_0_ = f32[32,8,128]{2,1,0:T(8,128)S(1)} all-to-all(f32[32,8,128]{2,1,0:T(8,128)S(1)} %broadcast_in_dim.8), channel_id=1, replica_groups=mesh['y'=4,'x'=4,'z'=8,'core'=2] {'y','z'}, dimensions={0} | all-to-all | bytes 262144 | tf_op jit(solution)/shard_map/all_to_all | solution.py:286
  111.0 0.3 collective-permute-start.21
  111.4 1.3 logits.2
  112.7 1.3 logits.3
  114.0 0.6 collective-permute-start.22
  114.6 1.3 weights.1
  115.9 0.1 collective-permute-start.23
  116.0 3.2 %collective-permute-start.24 = (f32[352,256]{1,0:T(8,128)S(1)}, f32[352,256]{1,0:T(8,128)S(1)}, u32[]{:S(2)}, u32[]{:S(2)}) collective-permute-start(f32[352,256]{1,0:T(8,128)S(1)} %get-tuple-element.95), channel_id=1, source_target_pairs={{0,48},{16,0},{32,16},{48,32},{1,49},{17,1},{33,17},{49,33},{2,50}... | collective-permute-start | bytes 1081352 | tf_op jit(solution)/shard_map/ppermute | solution.py:281
  119.2 0.9 pair.1
  120.1 4.4 %all-to-all-start.4 = ((f32[32,16,256]{2,1,0:T(8,128)}), f32[32,16,256]{2,1,0:T(8,128)S(1)}, u32[]{:S(2)}, u32[]{:S(2)}) async-start(f32[32,16,256]{2,1,0:T(8,128)} %pair.1), calls=%async_computation.4 | async-start | bytes 1048576 | tf_op jit(solution)/shard_map/all_to_all | solution.py:419
  124.5 3.1 %collective-permute-done.23.refs_2_ = f32[352,256]{1,0:T(8,128)S(1)} collective-permute-done((f32[352,256]{1,0:T(8,128)S(1)}, f32[352,256]{1,0:T(8,128)S(1)}, u32[]{:S(2)}, u32[]{:S(2)}) %collective-permute-start.23) | collective-permute-done | bytes 360480 | tf_op jit(solution)/shard_map/ppermute | solution.py:281
  127.5 0.1 relay.1
  127.6 0.1 collective-permute-start.25
  127.7 3.2 %collective-permute-start.26 = (f32[416,256]{1,0:T(8,128)S(1)}, f32[416,256]{1,0:T(8,128)S(1)}, u32[]{:S(2)}, u32[]{:S(2)}) collective-permute-start(f32[416,256]{1,0:T(8,128)S(1)} %get-tuple-element.99), channel_id=1, source_target_pairs={{0,48},{16,0},{32,16},{48,32},{1,49},{17,1},{33,17},{49,33},{2,50}... | collective-permute-start | bytes 1277960 | tf_op jit(solution)/shard_map/ppermute | solution.py:281
  130.9 8.9 %collective-permute-done.25.refs_4_ = f32[416,256]{1,0:T(8,128)S(1)} collective-permute-done((f32[416,256]{1,0:T(8,128)S(1)}, f32[416,256]{1,0:T(8,128)S(1)}, u32[]{:S(2)}, u32[]{:S(2)}) %collective-permute-start.25) | collective-permute-done | bytes 426016 | tf_op jit(solution)/shard_map/ppermute | solution.py:281
  139.8 1.0 proto_grad.1
  140.9 1.2 all-to-all-done.4.refs_1_
  142.1 0.8 row_grad.1
  (32 shorter events, 0.2 us)
Async XLA Ops:
  0.6 16.3 %collective-permute-start = (bf16[512,256]{1,0:T(8,128)(2,1)}, bf16[512,256]{1,0:T(8,128)(2,1)S(1)}, u32[]{:S(2)}, u32[]{:S(2)}) collective-permute-start(bf16[512,256]{1,0:T(8,128)(2,1)} %refs_0_.5), channel_id=1, source_target_pairs={{0,16},{16,32},{32,48},{48,0},{1,17},{17,33},{33,49},{49,1},{2,18}... | collective-permute-start | bytes 786440 | tf_op jit(solution)/shard_map/ppermute | solution.py:281
  2.2 16.9 %collective-permute-start.1 = (bf16[512,256]{1,0:T(8,128)(2,1)}, bf16[512,256]{1,0:T(8,128)(2,1)S(1)}, u32[]{:S(2)}, u32[]{:S(2)}) collective-permute-start(bf16[512,256]{1,0:T(8,128)(2,1)} %refs_0_.5), channel_id=1, source_target_pairs={{0,48},{16,0},{32,16},{48,32},{1,49},{17,1},{33,17},{49,33},{2,50}... | collective-permute-start | bytes 786440 | tf_op jit(solution)/shard_map/ppermute | solution.py:281
  5.5 28.4 %all-to-all-start = ((bf16[32,16,512]{2,1,0:T(8,128)(2,1)}), bf16[32,16,512]{2,1,0:T(8,128)(2,1)S(1)}, u32[]{:S(2)}, u32[]{:S(2)}) async-start(bf16[32,16,512]{2,1,0:T(8,128)(2,1)} %pack.1), calls=%async_computation | async-start | bytes 1048576 | tf_op jit(solution)/shard_map/all_to_all | solution.py:328
  16.9 12.5 %copy-start.2 = (bf16[512,256]{1,0:T(8,128)(2,1)S(1)}, bf16[512,256]{1,0:T(8,128)(2,1)}, u32[]{:S(2)}) copy-start(bf16[512,256]{1,0:T(8,128)(2,1)} %refs_0_.5) | copy-start | bytes 786436
  16.9 12.9 %collective-permute-start.5 = (bf16[512,256]{1,0:T(8,128)(2,1)}, bf16[512,256]{1,0:T(8,128)(2,1)S(1)}, u32[]{:S(2)}, u32[]{:S(2)}) collective-permute-start(bf16[512,256]{1,0:T(8,128)(2,1)} %refs_0_.8), channel_id=1, source_target_pairs={{0,48},{16,0},{32,16},{48,32},{1,49},{17,1},{33,17},{49,33},{2,50}... | collective-permute-start | bytes 786440 | tf_op jit(solution)/shard_map/ppermute | solution.py:281
  18.6 11.3 %collective-permute-start.4 = (bf16[512,256]{1,0:T(8,128)(2,1)}, bf16[512,256]{1,0:T(8,128)(2,1)S(1)}, u32[]{:S(2)}, u32[]{:S(2)}) collective-permute-start(bf16[512,256]{1,0:T(8,128)(2,1)} %refs_0_.8), channel_id=1, source_target_pairs={{0,16},{16,32},{32,48},{48,0},{1,17},{17,33},{33,49},{49,1},{2,18}... | collective-permute-start | bytes 786440 | tf_op jit(solution)/shard_map/ppermute | solution.py:281
  19.1 10.4 %collective-permute-start.2 = (bf16[256,256]{1,0:T(8,128)(2,1)S(1)}, bf16[256,256]{1,0:T(8,128)(2,1)S(1)}, u32[]{:S(2)}, u32[]{:S(2)}) collective-permute-start(bf16[256,256]{1,0:T(8,128)(2,1)S(1)} %get-tuple-element.51), channel_id=1, source_target_pairs={{0,16},{16,32},{32,48},{48,0},{1,17},{17,33},{33,49},{49,1},{2,18}... | collective-permute-start | bytes 393224 | tf_op jit(solution)/shard_map/ppermute | solution.py:281
  19.4 10.0 %collective-permute-start.3 = (bf16[256,256]{1,0:T(8,128)(2,1)S(1)}, bf16[256,256]{1,0:T(8,128)(2,1)S(1)}, u32[]{:S(2)}, u32[]{:S(2)}) collective-permute-start(bf16[256,256]{1,0:T(8,128)(2,1)S(1)} %get-tuple-element.52), channel_id=1, source_target_pairs={{0,48},{16,0},{32,16},{48,32},{1,49},{17,1},{33,17},{49,33},{2,50}... | collective-permute-start | bytes 393224 | tf_op jit(solution)/shard_map/ppermute | solution.py:281
  34.0 4.2 %collective-permute-start.6 = (bf16[512,512]{1,0:T(8,128)(2,1)S(1)}, bf16[512,512]{1,0:T(8,128)(2,1)S(1)}, u32[]{:S(2)}, u32[]{:S(2)}) collective-permute-start(bf16[512,512]{1,0:T(8,128)(2,1)S(1)} %bitcast.1), channel_id=1, source_target_pairs={{0,1},{1,0},{2,3},{3,2},{4,5},{5,4},{6,7},{7,6},{8,9},{9,8},{10,11... | collective-permute-start | bytes 1572872 | tf_op jit(solution)/shard_map/ppermute | solution.py:281
  34.0 12.6 %collective-permute-start.11 = (bf16[256,256]{1,0:T(8,128)(2,1)S(1)}, bf16[256,256]{1,0:T(8,128)(2,1)S(1)}, u32[]{:S(2)}, u32[]{:S(2)}) collective-permute-start(bf16[256,256]{1,0:T(8,128)(2,1)S(1)} %get-tuple-element.66), channel_id=1, source_target_pairs={{0,16},{16,32},{32,48},{48,0},{1,17},{17,33},{33,49},{49,1},{2,18}... | collective-permute-start | bytes 393224 | tf_op jit(solution)/shard_map/ppermute | solution.py:281
  34.4 12.3 %collective-permute-start.12 = (bf16[256,256]{1,0:T(8,128)(2,1)S(1)}, bf16[256,256]{1,0:T(8,128)(2,1)S(1)}, u32[]{:S(2)}, u32[]{:S(2)}) collective-permute-start(bf16[256,256]{1,0:T(8,128)(2,1)S(1)} %get-tuple-element.67), channel_id=1, source_target_pairs={{0,48},{16,0},{32,16},{48,32},{1,49},{17,1},{33,17},{49,33},{2,50}... | collective-permute-start | bytes 393224 | tf_op jit(solution)/shard_map/ppermute | solution.py:281
  39.0 5.3 %collective-permute-start.7 = (f32[4,512]{1,0:T(4,128)S(1)}, f32[4,512]{1,0:T(4,128)S(1)}, u32[]{:S(2)}, u32[]{:S(2)}) collective-permute-start(f32[4,512]{1,0:T(4,128)S(1)} %get-tuple-element.60), channel_id=1, source_target_pairs={{0,32},{16,48},{32,0},{48,16},{1,33},{17,49},{33,1},{49,17},{2,34}... | collective-permute-start | bytes 24584 | tf_op jit(solution)/shard_map/ppermute | solution.py:281
  39.7 4.6 %collective-permute-start.8 = (f32[4,512]{1,0:T(4,128)S(1)}, f32[4,512]{1,0:T(4,128)S(1)}, u32[]{:S(2)}, u32[]{:S(2)}) collective-permute-start(f32[4,512]{1,0:T(4,128)S(1)} %get-tuple-element.61), channel_id=1, source_target_pairs={{0,48},{16,0},{32,16},{48,32},{1,49},{17,1},{33,17},{49,33},{2,50}... | collective-permute-start | bytes 24584 | tf_op jit(solution)/shard_map/ppermute | solution.py:281
  40.8 4.9 %collective-permute-start.9 = (f32[4,512]{1,0:T(4,128)S(1)}, f32[4,512]{1,0:T(4,128)S(1)}, u32[]{:S(2)}, u32[]{:S(2)}) collective-permute-start(f32[4,512]{1,0:T(4,128)S(1)} %get-tuple-element.62), channel_id=1, source_target_pairs={{0,16},{16,32},{32,48},{48,0},{1,17},{17,33},{33,49},{49,1},{2,18}... | collective-permute-start | bytes 24584 | tf_op jit(solution)/shard_map/ppermute | solution.py:281
  45.7 1.0 copy-start
  46.4 1.3 collective-permute-start.10
  63.9 7.0 %collective-permute-start.13 = (f32[4,512]{1,0:T(4,128)S(1)}, f32[4,512]{1,0:T(4,128)S(1)}, u32[]{:S(2)}, u32[]{:S(2)}) collective-permute-start(f32[4,512]{1,0:T(4,128)S(1)} %get-tuple-element.73), channel_id=1, source_target_pairs={{0,32},{16,48},{32,0},{48,16},{1,33},{17,49},{33,1},{49,17},{2,34}... | collective-permute-start | bytes 24584 | tf_op jit(solution)/shard_map/ppermute | solution.py:281
  64.8 6.1 %collective-permute-start.14 = (f32[4,512]{1,0:T(4,128)S(1)}, f32[4,512]{1,0:T(4,128)S(1)}, u32[]{:S(2)}, u32[]{:S(2)}) collective-permute-start(f32[4,512]{1,0:T(4,128)S(1)} %get-tuple-element.74), channel_id=1, source_target_pairs={{0,48},{16,0},{32,16},{48,32},{1,49},{17,1},{33,17},{49,33},{2,50}... | collective-permute-start | bytes 24584 | tf_op jit(solution)/shard_map/ppermute | solution.py:281
  66.0 4.9 %collective-permute-start.15 = (f32[4,512]{1,0:T(4,128)S(1)}, f32[4,512]{1,0:T(4,128)S(1)}, u32[]{:S(2)}, u32[]{:S(2)}) collective-permute-start(f32[4,512]{1,0:T(4,128)S(1)} %get-tuple-element.75), channel_id=1, source_target_pairs={{0,16},{16,32},{32,48},{48,0},{1,17},{17,33},{33,49},{49,1},{2,18}... | collective-permute-start | bytes 24584 | tf_op jit(solution)/shard_map/ppermute | solution.py:281
  71.6 1.2 collective-permute-start.16
  87.7 5.2 %collective-permute-start.17 = (f32[4,512]{1,0:T(4,128)S(1)}, f32[4,512]{1,0:T(4,128)S(1)}, u32[]{:S(2)}, u32[]{:S(2)}) collective-permute-start(f32[4,512]{1,0:T(4,128)S(1)} %get-tuple-element.81), channel_id=1, source_target_pairs={{0,32},{16,48},{32,0},{48,16},{1,33},{17,49},{33,1},{49,17},{2,34}... | collective-permute-start | bytes 24584 | tf_op jit(solution)/shard_map/ppermute | solution.py:281
  88.8 4.1 %collective-permute-start.18 = (f32[4,512]{1,0:T(4,128)S(1)}, f32[4,512]{1,0:T(4,128)S(1)}, u32[]{:S(2)}, u32[]{:S(2)}) collective-permute-start(f32[4,512]{1,0:T(4,128)S(1)} %get-tuple-element.82), channel_id=1, source_target_pairs={{0,48},{16,0},{32,16},{48,32},{1,49},{17,1},{33,17},{49,33},{2,50}... | collective-permute-start | bytes 24584 | tf_op jit(solution)/shard_map/ppermute | solution.py:281
  90.1 4.9 %collective-permute-start.19 = (f32[4,512]{1,0:T(4,128)S(1)}, f32[4,512]{1,0:T(4,128)S(1)}, u32[]{:S(2)}, u32[]{:S(2)}) collective-permute-start(f32[4,512]{1,0:T(4,128)S(1)} %get-tuple-element.83), channel_id=1, source_target_pairs={{0,16},{16,32},{32,48},{48,0},{1,17},{17,33},{33,49},{49,1},{2,18}... | collective-permute-start | bytes 24584 | tf_op jit(solution)/shard_map/ppermute | solution.py:281
  95.6 1.3 collective-permute-start.20
  111.0 1.6 %collective-permute-start.21 = (f32[8,128]{1,0:T(8,128)S(1)}, f32[8,128]{1,0:T(8,128)S(1)}, u32[]{:S(2)}, u32[]{:S(2)}) collective-permute-start(f32[8,128]{1,0:T(8,128)S(1)} %scales.1.refs_3_), channel_id=1, source_target_pairs={{0,1},{1,0},{2,3},{3,2},{4,5},{5,4},{6,7},{7,6},{8,9},{9,8},{10,11... | collective-permute-start | bytes 12296 | tf_op jit(solution)/shard_map/ppermute | solution.py:281
  114.0 5.2 %collective-permute-start.22 = (f32[512,256]{1,0:T(8,128)S(1)}, f32[512,256]{1,0:T(8,128)S(1)}, u32[]{:S(2)}, u32[]{:S(2)}) collective-permute-start(f32[512,256]{1,0:T(8,128)S(1)} %get-tuple-element.93), channel_id=1, source_target_pairs={{0,1},{1,0},{2,3},{3,2},{4,5},{5,4},{6,7},{7,6},{8,9},{9,8},{10,11... | collective-permute-start | bytes 1572872 | tf_op jit(solution)/shard_map/ppermute | solution.py:281
  115.9 11.6 %collective-permute-start.23 = (f32[352,256]{1,0:T(8,128)S(1)}, f32[352,256]{1,0:T(8,128)S(1)}, u32[]{:S(2)}, u32[]{:S(2)}) collective-permute-start(f32[352,256]{1,0:T(8,128)S(1)} %get-tuple-element.94), channel_id=1, source_target_pairs={{0,16},{16,32},{32,48},{48,0},{1,17},{17,33},{33,49},{49,1},{2,18}... | collective-permute-start | bytes 1081352 | tf_op jit(solution)/shard_map/ppermute | solution.py:281
  116.0 11.5 %collective-permute-start.24 = (f32[352,256]{1,0:T(8,128)S(1)}, f32[352,256]{1,0:T(8,128)S(1)}, u32[]{:S(2)}, u32[]{:S(2)}) collective-permute-start(f32[352,256]{1,0:T(8,128)S(1)} %get-tuple-element.95), channel_id=1, source_target_pairs={{0,48},{16,0},{32,16},{48,32},{1,49},{17,1},{33,17},{49,33},{2,50}... | collective-permute-start | bytes 1081352 | tf_op jit(solution)/shard_map/ppermute | solution.py:281
  120.1 22.0 %all-to-all-start.4 = ((f32[32,16,256]{2,1,0:T(8,128)}), f32[32,16,256]{2,1,0:T(8,128)S(1)}, u32[]{:S(2)}, u32[]{:S(2)}) async-start(f32[32,16,256]{2,1,0:T(8,128)} %pair.1), calls=%async_computation.4 | async-start | bytes 1048576 | tf_op jit(solution)/shard_map/all_to_all | solution.py:419
  127.5 12.3 %copy-start.1 = (bf16[512,256]{1,0:T(8,128)(2,1)S(1)}, bf16[512,256]{1,0:T(8,128)(2,1)}, u32[]{:S(2)}) copy-start(bf16[512,256]{1,0:T(8,128)(2,1)} %refs_0_.8) | copy-start | bytes 786436
  127.5 14.6 %copy-start.3 = (bf16[16,256]{1,0:T(8,128)(2,1)S(1)}, bf16[16,256]{1,0:T(8,128)(2,1)}, u32[]{:S(2)}) copy-start(bf16[16,256]{1,0:T(8,128)(2,1)} %refs_0_.7) | copy-start | bytes 24580
  127.6 12.2 %collective-permute-start.25 = (f32[416,256]{1,0:T(8,128)S(1)}, f32[416,256]{1,0:T(8,128)S(1)}, u32[]{:S(2)}, u32[]{:S(2)}) collective-permute-start(f32[416,256]{1,0:T(8,128)S(1)} %get-tuple-element.98), channel_id=1, source_target_pairs={{0,16},{16,32},{32,48},{48,0},{1,17},{17,33},{33,49},{49,1},{2,18}... | collective-permute-start | bytes 1277960 | tf_op jit(solution)/shard_map/ppermute | solution.py:281
  127.7 12.1 %collective-permute-start.26 = (f32[416,256]{1,0:T(8,128)S(1)}, f32[416,256]{1,0:T(8,128)S(1)}, u32[]{:S(2)}, u32[]{:S(2)}) collective-permute-start(f32[416,256]{1,0:T(8,128)S(1)} %get-tuple-element.99), channel_id=1, source_target_pairs={{0,48},{16,0},{32,16},{48,32},{1,49},{17,1},{33,17},{49,33},{2,50}... | collective-permute-start | bytes 1277960 | tf_op jit(solution)/shard_map/ppermute | solution.py:281
